TPU v7x, 32 devices: a whole 2x2x4 slice. The times are simulated.
32 devices in a mesh: dp: 8 (over z, y), col: 4 (over x, core).
Axes of the slice: x: 2, y: 2, z: 4, core: 2. Of those that a mesh axis runs over, the one named last changes fastest.
Arguments:
- bin_index: int32 [4096, 16], P('dp'), may hold values from 0 to 47
- bin_fraction: float32 [4096, 16], P('dp'), may hold values from 0 to 1
- row_mask: int32 [4096], P('dp'), may hold values from 0 to 1, as said below
- targets: int32 [4096], P('dp'), may hold values from 0 to 15
- w_first: float32 [768, 512], P('dp', 'col'), may hold values from -0.21875 to 0.21875
- w_second: float32 [512, 512], P('dp', 'col'), may hold values from -0.25 to 0.25
- w_head: float32 [32, 512, 16], P(None, 'dp'), may hold values from -0.5 to 0.5
- adapters: float32 [5, 32, 512], P(None, None, 'col'), may hold values from -1.5 to 1.5, as said below
- gains: float32 [32, 768], replicated, may hold values from 0.5 to 2
- head_bias: float32 [32, 16], replicated, may hold values from -3 to 3
- first_row: float32 [768], P('dp'), may hold values from 2.4414062e-09 to 1.8310548e-08
- first_col: float32 [512], P('col'), may hold values from 2.4414062e-09 to 1.8310548e-08
- second_row: float32 [512], P('dp'), may hold values from 1.4648438e-09 to 1.0986328e-08
- second_col: float32 [512], P('col'), may hold values from 1.4648438e-09 to 1.0986328e-08
- head_row: float32 [32, 512], P(None, 'dp'), may hold values from 1.953125e-09 to 1.4648437e-08
- head_col: float32 [32, 16], replicated, may hold values from 1.953125e-09 to 1.4648437e-08
- adapter_sq: float32 [5, 32, 512], P(None, None, 'col'), may hold values from 4.8828126e-11 to 3.6621095e-10
- gain_sq: float32 [32, 768], replicated, may hold values from 4.8828126e-11 to 3.6621095e-10
- bias_sq: float32 [32, 16], replicated, may hold values from 1.4648438e-09 to 1.0986328e-08
Outputs:
- first_grad: float32 [768, 512], P('dp', 'col')
- first_row_new: float32 [768], P('dp')
- first_col_new: float32 [512], P('col')
- first_new: float32 [768, 512], P('dp', 'col')
- second_grad: float32 [512, 512], P('dp', 'col')
- second_row_new: float32 [512], P('dp')
- second_col_new: float32 [512], P('col')
- second_new: float32 [512, 512], P('dp', 'col')
- head_grad: float32 [32, 512, 16], P(None, 'dp')
- head_row_new: float32 [32, 512], P(None, 'dp')
- head_col_new: float32 [32, 16], replicated
- head_new: float32 [32, 512, 16], P(None, 'dp')
- adapter_grad: float32 [5, 32, 512], P(None, None, 'col')
- adapter_sq_new: float32 [5, 32, 512], P(None, None, 'col')
- adapter_new: float32 [5, 32, 512], P(None, None, 'col')
- gain_grad: float32 [32, 768], replicated
- gain_sq_new: float32 [32, 768], replicated
- gain_new: float32 [32, 768], replicated
- bias_grad: float32 [32, 16], replicated
- bias_sq_new: float32 [32, 16], replicated
- bias_new: float32 [32, 16], replicated
- loss_sum: float32 [], replicated
- row_total: float32 [], replicated
- residual_rms: float32 [], replicated
- branch_rms: float32 [], replicated
Inputs may be any that keep to these rules, and one draw needn't show every extreme that they name: `row_mask`: in each aligned block of 512 rows the ones form a leading run, longer on average in later blocks; the last block is all ones. `adapters`: scales (kinds 0, 2, 3) lie in 0.5 to 1.5; biases (kinds 1, 4) in -1.5 to 1.5.
All inputs are finite; a program needn't handle non-finite values.
Results may differ from a plain program's by a relative error of at most 0.0066.
The roundings to bfloat16 on the way count: a program that leaves them out, or rounds other values in their place, can miss the bound.
Values may be sent and summed in bfloat16 or wider, within the bound.
A program may use at most 256 MiB of HBM per device.

v0:
```python
import jax
import jax.numpy as jnp
from jax import lax
from jax.sharding import PartitionSpec as P

FEATS = 16
BINS = 48
CLASSES = 16
STEP = 10


EPS_SQUARE = 1e-30
CLIP_LIMIT = 1.0
RELATIVE_RATE = 0.4
RATE_FLOOR = 0.001
HIGH = lax.Precision.HIGHEST


def encode(bin_index, bin_fraction):
    levels = jnp.arange(BINS, dtype=jnp.int32)
    under_bin = levels[None, None, :] < bin_index[:, :, None]
    at_bin = levels[None, None, :] == bin_index[:, :, None]
    fraction = bin_fraction[:, :, None]
    encoded = jnp.where(
        under_bin, jnp.ones_like(fraction), jnp.where(at_bin, fraction, jnp.zeros_like(fraction))
    )
    return encoded.reshape(bin_index.shape[0], FEATS * BINS)


def silu_slope(values):
    sigmoid_of = jax.nn.sigmoid(values)
    return sigmoid_of * (1.0 + values * (1.0 - sigmoid_of))


def shared_product(left, right):
    shape_left = left.shape
    flat = jnp.dot(left.reshape(-1, shape_left[-1]), right, preferred_element_type=jnp.float32)
    return flat.reshape(shape_left[:-1] + (right.shape[1],))


def outer_sum(left, right):
    return jnp.einsum(
        "nk,nd->kd",
        left.reshape(-1, left.shape[-1]),
        right.reshape(-1, right.shape[-1]),
        preferred_element_type=jnp.float32,
    )


def finish(weight, update, update_sq, weight_sq, entries):
    rms_update = jnp.sqrt(update_sq / entries)
    rms_weight = jnp.sqrt(weight_sq / entries)
    update = update / jnp.maximum(1.0, rms_update / CLIP_LIMIT)
    return weight - RELATIVE_RATE * jnp.maximum(RATE_FLOOR, rms_weight) * update


def local(
    bin_index,
    bin_fraction,
    row_mask,
    targets,
    w_first,
    w_second,
    w_head,
    adapters,
    gains,
    head_bias,
    first_row,
    first_col,
    second_row,
    second_col,
    head_row,
    head_col,
    adapter_sq,
    gain_sq,
    bias_sq,
):
    count_col = lax.axis_size("col")
    count_dp = lax.axis_size("dp")
    col_place = lax.axis_index("col")
    members = gains.shape[0]
    enc_width = gains.shape[1]
    col_width = adapters.shape[2]
    full_width = col_width * count_col
    decay = 1.0 - STEP ** (-0.8)
    first_full, second_full, head_full = (
        lax.all_gather(w_first.astype(jnp.bfloat16), "dp", axis=0, tiled=True),
        lax.all_gather(w_second.astype(jnp.bfloat16), "dp", axis=0, tiled=True),
        lax.all_gather(w_head.astype(jnp.bfloat16), "dp", axis=1, tiled=True),
    )
    row_total = lax.psum(jnp.sum(row_mask.astype(jnp.float32)), "dp")
    bin_use, fraction_use, target_use, mask_use = (bin_index, bin_fraction, targets, row_mask)
    first_use, second_use, adapter_use = (first_full, second_full, adapters)
    weight_rows = mask_use.astype(jnp.float32)
    encoded = encode(bin_use, fraction_use)
    first_in = (encoded[:, None, :] * gains[None]).astype(jnp.bfloat16)
    first_out = shared_product(first_in, first_use)
    first_pre = first_out * adapter_use[0] + adapter_use[1]
    stream_one = jax.nn.silu(first_pre)
    second_in = (stream_one * adapter_use[2]).astype(jnp.bfloat16)
    second_all = lax.all_gather(second_in, "col", axis=2, tiled=True)
    second_out = shared_product(second_all, second_use)
    second_pre = second_out * adapter_use[3] + adapter_use[4]
    branch = jax.nn.silu(second_pre)
    stream_two = stream_one + branch
    stream_all = lax.all_gather(stream_two.astype(jnp.bfloat16), "col", axis=2, tiled=True)
    head_own = lax.dynamic_slice_in_dim(head_full, col_place * col_width, col_width, 1)
    logits = (
        jnp.einsum("rmd,mdc->rmc", stream_all, head_full, preferred_element_type=jnp.float32)
        + head_bias
    )
    log_total = jax.nn.logsumexp(logits, axis=-1)
    onehot = jax.nn.one_hot(target_use, CLASSES, dtype=jnp.float32)[:, None, :]
    chosen = jnp.sum(logits * onehot, axis=-1)
    weight = weight_rows[:, None]
    loss_part = jnp.sum((log_total - chosen) * weight)
    softmax_out = jnp.exp(logits - log_total[:, :, None])
    loss_scale = 1.0 / (members * row_total)
    logit_grad = ((softmax_out - onehot) * (weight * loss_scale)[:, :, None]).astype(jnp.bfloat16)
    bias_part = jnp.sum(logit_grad.astype(jnp.float32), axis=0)
    head_part = jnp.einsum(
        "rmd,rmc->mdc", stream_all, logit_grad, preferred_element_type=jnp.float32
    )
    stream_grad = jnp.einsum(
        "rmc,mdc->rmd", logit_grad, head_own, preferred_element_type=jnp.float32
    )
    pre_grad = stream_grad * silu_slope(second_pre)
    scale_two = jnp.sum(pre_grad * second_out, axis=0)
    bias_two = jnp.sum(pre_grad, axis=0)
    out_grad = (pre_grad * adapter_use[3]).astype(jnp.bfloat16)
    second_part = outer_sum(second_all, out_grad)
    partial_in = jnp.einsum(
        "rmo,ko->rmk", out_grad, second_full, preferred_element_type=jnp.float32
    )
    in_grad = lax.psum_scatter(partial_in, "col", scatter_dimension=2, tiled=True)
    scale_in = jnp.sum(in_grad * stream_one, axis=0)
    one_grad = stream_grad + in_grad * adapter_use[2]
    low_grad = one_grad * silu_slope(first_pre)
    scale_one = jnp.sum(low_grad * first_out, axis=0)
    bias_one = jnp.sum(low_grad, axis=0)
    first_out_grad = (low_grad * adapter_use[0]).astype(jnp.bfloat16)
    first_part = outer_sum(first_in, first_out_grad)
    back_terms = jnp.einsum(
        "rmd,kd->rmk", first_out_grad, first_use, preferred_element_type=jnp.float32
    )
    gain_part = jnp.einsum("rk,rmk->mk", encoded, back_terms, precision=HIGH)
    adapter_part = jnp.stack([scale_one, bias_one, scale_in, scale_two, bias_two])
    residual_part = jnp.sum(stream_one * stream_one * weight[:, :, None])
    branch_part = jnp.sum(branch * branch * weight[:, :, None])
    adapter_grad, bias_grad, loss_sum = lax.psum((adapter_part, bias_part, loss_part), "dp")
    gain_grad, residual_sq, branch_sq = lax.psum(
        (gain_part, residual_part, branch_part), ("dp", "col")
    )
    first_grad, second_grad, head_grad = (
        lax.psum_scatter(first_part, "dp", scatter_dimension=0, tiled=True),
        lax.psum_scatter(second_part, "dp", scatter_dimension=0, tiled=True),
        lax.psum_scatter(head_part, "dp", scatter_dimension=1, tiled=True),
    )
    first_square = first_grad * first_grad + EPS_SQUARE
    second_square = second_grad * second_grad + EPS_SQUARE
    head_square = head_grad * head_grad + EPS_SQUARE
    first_rowsum, second_rowsum = lax.psum(
        (jnp.sum(first_square, axis=1), jnp.sum(second_square, axis=1)), "col"
    )
    first_row_new = decay * first_row + (1.0 - decay) * (first_rowsum / full_width)
    second_row_new = decay * second_row + (1.0 - decay) * (second_rowsum / full_width)
    head_row_new = decay * head_row + (1.0 - decay) * jnp.mean(head_square, axis=-1)
    stats = lax.psum(
        (
            jnp.sum(first_square, axis=0),
            jnp.sum(second_square, axis=0),
            jnp.sum(head_square, axis=1),
            jnp.sum(first_row_new),
            jnp.sum(second_row_new),
            jnp.sum(head_row_new, axis=1),
        ),
        "dp",
    )
    first_colsum, second_colsum, head_colsum, first_rowtotal, second_rowtotal, head_rowtotal = stats
    first_col_new = decay * first_col + (1.0 - decay) * (first_colsum / enc_width)
    second_col_new = decay * second_col + (1.0 - decay) * (second_colsum / full_width)
    head_col_new = decay * head_col + (1.0 - decay) * (head_colsum / full_width)
    first_estimate = first_row_new[:, None] * first_col_new[None, :] / (first_rowtotal / enc_width)
    second_estimate = (
        second_row_new[:, None] * second_col_new[None, :] / (second_rowtotal / full_width)
    )
    head_estimate = (
        head_row_new[:, :, None]
        * head_col_new[:, None, :]
        / (head_rowtotal / full_width)[:, None, None]
    )
    first_update = first_grad * lax.rsqrt(first_estimate)
    second_update = second_grad * lax.rsqrt(second_estimate)
    head_update = head_grad * lax.rsqrt(head_estimate)
    adapter_sq_new = decay * adapter_sq + (1.0 - decay) * (adapter_grad * adapter_grad + EPS_SQUARE)
    adapter_update = adapter_grad * lax.rsqrt(adapter_sq_new)
    gain_sq_new = decay * gain_sq + (1.0 - decay) * (gain_grad * gain_grad + EPS_SQUARE)
    gain_update = gain_grad * lax.rsqrt(gain_sq_new)
    bias_sq_new = decay * bias_sq + (1.0 - decay) * (bias_grad * bias_grad + EPS_SQUARE)
    bias_update = bias_grad * lax.rsqrt(bias_sq_new)
    share_col = 1.0 / count_col
    share_dp = 1.0 / count_dp
    sums = lax.psum(
        (
            jnp.sum(first_update * first_update),
            jnp.sum(w_first * w_first),
            jnp.sum(second_update * second_update),
            jnp.sum(w_second * w_second),
            jnp.sum(head_update * head_update) * share_col,
            jnp.sum(w_head * w_head) * share_col,
            jnp.sum(adapter_update * adapter_update, axis=(1, 2)) * share_dp,
            jnp.sum(adapters * adapters, axis=(1, 2)) * share_dp,
        ),
        ("dp", "col"),
    )
    first_new = finish(w_first, first_update, sums[0], sums[1], enc_width * full_width)
    second_new = finish(w_second, second_update, sums[2], sums[3], full_width * full_width)
    head_new = finish(w_head, head_update, sums[4], sums[5], members * full_width * CLASSES)
    adapter_new = finish(
        adapters,
        adapter_update,
        sums[6].reshape(5, 1, 1),
        sums[7].reshape(5, 1, 1),
        members * full_width,
    )
    gain_new = finish(
        gains,
        gain_update,
        jnp.sum(gain_update * gain_update),
        jnp.sum(gains * gains),
        members * enc_width,
    )
    bias_new = finish(
        head_bias,
        bias_update,
        jnp.sum(bias_update * bias_update),
        jnp.sum(head_bias * head_bias),
        members * CLASSES,
    )
    residual_rms = jnp.sqrt(residual_sq / (row_total * members * full_width))
    branch_rms = jnp.sqrt(branch_sq / (row_total * members * full_width))
    return (
        first_grad,
        first_row_new,
        first_col_new,
        first_new,
        second_grad,
        second_row_new,
        second_col_new,
        second_new,
        head_grad,
        head_row_new,
        head_col_new,
        head_new,
        adapter_grad,
        adapter_sq_new,
        adapter_new,
        gain_grad,
        gain_sq_new,
        gain_new,
        bias_grad,
        bias_sq_new,
        bias_new,
        loss_sum,
        row_total,
        residual_rms,
        branch_rms,
    )


def solution(mesh):
    placed = (
        P("dp", None),
        P("dp", None),
        P("dp"),
        P("dp"),
        P("dp", "col"),
        P("dp", "col"),
        P(None, "dp", None),
        P(None, None, "col"),
        P(),
        P(),
        P("dp"),
        P("col"),
        P("dp"),
        P("col"),
        P(None, "dp"),
        P(),
        P(None, None, "col"),
        P(),
        P(),
    )
    return jax.shard_map(
        local,
        mesh=mesh,
        in_specs=placed,
        out_specs=(
            P("dp", "col"),
            P("dp"),
            P("col"),
            P("dp", "col"),
            P("dp", "col"),
            P("dp"),
            P("col"),
            P("dp", "col"),
            P(None, "dp", None),
            P(None, "dp"),
            P(),
            P(None, "dp", None),
            P(None, None, "col"),
            P(None, None, "col"),
            P(None, None, "col"),
            P(),
            P(),
            P(),
            P(),
            P(),
            P(),
            P(),
            P(),
            P(),
            P(),
        ),
        check_vma=False,
    )
```

profile of v0, /device:TPU:0, one launch (start us, length us, event | category | flops | bytes accessed | tf_op | source)
XLA Modules:
  0.0 1094.5 jit_solution(17996614689594753248)
XLA Ops:
  7.3 1.5 multiply_reduce_fusion.15
  8.8 0.8 slice_bitcast_fusion.1
  9.7 32.4 %all_gather.16 = bf16[768,128]{1,0:T(8,128)(2,1)S(1)} all-gather(bf16[96,128]{1,0:T(8,128)(2,1)S(1)} %get-tuple-element.137), channel_id=1, replica_groups=mesh['dp'=8,'col'=4] {'dp'}, dimensions={0}, use_global_device_ids=true | all-gather | bytes 221184 | tf_op jit(solution)/shard_map/all_gather | solution.py:87
  42.1 1.0 fusion.12
  43.1 15.0 %multiply_convert_fusion.5 = (bf16[512,32,128]{2,0,1:T(8,128)(2,1)}, f32[512,32,128]{2,0,1:T(8,128)}) fusion(f32[32,128]{1,0:T(8,128)S(1)} %get-tuple-element.133, f32[32,128]{1,0:T(8,128)S(1)} %get-tuple-element.134, f32[32,128]{1,0:T(8,128)S(1)} %get-tuple-element.135, bf16[768,128]{1,0:T(8,128)(2,1)S(1)} %all_gather.16, f32[32,768]{1,0:T(8,128)} %param.27, ...), kind=kOutput, calls=%fused_computation.22 | convolution fusion | flops 3263168512 | bytes 14499840 | tf_op jit(solution)/shard_map/dot_general | solution.py:37
  58.3 0.6 multiply_reduce_fusion.17
  58.9 30.5 %all_gather.18 = bf16[512,128]{1,0:T(8,128)(2,1)S(1)} all-gather(bf16[64,128]{1,0:T(8,128)(2,1)S(1)} %get-tuple-element.141), channel_id=1, replica_groups=mesh['dp'=8,'col'=4] {'dp'}, dimensions={0}, use_global_device_ids=true | all-gather | bytes 147456 | tf_op jit(solution)/shard_map/all_gather | solution.py:88
  89.4 78.1 %all-gather.3.cloned.1.call-done = bf16[512,32,512]{2,0,1:T(8,128)(2,1)} async-done(((bf16[512,32,128]{2,0,1:T(8,128)(2,1)}), bf16[512,32,512]{2,0,1:T(8,128)(2,1)}) %all-gather.3.cloned.1.call-update) | async-done | bytes 16777232 | tf_op jit(solution)/shard_map/all_gather | solution.py:101
  167.5 13.5 %add_convert_fusion = (bf16[512,32,128]{2,0,1:T(8,128)(2,1)}, f32[512,32,128]{2,0,1:T(8,128)}) fusion(f32[32,128]{1,0:T(8,128)S(1)} %get-tuple-element.132, f32[32,128]{1,0:T(8,128)S(1)} %get-tuple-element.131, f32[32,128]{1,0:T(8,128)S(1)} %get-tuple-element.134, f32[512,32,128]{2,0,1:T(8,128)} %get-tuple-element.143, ...), kind=kOutput, calls=%fused_computation.18 | convolution fusion | flops 2176843776 | bytes 37945344 | tf_op jit(solution)/shard_map/dot_general | solution.py:37
  181.7 22.0 %psum.161 = f32[]{:T(128)} all-reduce(f32[]{:T(128)} %convert_reduce_fusion.1), channel_id=1, replica_groups=mesh['dp'=8,'col'=4] {'dp'}, use_global_device_ids=true, to_apply=%region_3.4 | all-reduce | flops 1 | bytes 8 | tf_op jit(solution)/shard_map/psum | solution.py:91
  203.8 0.7 multiply_reduce_fusion.8
  204.7 41.3 %all_gather.15 = bf16[32,512,16]{0,2,1:T(8,128)(2,1)S(1)} all-gather(bf16[32,64,16]{0,2,1:T(8,128)(2,1)S(1)} %copy.63), channel_id=1, replica_groups=mesh['dp'=8,'col'=4] {'dp'}, dimensions={1}, use_global_device_ids=true | all-gather | bytes 589824 | tf_op jit(solution)/shard_map/all_gather | solution.py:89
  246.0 2.2 copy.64
  248.9 40.5 %all-gather.5.cloned.1.call-done = bf16[512,32,512]{2,0,1:T(8,128)(2,1)} async-done(((bf16[512,32,128]{2,0,1:T(8,128)(2,1)}), bf16[512,32,512]{2,0,1:T(8,128)(2,1)}) %all-gather.5.cloned.1.call-update) | async-done | bytes 16777232 | tf_op jit(solution)/shard_map/all_gather | solution.py:106
  289.4 8.1 fusion.35
  298.0 0.6 multiply_reduce_fusion.13
  298.6 0.9 convert_reduce_fusion
  299.5 7.8 bitcast_multiply_fusion
  307.4 3.2 copy-done
  310.6 9.1 fusion.15
  319.7 8.1 fusion.36
  327.8 7.5 copy.88
  335.2 8.4 reshape.171
  343.9 16.8 %fusion.11 = f32[512,32,512]{2,0,1:T(8,128)} fusion(f32[512,32,128]{2,0,1:T(8,128)} %copy-done, f32[32,128]{1,0:T(8,128)S(1)} %get-tuple-element.131, bf16[512,128]{1,0:T(8,128)(2,1)S(1)} %all_gather.18), kind=kOutput, calls=%fused_computation.30 | convolution fusion | flops 2151677952 | bytes 42090496 | tf_op jit(solution)/shard_map/rmo,ko->rmk/dot_general | solution.py:132
  360.8 0.8 copy-done.8
  361.6 0.6 multiply_reduce_fusion.10
  364.9 0.7 copy.72
  365.5 0.7 copy.70
  366.2 1.7 copy.90
  369.3 11.8 %reduce-scatter.11.cloned.1.call-done = f32[64,128]{1,0:T(8,128)} async-done(((f32[512,128]{1,0:T(8,128)}), f32[64,128]{1,0:T(8,128)}) %reduce-scatter.11.cloned.1.call-update) | async-done | bytes 32784 | tf_op jit(solution)/shard_map/reduce_scatter | solution.py:156
  381.1 1.4 fusion.28
  382.5 64.2 %reduce-scatter.13.cloned.1.call-done = f32[64,512]{1,0:T(8,128)} async-done(((f32[512,512]{1,0:T(8,128)}), f32[64,512]{1,0:T(8,128)}) %reduce-scatter.13.cloned.1.call-update) | async-done | bytes 131088
  446.7 1.3 reshape.172
  448.7 0.8 fusion.32
  449.6 233.7 %reduce-scatter.7.cloned.1.call-done = f32[512,32,128]{2,0,1:T(8,128)} async-done(((f32[512,32,512]{2,0,1:T(8,128)}), f32[512,32,128]{2,0,1:T(8,128)}) %reduce-scatter.7.cloned.1.call-update) | async-done | bytes 8388624 | tf_op jit(solution)/shard_map/reduce_scatter | solution.py:135
  683.3 21.0 %multiply_reduce_fusion.1 = (f32[]{:T(128)}, f32[32,128]{1,0:T(8,128)S(1)}, f32[32,128]{1,0:T(8,128)S(1)}, f32[32,128]{1,0:T(8,128)S(1)}, f32[32,128]{1,0:T(8,12...) fusion(f32[512]{0:T(512)} %copy-done.28, f32[32,128]{1,0:T(8,128)} %copy-done.22, ...), kind=kLoop, calls=%fused_computation.11 | loop fusion | flops 69185536 | bytes 50497544 | tf_op jit(solution)/shard_map/reduce_sum | solution.py:149
  704.3 1.1 multiply_convert_fusion.3
  705.7 14.9 %multiply_reduce_fusion = f32[768,32]{0,1:T(8,128)} fusion(f32[768,512]{0,1:T(8,128)S(1)} %copy-done.5, bf16[512,32,128]{2,0,1:T(8,128)(2,1)S(1)} %multiply_convert_fusion.3, bf16[768,128]{1,0:T(8,128)(2,1)S(1)} %all_gather.16), kind=kOutput, calls=%fused_computation | convolution fusion | flops 3246366720 | bytes 6062080 | tf_op jit(solution)/shard_map/rmd,kd->rmk/dot_general | solution.py:143
  720.7 0.6 copy-done.19
  721.9 9.6 fusion.14
  731.5 109.8 %all-reduce.8.cloned.1.call-done = f32[32,768]{1,0:T(8,128)} async-done(((f32[32,768]{1,0:T(8,128)}), f32[32,768]{1,0:T(8,128)}) %all-reduce.8.cloned.1.call-update) | async-done | bytes 98320 | tf_op jit(solution)/shard_map/psum | solution.py:151
  841.3 1.5 multiply_reduce_fusion.9
  843.5 1.6 multiply_subtract_fusion.1
  845.1 70.2 %all-reduce.6.cloned.1.call-done = f32[5,32,128]{2,1,0:T(8,128)} async-done(((f32[5,32,128]{2,1,0:T(8,128)}), f32[5,32,128]{2,1,0:T(8,128)}) %all-reduce.6.cloned.1.call-update) | async-done | bytes 81936 | tf_op jit(solution)/shard_map/psum | solution.py:150
  915.3 1.0 multiply_reduce_fusion.11
  916.3 64.3 %reduce-scatter.9.cloned.1.call-done = f32[96,128]{1,0:T(8,128)} async-done(((f32[768,128]{1,0:T(8,128)}), f32[96,128]{1,0:T(8,128)}) %reduce-scatter.9.cloned.1.call-update) | async-done | bytes 49168 | tf_op jit(solution)/shard_map/reduce_scatter | solution.py:155
  980.6 0.9 fusion.25
  981.6 5.7 all-reduce.2
  988.5 36.7 %all-reduce.1 = (f32[128]{0:T(128)S(1)}, f32[]{:T(128)}, f32[]{:T(128)}, f32[128]{0:T(128)S(1)}, f32[32]{0:T(128)S(1)}, /*index=5*/f32[32,16]{1,0:T(8,128)S(1)}, f32[32,16]{1,0:T(8,128)S(1)}, f32[]{:T(128)}) all-reduce(f32[128]{0:T(128)S(1)} %get-tuple-element.86, f32[]{:T(128)} %get-tuple-element.127, ...), channel_id=1, replica_groups=mesh['dp'=8,'col'=4] {'dp'}, use_global_device_ids=true, to_apply=%region_9.10 | all-reduce | flops 1315 | bytes 10520 | tf_op jit(solution)/shard_map/psum | solution.py:168
  1025.8 0.7 copy.75
  1026.5 0.6 multiply_reduce_fusion.18
  1027.8 0.7 copy.77
  1028.5 0.7 copy.74
  1029.2 0.8 multiply_reduce_fusion.7
  1031.3 1.5 multiply_reduce_fusion.14
  1032.8 0.7 multiply_reduce_fusion.16
  1033.5 37.4 %all-reduce = (f32[]{:T(128)}, f32[]{:T(128)}, f32[]{:T(128)}, f32[]{:T(128)}, f32[]{:T(128)}, /*index=5*/f32[]{:T(128)}, f32[5]{0:T(128)S(1)}, f32[5]{0:T(128)S(1)}, f32[]{:T(128)}, f32[]{:T(128)}) all-reduce(f32[]{:T(128)} %multiply_reduce_fusion.14, f32[]{:T(128)} %get-tuple-element.136, ...), channel_id=1, replica_groups=mesh['dp'=8,'col'=4] {'dp','col'}, use_global_device_ids=true, to_apply=%region_15.16 | all-reduce | flops 18 | bytes 144 | tf_op jit(solution)/shard_map/psum | solution.py:203
  1076.5 0.7 copy.76
  1077.2 0.9 multiply_subtract_fusion
  1078.1 0.7 multiply_subtract_fusion.4
  1078.8 1.5 multiply_subtract_fusion.3
  1080.3 1.6 multiply_subtract_fusion.2
  1081.9 1.5 copy.100
  1083.4 1.5 copy.101
  (130 shorter events, 6.3 us)
Async XLA Ops:
  7.2 160.3 %all-gather.3.cloned.1.call-start = ((), (), s32[]{:S(2)}) async-start(), calls=%async_computation.4 | async-start | bytes 20971520 | tf_op jit(solution)/shard_map/all_gather | solution.py:101
  9.6 48.6 %copy-start.23 = (f32[32,128]{1,0:T(8,128)}, f32[32,128]{1,0:T(8,128)S(1)}, u32[]{:S(2)}) copy-start(f32[32,128]{1,0:T(8,128)S(1)} %get-tuple-element.133) | copy-start | bytes 49156
  9.6 157.9 %copy-start.13 = (f32[32,128]{1,0:T(8,128)}, f32[32,128]{1,0:T(8,128)S(1)}, u32[]{:S(2)}) copy-start(f32[32,128]{1,0:T(8,128)S(1)} %get-tuple-element.135) | copy-start | bytes 49156
  9.6 157.9 %copy-start.24 = (f32[32,128]{1,0:T(8,128)}, f32[32,128]{1,0:T(8,128)S(1)}, u32[]{:S(2)}) copy-start(f32[32,128]{1,0:T(8,128)S(1)} %get-tuple-element.134) | copy-start | bytes 49156
  9.6 289.9 %copy-start.22 = (f32[32,128]{1,0:T(8,128)}, f32[32,128]{1,0:T(8,128)S(1)}, u32[]{:S(2)}) copy-start(f32[32,128]{1,0:T(8,128)S(1)} %get-tuple-element.132) | copy-start | bytes 49156
  43.1 15.1 %copy-start.1 = (f32[512,768]{0,1:T(8,128)}, f32[512,768]{0,1:T(8,128)S(1)}, u32[]{:S(2)}) copy-start(f32[512,768]{0,1:T(8,128)S(1)} %fusion.12) | copy-start | bytes 4718596
  43.1 15.1 %copy-start.17 = (f32[64,128]{1,0:T(8,128)S(1)}, f32[64,128]{1,0:T(8,128)}, u32[]{:S(2)}) copy-start(f32[64,128]{1,0:T(8,128)} %param.24) | copy-start | bytes 98308
  58.2 231.2 %all-gather.5.cloned.1.call-start = ((), (), s32[]{:S(2)}) async-start(), calls=%async_computation.5 | async-start | bytes 20971520 | tf_op jit(solution)/shard_map/all_gather | solution.py:106
  167.5 13.6 %copy-start.29 = (s32[512]{0:T(512)S(1)}, s32[512]{0:T(512)}, u32[]{:S(2)}) copy-start(s32[512]{0:T(512)} %param.21) | copy-start | bytes 6148
  167.5 36.2 %copy-start.27 = (f32[32,16]{0,1:T(8,128)S(1)}, f32[32,16]{0,1:T(8,128)}, u32[]{:S(2)}) copy-start(f32[32,16]{0,1:T(8,128)} %param.28) | copy-start | bytes 6148
  167.5 36.3 %copy-start.6 = (f32[32,64,16]{1,2,0:T(8,128)S(1)}, f32[32,64,16]{1,2,0:T(8,128)}, u32[]{:S(2)}) copy-start(f32[32,64,16]{1,2,0:T(8,128)} %param.25) | copy-start | bytes 393220
  181.0 67.9 %copy-start.37 = (s32[512]{0:T(512)S(1)}, s32[512]{0:T(512)}, u32[]{:S(2)}) copy-start(s32[512]{0:T(512)} %param.22) | copy-start | bytes 6148
  181.1 200.0 %reduce-scatter.11.cloned.1.call-start = ((), (), s32[]{:S(2)}) async-start(), calls=%async_computation.8 | async-start | bytes 294912 | tf_op jit(solution)/shard_map/reduce_scatter | solution.py:156
  203.7 94.3 %copy-start.28 = (f32[512]{0:T(512)}, f32[512]{0:T(512)S(1)}, u32[]{:S(2)}) copy-start(f32[512]{0:T(512)S(1)} %convert_element_type.51) | copy-start | bytes 6148
  307.4 3.2 copy-start
  319.7 127.0 %reduce-scatter.13.cloned.1.call-start = ((), (), s32[]{:S(2)}) async-start(), calls=%async_computation.11 | async-start | bytes 1179648
  343.6 339.6 %reduce-scatter.7.cloned.1.call-start = ((), (), s32[]{:S(2)}) async-start(), calls=%async_computation.6 | async-start | bytes 41943040 | tf_op jit(solution)/shard_map/reduce_scatter | solution.py:135
  360.7 0.9 copy-start.8
  360.7 4.2 copy-start.30
  360.7 4.8 copy-start.31
  360.7 5.5 copy-start.2
  360.7 7.8 copy-start.7
  360.7 480.6 %all-reduce.8.cloned.1.call-start = ((), (), s32[]{:S(2)}) async-start(), calls=%async_computation.10 | async-start | bytes 196608 | tf_op jit(solution)/shard_map/psum | solution.py:151
  448.6 628.6 %copy-start.3 = (f32[32,64,16]{1,2,0:T(8,128)}, f32[32,64,16]{1,2,0:T(8,128)S(1)}, u32[]{:S(2)}) copy-start(f32[32,64,16]{1,2,0:T(8,128)S(1)} %copy.89) | copy-start | bytes 393220
  449.5 627.6 %copy-start.15 = (f32[32,64]{1,0:T(8,128)}, f32[32,64]{1,0:T(8,128)S(1)}, u32[]{:S(2)}) copy-start(f32[32,64]{1,0:T(8,128)S(1)} %get-tuple-element.161) | copy-start | bytes 24580
  683.3 21.1 %copy-start.14 = (f32[32,128]{1,0:T(8,128)S(1)}, f32[32,128]{1,0:T(8,128)}, u32[]{:S(2)}) copy-start(f32[32,128]{1,0:T(8,128)} %copy-done.13) | copy-start | bytes 49156
  704.3 1.4 copy-start.5
  705.7 14.9 %copy-start.4 = (bf16[512,32,128]{2,0,1:T(8,128)(2,1)}, bf16[512,32,128]{2,0,1:T(8,128)(2,1)S(1)}, u32[]{:S(2)}) copy-start(bf16[512,32,128]{2,0,1:T(8,128)(2,1)S(1)} %multiply_convert_fusion.3) | copy-start | bytes 12582916
  720.6 194.7 %all-reduce.6.cloned.1.call-start = ((), (), s32[]{:S(2)}) async-start(), calls=%async_computation.9 | async-start | bytes 163840 | tf_op jit(solution)/shard_map/psum | solution.py:150
  720.7 0.6 copy-start.19
  721.4 119.9 %copy-start.20 = (f32[32,768]{1,0:T(8,128)S(1)}, f32[32,768]{1,0:T(8,128)}, u32[]{:S(2)}) copy-start(f32[32,768]{1,0:T(8,128)} %param.36) | copy-start | bytes 294916
  721.4 193.9 %copy-start.21 = (f32[5,32,128]{2,1,0:T(8,128)S(1)}, f32[5,32,128]{2,1,0:T(8,128)}, u32[]{:S(2)}) copy-start(f32[5,32,128]{2,1,0:T(8,128)} %param.35) | copy-start | bytes 245764
  721.4 260.2 %copy-start.38 = (f32[64]{0:T(128)S(1)}, f32[64]{0:T(128)}, u32[]{:S(2)}) copy-start(f32[64]{0:T(128)} %get-tuple-element.89) | copy-start | bytes 772
  721.4 265.8 %copy-start.40 = (f32[96]{0:T(128)S(1)}, f32[96]{0:T(128)}, u32[]{:S(2)}) copy-start(f32[96]{0:T(128)} %param.29) | copy-start | bytes 1156
  721.4 266.4 %copy-start.41 = (f32[64]{0:T(128)S(1)}, f32[64]{0:T(128)}, u32[]{:S(2)}) copy-start(f32[64]{0:T(128)} %param.31) | copy-start | bytes 772
  721.4 267.0 %copy-start.25 = (f32[32,16]{1,0:T(8,128)S(1)}, f32[32,16]{1,0:T(8,128)}, u32[]{:S(2)}) copy-start(f32[32,16]{1,0:T(8,128)} %get-tuple-element.121) | copy-start | bytes 6148
  721.4 267.0 %copy-start.36 = (f32[128]{0:T(128)S(1)}, f32[128]{0:T(128)}, u32[]{:S(2)}) copy-start(f32[128]{0:T(128)} %get-tuple-element.88) | copy-start | bytes 1540
  721.5 305.0 %copy-start.16 = (f32[32,16]{1,0:T(8,128)S(1)}, f32[32,16]{1,0:T(8,128)}, u32[]{:S(2)}) copy-start(f32[32,16]{1,0:T(8,128)} %copy.72) | copy-start | bytes 6148
  721.5 307.0 %copy-start.26 = (f32[32,16]{1,0:T(8,128)S(1)}, f32[32,16]{1,0:T(8,128)}, u32[]{:S(2)}) copy-start(f32[32,16]{1,0:T(8,128)} %copy.70) | copy-start | bytes 6148
  721.5 309.8 %copy-start.42 = (f32[128]{0:T(128)S(1)}, f32[128]{0:T(128)}, u32[]{:S(2)}) copy-start(f32[128]{0:T(128)} %param.32) | copy-start | bytes 1540
  721.5 309.8 %copy-start.43 = (f32[128]{0:T(128)S(1)}, f32[128]{0:T(128)}, u32[]{:S(2)}) copy-start(f32[128]{0:T(128)} %param.30) | copy-start | bytes 1540
  721.5 311.3 %copy-start.11 = (f32[64,128]{1,0:T(8,128)S(1)}, f32[64,128]{1,0:T(8,128)}, u32[]{:S(2)}) copy-start(f32[64,128]{1,0:T(8,128)} %reduce-scatter.11.cloned.1.call-done) | copy-start | bytes 98308
  721.5 312.0 %copy-start.39 = (f32[5]{0:T(128)S(1)}, f32[5]{0:T(128)}, u32[]{:S(2)}) copy-start(f32[5]{0:T(128)} %broadcast_multiply_fusion.2) | copy-start | bytes 64
  721.5 356.5 %copy-start.18 = (f32[64,128]{1,0:T(8,128)S(1)}, f32[64,128]{1,0:T(8,128)}, u32[]{:S(2)}) copy-start(f32[64,128]{1,0:T(8,128)} %param.24) | copy-start | bytes 98308
  721.5 357.2 %copy-start.12 = (f32[96,128]{1,0:T(8,128)S(1)}, f32[96,128]{1,0:T(8,128)}, u32[]{:S(2)}) copy-start(f32[96,128]{1,0:T(8,128)} %param.23) | copy-start | bytes 147460
  721.5 259.1 %reduce-scatter.9.cloned.1.call-start = ((), (), s32[]{:S(2)}) async-start(), calls=%async_computation.7 | async-start | bytes 442368 | tf_op jit(solution)/shard_map/reduce_scatter | solution.py:155
  842.8 242.1 %copy-start.9 = (f32[32,768]{1,0:T(8,128)}, f32[32,768]{1,0:T(8,128)S(1)}, u32[]{:S(2)}) copy-start(f32[32,768]{1,0:T(8,128)S(1)} %get-tuple-element.168) | copy-start | bytes 294916
  916.3 168.6 %copy-start.10 = (f32[5,32,128]{2,1,0:T(8,128)}, f32[5,32,128]{2,1,0:T(8,128)S(1)}, u32[]{:S(2)}) copy-start(f32[5,32,128]{2,1,0:T(8,128)S(1)} %get-tuple-element.165) | copy-start | bytes 245764
  987.8 97.1 %copy-start.32 = (f32[96]{0:T(128)}, f32[96]{0:T(128)S(1)}, u32[]{:S(2)}) copy-start(f32[96]{0:T(128)S(1)} %get-tuple-element.153) | copy-start | bytes 1156
  988.4 96.5 %copy-start.33 = (f32[64]{0:T(128)}, f32[64]{0:T(128)S(1)}, u32[]{:S(2)}) copy-start(f32[64]{0:T(128)S(1)} %get-tuple-element.157) | copy-start | bytes 772
  1031.3 53.7 %copy-start.34 = (f32[128]{0:T(128)}, f32[128]{0:T(128)S(1)}, u32[]{:S(2)}) copy-start(f32[128]{0:T(128)S(1)} %get-tuple-element.158) | copy-start | bytes 1540
  1031.3 53.7 %copy-start.35 = (f32[128]{0:T(128)}, f32[128]{0:T(128)S(1)}, u32[]{:S(2)}) copy-start(f32[128]{0:T(128)S(1)} %get-tuple-element.154) | copy-start | bytes 1540
Sparse Core Ops, SparseCore 0:
  58.3 109.1 all-gather.2
  181.2 108.1 all-gather.4
  319.8 61.2 reduce-scatter.10
  384.3 62.3 reduce-scatter.12
  449.3 233.8 reduce-scatter.6
  720.7 120.5 all-reduce.7
  845.7 69.5 all-reduce.5
  919.5 61.0 reduce-scatter.8
where the time goes:
time: 1100 us; the launch traced here: 1090 us
  waiting for transfers between devices  673 us (61%)
  blocking collectives  206 us (19%)
  matrix products  103 us (9%)
  other arithmetic  47.4 us (4%)
  local copies, waits for them, and re-layouts  35 us (3%)
  between operations  29.7 us (3%)
    reduce_scatter x1, waiting for transfers between devices, local(): lax.psum_scatter(partial_in, 'col', scatter_dimension=2, tiled=True)  234 us
    psum x1, waiting for transfers between devices, local(): lax.psum((gain_part, residual_part, branch_part), ('dp', 'col'))  110 us
    all_gather x1, waiting for transfers between devices, local(): second_all = lax.all_gather(second_in, 'col', axis=2, tiled=True)  78.1 us
    psum x1, waiting for transfers between devices, local(): lax.psum((adapter_part, bias_part, loss_part), 'dp')  70.2 us
    unnamed x9, waiting for transfers between devices  64.4 us
    reduce_scatter x1, waiting for transfers between devices, local(): lax.psum_scatter(first_part, 'dp', scatter_dimension=0, tiled=True)  64.3 us
    all_gather x1, blocking collectives, local(): lax.all_gather(w_head.astype(jnp.bfloat16), 'dp', axis=1, tiled=True)  41.3 us
    all_gather x1, waiting for transfers between devices, local(): lax.all_gather(stream_two.astype(jnp.bfloat16), 'col', axis=2, tiled=True)  40.5 us
  transfers between devices with their start and end apart: 8, of which 8 were waited for; matrix products, arithmetic and copies ran while one was open for 6% of the time, Pallas kernels for 0%

commit v1 on v0

v1 whole, which is shorter than its diff:
```python
import functools
import jax, jax.numpy as jnp
from jax import lax
from jax.experimental import pallas as pl
from jax.experimental.pallas import tpu as pltpu
from jax.sharding import PartitionSpec as P

FEATS, BINS, CLASSES = 16, 48, 16
STEP = 10
EPS_SQUARE = 1e-30
CLIP_LIMIT = 1.0
RELATIVE_RATE = 0.4
RATE_FLOOR = 0.001
R = 32
f32, bf16 = jnp.float32, jnp.bfloat16

def dot(a, b):
    return jnp.dot(a, b, preferred_element_type=f32)
def dot_t(a, b):
    return lax.dot_general(a, b, (((1,), (1,)), ((), ())), preferred_element_type=f32)
def t_dot(a, b):
    return lax.dot_general(a, b, (((0,), (0,)), ((), ())), preferred_element_type=f32)

MESH = pl.DeviceIdType.MESH


def far(array):
    return pltpu.with_memory_space_constraint(array, pltpu.HBM)


HIGH = lax.Precision.HIGHEST
VM = pl.BlockSpec(memory_space=pltpu.VMEM)
FAR = pl.BlockSpec(memory_space=pltpu.HBM)


def place():
    d, c = lax.axis_index("dp"), lax.axis_index("col")
    return d // 2, d % 2, c // 2, c % 2


def z_other(z, k):
    if k == 0:
        return z
    return [None, z + 1 - 2 * (z % 2), (z + 2) % 4, 3 - z][k]


def other(b, k):
    return 1 - b if k else b


def device(z, y, x, core):
    return (2 * z + y, 2 * x + core)


PLANE = ((0, 1), (1, 0), (1, 1))
DP_PEERS = tuple((kz, ky) for kz in range(4) for ky in range(2))[1:]
COL_PEERS = ((0, 1), (1, 0), (1, 1))
SPLIT = 112


class Sender:
    def __init__(self, send_sem, recv_sem):
        self.send_sem, self.recv_sem, self.count = send_sem, recv_sem, 0
        self.all = []

    def __call__(self, src, dst, target):
        i = self.count
        self.count += 1
        copy = pltpu.make_async_remote_copy(
            src_ref=src, dst_ref=dst, send_sem=self.send_sem.at[i], recv_sem=self.recv_sem.at[i],
            device_id=target, device_id_type=MESH)
        copy.start()
        self.all.append(copy)
        return copy


def greet(targets):
    barrier = pltpu.get_barrier_semaphore()
    for target in targets:
        pl.semaphore_signal(barrier, inc=1, device_id=target, device_id_type=MESH)
    return barrier, len(targets)


def hdot(a, b, dims=((1,), (0,))):
    return lax.dot_general(a, b, (dims, ((), ())), precision=HIGH, preferred_element_type=f32)


def gather_kernel(bin_index, bin_fraction, row_mask, targets, w_first, w_second, w_head, adapters_far,
                  buf, hbuf, adbuf, comp, info, table, recv,
                  w_first_v, w_second_v, w_head_v, adapters, bin_index_v, bin_fraction_v, row_mask_v, targets_v,
                  load_sem, send_sem, recv_sem):
    z, y, x, core = place()
    loads = [pltpu.make_async_copy(src, dst, load_sem.at[i]) for i, (src, dst) in enumerate((
        (w_first, w_first_v), (w_second, w_second_v), (w_head, w_head_v), (adapters_far, adapters),
        (bin_index, bin_index_v), (bin_fraction, bin_fraction_v), (row_mask, row_mask_v), (targets, targets_v)))]
    for load in loads:
        load.start()
    rows = bin_index.shape[1]
    rf, rs = w_first.shape[0], w_second.shape[0]
    me_c = 2 * x + core
    mem = adbuf.shape[2]
    near = [device(z_other(z, kz), other(y, ky), x, core) for kz, ky in DP_PEERS]
    near += [device(z, y, other(x, kx), other(core, kc)) for kx, kc in COL_PEERS]
    near += [device(z, 1 - y, 1 - x, core)]
    barrier, count = greet(near)
    loads[0].wait()
    loads[1].wait()
    buf[z, y, x, core, 0:rf, :] = w_first_v[...].astype(bf16)
    buf[z, y, x, core, rf:rf + rs, :] = w_second_v[...].astype(bf16)
    pl.semaphore_wait(barrier, count)
    send = Sender(send_sem, recv_sem)
    s0, s1 = pl.ds(0, SPLIT), pl.ds(SPLIT, rf + rs - SPLIT)
    own0, own1 = buf.at[z, y, x, core, s0], buf.at[z, y, x, core, s1]
    a0 = [send(own0, own0, device(z_other(z, k), y, x, core)) for k in (1, 2, 3)]
    a1 = [send(own1, own1, device(z, other(y, ky), other(x, kx), core)) for ky, kx in PLANE]
    for load in loads[2:]:
        load.wait()
    hbuf[z, y] = w_head_v[pl.ds(me_c * mem, mem)].reshape(mem * CLASSES, rs).T.astype(bf16)
    adbuf[me_c] = adapters[:, pl.ds(pl.multiple_of(me_c * mem, mem), mem), :]
    slot = rows // 8
    i_row = lax.broadcasted_iota(jnp.int32, (rows, rows), 0)
    i_col = lax.broadcasted_iota(jnp.int32, (rows, rows), 1)
    me_d = 2 * z + y
    wanted = (i_row % slot) * 8 + (i_row // slot + me_d) % 8
    deal = (i_col == wanted).astype(bf16)
    frac = bin_fraction_v[...]
    hi = frac.astype(bf16).astype(f32)
    mask = row_mask_v[...].astype(f32)
    length = jnp.sum(mask, axis=1, keepdims=True)
    high = jnp.floor(length * (1.0 / 16.0))
    c_i = lax.broadcasted_iota(jnp.int32, (CLASSES, rows), 0)
    m_i = lax.broadcasted_iota(jnp.int32, (64, rows), 0)
    marks = jnp.where(m_i == 0, mask, jnp.where(m_i == 1, high, jnp.where(m_i == 2, length - 16.0 * high, 0.0)))
    columns = jnp.concatenate([bin_index_v[...].astype(f32), hi, frac - hi, jnp.where(c_i == targets_v[...], mask, 0.0), marks], axis=0)
    table[...] = dot_t(deal, columns.astype(bf16)).astype(bf16)
    own_rows = pl.ds(pl.multiple_of(me_d * slot, slot), slot)
    recv[own_rows, :] = table[own_rows, :]
    t = []
    for kz, ky in DP_PEERS:
        pz, py = z_other(z, kz), other(y, ky)
        theirs = pl.ds(pl.multiple_of((2 * pz + py) * slot, slot), slot)
        t.append(send(table.at[theirs], recv.at[own_rows], device(pz, py, x, core)))
    h = [send(hbuf.at[z, y], hbuf.at[z, y], device(z_other(z, k), y, x, core)) for k in (1, 2, 3)]
    for kx, kc in COL_PEERS:
        px, pc = other(x, kx), other(core, kc)
        theirs = pl.ds(pl.multiple_of((2 * px + pc) * mem, mem), mem)
        send(adapters.at[:, theirs, :], adbuf.at[me_c], device(z, y, px, pc))
    ad = send.all[-3:]
    for cp in a0:
        cp.wait_recv()
    b0 = [send(buf.at[:, y, x, core, s0], buf.at[:, y, x, core, s0], device(z, other(y, ky), other(x, kx), core))
          for ky, kx in PLANE]
    mate = device(z, y, x, 1 - core)
    for cp in a1:
        cp.wait_recv()
    b1 = [send(buf.at[z, :, :, core, s1], buf.at[z, :, :, core, s1], device(z_other(z, k), y, x, core))
          for k in (1, 2, 3)]
    last = [send(buf.at[:, y, x, core, s0], buf.at[:, y, x, core, s0], mate),
            send(buf.at[z, :, :, core, s1], buf.at[z, :, :, core, s1], mate)]
    for cp in h:
        cp.wait_recv()
    h2 = send(hbuf.at[:, y], hbuf.at[:, y], device(z, 1 - y, x, core))
    for cp in t:
        cp.wait_recv()
    lane8 = lax.broadcasted_iota(jnp.int32, (8, 128), 1)
    got = recv[...]
    mask_row = dot_t((lane8 == 64).astype(bf16), got)
    pos = dot(mask_row.astype(bf16), (i_row < i_col).astype(bf16))
    spot = jnp.where(mask_row > 0.5, pos, -1.0)[0:1]
    perm = (i_row.astype(f32) == spot).astype(bf16)
    comp[...] = dot(perm, got).astype(bf16)
    lane = lax.broadcasted_iota(jnp.int32, (1, 128), 1)
    per_row = jnp.where(lane == 65, 16.0, jnp.where(lane == 66, 1.0, 0.0))
    total = jnp.sum(jnp.sum(got.astype(f32), axis=0, keepdims=True) * per_row, axis=1, keepdims=True) / slot
    info[0:1, :] = jnp.zeros((1, 128), f32) + jnp.sum(mask_row[0:1], axis=1, keepdims=True)
    info[1:2, :] = jnp.zeros((1, 128), f32) + total
    info[2:8, :] = jnp.zeros((6, 128), f32)
    for cp, k in zip(b1, (1, 2, 3)):
        cp.wait_recv()
        pz = z_other(z, k)
        last.append(send(buf.at[pz, :, :, core, s1], buf.at[pz, :, :, core, s1], mate))
    for cp, (ky, kx) in zip(b0, PLANE):
        cp.wait_recv()
        py, px = other(y, ky), other(x, kx)
        last.append(send(buf.at[:, py, px, core, s0], buf.at[:, py, px, core, s0], mate))
    for cp in last + ad + [h2]:
        cp.wait_recv()
    for cp in send.all:
        cp.wait_send()


def call_gather(bin_index, bin_fraction, row_mask, targets, w_first, w_second, w_head, adapters, mem):
    rows = bin_index.shape[1]
    both = w_first.shape[0] + w_second.shape[0]
    return pl.pallas_call(
        gather_kernel,
        out_shape=(
            jax.ShapeDtypeStruct((4, 2, 2, 2, both, 128), bf16),
            jax.ShapeDtypeStruct((4, 2, w_head.shape[2], 128), bf16),
            jax.ShapeDtypeStruct((4, 5, mem, 128), f32),
            jax.ShapeDtypeStruct((rows, 128), bf16),
            jax.ShapeDtypeStruct((8, 128), f32),
        ),
        in_specs=[FAR] * 8, out_specs=(VM,) * 5,
        scratch_shapes=[pltpu.VMEM((rows, 128), bf16), pltpu.VMEM((rows, 128), bf16),
                        pltpu.VMEM(w_first.shape, f32), pltpu.VMEM(w_second.shape, f32),
                        pltpu.VMEM(w_head.shape, f32), pltpu.VMEM(adapters.shape, f32),
                        pltpu.VMEM(bin_index.shape, jnp.int32), pltpu.VMEM(bin_fraction.shape, f32),
                        pltpu.VMEM((1, rows), jnp.int32), pltpu.VMEM((1, rows), jnp.int32),
                        pltpu.SemaphoreType.DMA((8,)),
                        pltpu.SemaphoreType.DMA((40,)), pltpu.SemaphoreType.DMA((40,))],
        compiler_params=pltpu.CompilerParams(collective_id=0, has_side_effects=True, vmem_limit_bytes=16 << 20),
    )(*map(far, (bin_index, bin_fraction, row_mask.reshape(1, -1), targets.reshape(1, -1),
                 w_first, w_second, w_head, adapters)))


def seg_max(x):
    lane = lax.broadcasted_iota(jnp.int32, x.shape, 1)
    n = x.shape[1]
    for s in (1, 2, 4, 8):
        up = pltpu.roll(x, n - s, 1)
        dn = pltpu.roll(x, s, 1)
        x = jnp.maximum(x, jnp.where((lane & s) == 0, up, dn))
    return x


def compute_kernel(members, buf, hbuf, adbuf, comp, info, gains_far, bias_far,
                   gbuf, hb, small,
                   w1, w2, w2t, head, headt, adapters, gains, enc_all, fog_all,
                   first_acc, second_acc, head_acc, adapt, gain_acc, sums, gains_all, bias_all, load_sem):
    rows_all = comp.shape[0]
    enc_w, width = w1.shape
    mem = adbuf.shape[2]
    hw = mem * CLASSES
    rf, rs = enc_w // 8, width // 8
    me_c = lax.axis_index("col")
    loads = [pltpu.make_async_copy(gains_far, gains_all, load_sem.at[0]),
             pltpu.make_async_copy(bias_far, bias_all, load_sem.at[1])]
    for load in loads:
        load.start()
    for d in range(8):
        for c in range(4):
            lanes = slice(128 * c, 128 * c + 128)
            w1[rf * d:rf * (d + 1), lanes] = buf[d // 2, d % 2, c // 2, c % 2, 0:rf, :]
            w2[rs * d:rs * (d + 1), lanes] = buf[d // 2, d % 2, c // 2, c % 2, rf:rf + rs, :]
        head[rs * d:rs * (d + 1), :] = hbuf[d // 2, d % 2]
    for c in range(4):
        adapters[:, :, 128 * c:128 * c + 128] = adbuf[c]
    w2t[...] = w2[...].T
    headt[...] = head[...].T
    for load in loads:
        load.wait()
    own = pl.ds(pl.multiple_of(me_c * mem, mem), mem)
    gains[...] = gains_all[own, :]
    owner = lax.broadcasted_iota(jnp.int32, (1, hw), 1) // CLASSES
    fold = (lax.broadcasted_iota(jnp.int32, (CLASSES, hw), 1) % CLASSES
            == lax.broadcasted_iota(jnp.int32, (CLASSES, hw), 0)).astype(f32)
    wide = hdot(bias_all[...], fold, ((0,), (0,)))
    at = lax.broadcasted_iota(jnp.int32, (members, hw), 0)
    bias = jnp.sum(jnp.where(at == me_c * mem + owner, wide, 0.0), axis=0, keepdims=True)
    n_rows = jnp.max(info[0:1, :]).astype(jnp.int32)
    loss_scale = 1.0 / (members * info[1:2, :])
    tiles = (n_rows + (R - 1)) // R
    fog_all[...] = jnp.zeros_like(fog_all)
    enc_all[...] = jnp.zeros_like(enc_all)
    second_acc[...] = jnp.zeros_like(second_acc)
    head_acc[...] = jnp.zeros_like(head_acc)
    adapt[...] = jnp.zeros_like(adapt)
    sums[...] = jnp.zeros_like(sums)

    kk = lax.broadcasted_iota(jnp.int32, (128, enc_w), 1)
    ll = lax.broadcasted_iota(jnp.int32, (128, enc_w), 0)
    ff = ll & (FEATS - 1)
    spread = ((ll < 48) & (kk >= ff * BINS) & (kk < (ff + 1) * BINS)).astype(bf16)
    lev = (lax.broadcasted_iota(jnp.int32, (1, enc_w), 1) % BINS).astype(f32)
    l2 = lax.broadcasted_iota(jnp.int32, (128, 2 * hw), 0)
    c2 = lax.broadcasted_iota(jnp.int32, (128, 2 * hw), 1)
    oh_spread = (l2 == jnp.where(c2 < hw, 48 + (c2 & (CLASSES - 1)), 64)).astype(bf16)
    s_i = lax.broadcasted_iota(jnp.int32, (hw, hw), 0) // CLASSES
    s_j = lax.broadcasted_iota(jnp.int32, (hw, hw), 1) // CLASSES
    seg = (s_i == s_j).astype(bf16)

    def tile(t, carry):
        rows = pl.ds(pl.multiple_of(t * R, R), R)
        T = comp[rows, :]
        enc = jnp.clip(dot(T, spread) - lev, 0.0, 1.0)
        enc_all[rows, :] = enc.astype(bf16)
        fin = jnp.concatenate([(enc * gains[m:m + 1, :]).astype(bf16) for m in range(mem)], axis=0)
        fo = dot(fin, w1[...])
        hs, us, sos, sins = [], [], [], []
        res = jnp.zeros((R, width), f32)
        for m in range(mem):
            h = fo[m * R:(m + 1) * R] * (0.5 * adapters[0, m:m + 1, :]) + 0.5 * adapters[1, m:m + 1, :]
            u = 1.0 + jnp.tanh(h)
            so = h * u
            res += so * so
            hs.append(h)
            us.append(u)
            sos.append(so)
            sins.append((so * adapters[2, m:m + 1, :]).astype(bf16))
        sin = jnp.concatenate(sins, axis=0)
        s2 = dot(sin, w2[...])
        h2s, u2s, brs, sts = [], [], [], []
        bres = jnp.zeros((R, width), f32)
        for m in range(mem):
            h = s2[m * R:(m + 1) * R] * (0.5 * adapters[3, m:m + 1, :]) + 0.5 * adapters[4, m:m + 1, :]
            u = 1.0 + jnp.tanh(h)
            br = h * u
            bres += br * br
            h2s.append(h)
            u2s.append(u)
            brs.append(br)
            sts.append((sos[m] + br).astype(bf16))
        st = jnp.concatenate(sts, axis=0)
        lo = dot(st, head[...])
        logits = bias
        for m in range(mem):
            logits = logits + jnp.where(owner == m, lo[m * R:(m + 1) * R], 0.0)
        top = seg_max(logits)
        ex = jnp.exp(logits - top)
        exh = ex.astype(bf16)
        exl = (ex - exh.astype(f32)).astype(bf16)
        tot = dot(exh, seg) + dot(exl, seg)
        ohm = dot(T, oh_spread)
        oh, mk = ohm[:, :hw], ohm[:, hw:]
        loss_c = (top + jnp.log(tot) - logits) * oh
        lgf = ((ex / tot * mk - oh) * loss_scale).astype(bf16).astype(f32)
        lgm = jnp.concatenate([jnp.where(owner == m, lgf, 0.0).astype(bf16) for m in range(mem)], axis=0)
        head_acc[...] += t_dot(lgm, st)
        sg = dot(lgm, headt[...])
        ogs = []
        for m in range(mem):
            pg = sg[m * R:(m + 1) * R] * (u2s[m] + brs[m] * (2.0 - u2s[m]))
            adapt[3, m:m + 1, :] += jnp.sum(pg * h2s[m], axis=0, keepdims=True)
            adapt[4, m:m + 1, :] += jnp.sum(pg, axis=0, keepdims=True)
            ogs.append((pg * (0.5 * adapters[3, m:m + 1, :])).astype(bf16))
        og = jnp.concatenate(ogs, axis=0)
        second_acc[...] += t_dot(sin, og)
        ig = dot(og, w2t[...])
        for m in range(mem):
            igm = ig[m * R:(m + 1) * R]
            adapt[2, m:m + 1, :] += jnp.sum(igm * sos[m], axis=0, keepdims=True)
            one = sg[m * R:(m + 1) * R] + igm * adapters[2, m:m + 1, :]
            low = one * (us[m] + sos[m] * (2.0 - us[m]))
            adapt[0, m:m + 1, :] += jnp.sum(low * hs[m], axis=0, keepdims=True)
            adapt[1, m:m + 1, :] += jnp.sum(low, axis=0, keepdims=True)
            fog_all[m, rows, :] = (low * (0.5 * adapters[0, m:m + 1, :])).astype(bf16)
        spare = jnp.maximum((t + 1) * R - n_rows, 0).astype(f32)
        sums[0:1, :hw] += jnp.sum(lgf, axis=0, keepdims=True)
        sums[1:2, :hw] += jnp.sum(loss_c, axis=0, keepdims=True)
        sums[2:3, :] += jnp.sum(res, axis=0, keepdims=True) - spare * res[R - 1:R]
        sums[3:4, :] += jnp.sum(bres, axis=0, keepdims=True) - spare * bres[R - 1:R]
        return carry

    lax.fori_loop(0, tiles, tile, 0)
    enct = enc_all[...].T
    gcol = jnp.concatenate([gains[...], jnp.zeros((128 - mem, enc_w), f32)], axis=0).T
    for m in range(mem):
        g = dot(enct, fog_all[m])
        gain_acc[:, m:m + 1] = jnp.sum(g * w1[...].astype(f32), axis=1, keepdims=True)
        if m == 0:
            first_acc[...] = g * gcol[:, m:m + 1]
        else:
            first_acc[...] += g * gcol[:, m:m + 1]
    gain_rows = gain_acc[...].T
    for d in range(8):
        for c in range(4):
            lanes = slice(128 * c, 128 * c + 128)
            gbuf[d // 2, d % 2, c // 2, c % 2, 0:rf, :] = first_acc[rf * d:rf * (d + 1), lanes].astype(bf16)
            gbuf[d // 2, d % 2, c // 2, c % 2, rf:rf + rs, :] = second_acc[rs * d:rs * (d + 1), lanes].astype(bf16)
    head_t = head_acc[...].T
    for d in range(8):
        hb[d // 2, d % 2] = head_t[rs * d:rs * (d + 1), :].astype(bf16)
    small[...] = jnp.zeros_like(small)
    a0, a1, a2 = adapt[0], adapt[1], adapt[2]
    a3, a4 = adapt[3], adapt[4]
    fixed = ((a0 - 0.5 * adapters[1] * a1) / adapters[0], 0.5 * a1, a2,
             (a3 - 0.5 * adapters[4] * a4) / adapters[3], 0.5 * a4)
    for m in range(mem):
        for k in range(4):
            for j in range(5):
                small[m, 8 * k + j:8 * k + j + 1, :] = fixed[j][m:m + 1, 128 * k:128 * k + 128]
        for i in range(enc_w // 128):
            small[m, 32 + i:33 + i, :] = gain_rows[m:m + 1, 128 * i:128 * i + 128]
    def four(row):
        return row[:, 0:128] + row[:, 128:256] + row[:, 256:384] + row[:, 384:512]
    small[0, 39:40, :] = sums[1:2, 0:128]
    small[1, 39:40, :] = four(sums[2:3, :])
    small[2, 39:40, :] = four(sums[3:4, :])
    small[3, 39:40, :] = sums[0:1, 0:128]


def call_compute(members, buf, hbuf, adbuf, comp, info, gains, bias):
    rows = comp.shape[0]
    enc_w = gains.shape[1]
    mem = adbuf.shape[2]
    width = adbuf.shape[0] * 128
    hw = mem * CLASSES
    return pl.pallas_call(
        functools.partial(compute_kernel, members),
        out_shape=(
            jax.ShapeDtypeStruct(buf.shape, bf16),
            jax.ShapeDtypeStruct(hbuf.shape, bf16),
            jax.ShapeDtypeStruct((8, 40, 128), f32),
        ),
        in_specs=[VM] * 5 + [FAR] * 2, out_specs=(VM,) * 3,
        scratch_shapes=[
            pltpu.VMEM((enc_w, width), bf16), pltpu.VMEM((width, width), bf16), pltpu.VMEM((width, width), bf16),
            pltpu.VMEM((width, hw), bf16), pltpu.VMEM((hw, width), bf16),
            pltpu.VMEM((5, mem, width), f32), pltpu.VMEM((mem, enc_w), f32),
            pltpu.VMEM((rows, enc_w), bf16), pltpu.VMEM((mem, rows, width), bf16),
            pltpu.VMEM((enc_w, width), f32), pltpu.VMEM((width, width), f32), pltpu.VMEM((hw, width), f32),
            pltpu.VMEM((5, mem, width), f32), pltpu.VMEM((enc_w, 128), f32), pltpu.VMEM((8, width), f32),
            pltpu.VMEM(gains.shape, f32), pltpu.VMEM(bias.shape, f32), pltpu.SemaphoreType.DMA((2,)),
        ],
        compiler_params=pltpu.CompilerParams(vmem_limit_bytes=30 << 20),
    )(buf, hbuf, adbuf, comp, info, far(gains), far(bias))


def reduce_kernel(enc_w, width, members,
                  gbuf, hb, small, info, w_first, w_second, w_head, adapters, gains, head_bias,
                  first_row, first_col, second_row, second_col, head_row, head_col, adapter_sq, gain_sq, bias_sq,
                  o_first_grad, o_first_row, o_first_col, o_first_new,
                  o_second_grad, o_second_row, o_second_col, o_second_new,
                  o_head_grad, o_head_row, o_head_col, o_head_new,
                  o_adapter_grad, o_adapter_sq, o_adapter_new,
                  o_gain_grad, o_gain_sq, o_gain_new,
                  o_bias_grad, o_bias_sq, o_bias_new,
                  o_loss, o_rows, o_residual, o_branch,
                  cbuf, sbuf, plane0, held0, zed0, zed1, held1, plane1, hy, hsum, hz, hcol,
                  fr, gall, ca, cg, colmsg, colall, rowmsg, rowall, msg, msgall, send_sem, recv_sem):
    z, y, x, core = place()
    me_c = 2 * x + core
    rf, rs = w_first.shape[0], w_second.shape[0]
    mem = members // 4
    hw = mem * CLASSES
    decay = 1.0 - STEP ** (-0.8)
    everyone = []
    for kz in range(4):
        for ky in range(2):
            for kx in range(2):
                for kc in range(2):
                    if kz or ky or kx or kc:
                        everyone.append(device(z_other(z, kz), other(y, ky), other(x, kx), other(core, kc)))
    barrier, count = greet(everyone)
    pl.semaphore_wait(barrier, count)
    send = Sender(send_sem, recv_sem)
    s0, s1 = pl.ds(0, SPLIT), pl.ds(SPLIT, rf + rs - SPLIT)
    mate = device(z, y, x, 1 - core)
    swap1 = send(gbuf.at[:, :, :, 1 - core, s1], cbuf.at[:, :, :, s1], mate)
    swap0 = send(gbuf.at[:, :, :, 1 - core, s0], cbuf.at[:, :, :, s0], mate)
    head1 = send(hb.at[:, 1 - y], hy, device(z, 1 - y, x, core))
    deal = [send(small.at[2 * z_other(z, kz) + other(y, ky)], fr.at[i], device(z_other(z, kz), other(y, ky), x, core))
            for i, (kz, ky) in enumerate(DP_PEERS)]
    w1, w2 = w_first[...], w_second[...]
    wh = [w_head[mem * c:mem * (c + 1)].reshape(hw, rs).T for c in range(4)]
    own_w = (jnp.sum(w1 * w1), jnp.sum(w2 * w2), sum(jnp.sum(w * w) for w in wh))
    adapter_w = [jnp.sum(adapters[j] * adapters[j]) for j in range(5)]
    swap1.wait_recv()
    sbuf[:, :, :, s1, :] = (gbuf[:, :, :, core, s1, :].astype(f32) + cbuf[:, :, :, s1, :].astype(f32)).astype(bf16)
    p1 = [send(sbuf.at[z_other(z, k), :, :, s1], zed1.at[k - 1], device(z_other(z, k), y, x, core)) for k in (1, 2, 3)]
    swap0.wait_recv()
    sbuf[:, :, :, s0, :] = (gbuf[:, :, :, core, s0, :].astype(f32) + cbuf[:, :, :, s0, :].astype(f32)).astype(bf16)
    p0 = [send(sbuf.at[:, other(y, ky), other(x, kx), s0], plane0.at[i], device(z, other(y, ky), other(x, kx), core))
          for i, (ky, kx) in enumerate(PLANE)]
    head1.wait_recv()
    hsum[...] = (hb[:, y].astype(f32) + hy[...].astype(f32)).astype(bf16)
    head2 = [send(hsum.at[z_other(z, k)], hz.at[k - 1], device(z_other(z, k), y, x, core)) for k in (1, 2, 3)]
    for cp in deal:
        cp.wait_recv()
    me_d = 2 * z + y
    mine = small[me_d]
    for i in range(7):
        mine = mine + fr[i]
    gall[me_d] = mine
    spread_dp = [send(gall.at[me_d], gall.at[me_d], device(z_other(z, kz), other(y, ky), x, core)) for kz, ky in DP_PEERS]
    for cp in p1:
        cp.wait_recv()
    part = sbuf[z, :, :, s1, :].astype(f32)
    for i in range(3):
        part = part + zed1[i].astype(f32)
    held1[...] = part.astype(bf16)
    q1 = [send(held1.at[other(y, ky), other(x, kx)], plane1.at[i], device(z, other(y, ky), other(x, kx), core))
          for i, (ky, kx) in enumerate(PLANE)]
    for cp in head2:
        cp.wait_recv()
    hown = hsum[z].astype(f32)
    for i in range(3):
        hown = hown + hz[i].astype(f32)
    hcol[me_c] = hown
    head3 = [send(hcol.at[me_c], hcol.at[me_c], device(z, y, other(x, kx), other(core, kc))) for kx, kc in COL_PEERS]
    for cp in p0:
        cp.wait_recv()
    part = sbuf[:, y, x, s0, :].astype(f32)
    for i in range(3):
        part = part + plane0[i].astype(f32)
    held0[...] = part.astype(bf16)
    q0 = [send(held0.at[z_other(z, k)], zed0.at[k - 1], device(z_other(z, k), y, x, core)) for k in (1, 2, 3)]
    for cp in spread_dp:
        cp.wait_recv()
    own8 = pl.ds(pl.multiple_of(8 * me_c, 8), 8)
    ca[me_c] = gall[:, own8, :]
    cg[me_c] = gall[:, 32:40, :]
    spread_col = []
    for kx, kc in COL_PEERS:
        px, pc = other(x, kx), other(core, kc)
        theirs = pl.ds(pl.multiple_of(8 * (2 * px + pc), 8), 8)
        spread_col.append(send(gall.at[:, theirs], ca.at[me_c], device(z, y, px, pc)))
        spread_col.append(send(gall.at[:, 32:40], cg.at[me_c], device(z, y, px, pc)))
    g0 = held0[z].astype(f32)
    g1 = held1[y, x].astype(f32)
    for cp in q1:
        cp.wait_recv()
    for i in range(3):
        g1 = g1 + plane1[i].astype(f32)
    for cp in q0:
        cp.wait_recv()
    for i in range(3):
        g0 = g0 + zed0[i].astype(f32)
    first = g0[0:rf]
    second = jnp.concatenate([g0[rf:SPLIT], g1], axis=0)
    o_first_grad[...] = first
    o_second_grad[...] = second
    first_sq = first * first + EPS_SQUARE
    second_sq = second * second + EPS_SQUARE
    for cp in head3:
        cp.wait_recv()
    hg = [hcol[c] for c in range(4)]
    hsq = [g * g + EPS_SQUARE for g in hg]
    seg8 = (lax.broadcasted_iota(jnp.int32, (mem, hw), 1) // CLASSES
            == lax.broadcasted_iota(jnp.int32, (mem, hw), 0)).astype(f32)
    ones8 = jnp.ones((8, 128), f32)
    hrow = [decay * head_row[mem * c:mem * (c + 1), :]
            + (1.0 - decay) / CLASSES * hdot(seg8, hsq[c], ((1,), (1,))) for c in range(4)]
    hrowx = [hdot(hrow[c], seg8, ((0,), (0,))) for c in range(4)]
    for c in range(4):
        o_head_row[mem * c:mem * (c + 1), :] = hrow[c]
    rowmsg[:, 0:rf] = hdot(ones8, first_sq, ((1,), (1,)))
    rowmsg[:, 128:128 + rs] = hdot(ones8, second_sq, ((1,), (1,)))
    rowall[me_c] = rowmsg[...]
    def add_up(v):
        return jnp.sum(v, axis=0, keepdims=True)
    colmsg[0:1, :] = add_up(first_sq)
    colmsg[1:2, :] = add_up(second_sq)
    for c in range(4):
        colmsg[2 + c:3 + c, :] = add_up(hsq[c])
        colmsg[8 + c:9 + c, :] = add_up(hrowx[c])
    colall[me_d] = colmsg[...]
    r1 = [send(colmsg, colall.at[me_d], device(z_other(z, kz), other(y, ky), x, core)) for kz, ky in DP_PEERS]
    r1 += [send(rowmsg, rowall.at[me_c], device(z, y, other(x, kx), other(core, kc))) for kx, kc in COL_PEERS]
    for cp in spread_col:
        cp.wait_recv()
    fold = (lax.broadcasted_iota(jnp.int32, (CLASSES, hw), 1) % CLASSES
            == lax.broadcasted_iota(jnp.int32, (CLASSES, hw), 0)).astype(f32)
    to8 = (lax.broadcasted_iota(jnp.int32, (8, members), 1) // mem
           == lax.broadcasted_iota(jnp.int32, (8, members), 0)).astype(f32)
    keep = (lax.broadcasted_iota(jnp.int32, (members, hw), 1) // CLASSES
            == lax.broadcasted_iota(jnp.int32, (members, hw), 0) % mem).astype(f32)
    def to_lanes(v):
        return hdot(to8, hdot(v, fold, ((0,), (0,))) * keep)
    def from_lanes(v):
        return hdot(fold, hdot(to8, v, ((0,), (0,))) * keep, ((1,), (1,)))
    def lane_sum(v):
        return jnp.sum(v, axis=1, keepdims=True)
    def total(v):
        return lane_sum(add_up(v))
    def step_size(weight_sq, entries):
        return RELATIVE_RATE * jnp.maximum(RATE_FLOOR, jnp.sqrt(weight_sq / entries))
    def apply(weight, update, update_sq, weight_sq, entries):
        limit = jnp.maximum(1.0, jnp.sqrt(update_sq / entries) / CLIP_LIMIT)
        return weight - step_size(weight_sq, entries) * (update / limit)
    adapter_up = []
    for j in range(5):
        grad = jnp.concatenate([ca[c, :, j, :] for c in range(4)], axis=0)
        sq = decay * adapter_sq[j] + (1.0 - decay) * (grad * grad + EPS_SQUARE)
        o_adapter_grad[j] = grad
        o_adapter_sq[j] = sq
        adapter_up.append(grad * lax.rsqrt(sq))
    for c in range(4):
        for i in range(enc_w // 128):
            o_gain_grad[mem * c:mem * (c + 1), 128 * i:128 * (i + 1)] = cg[c, :, i, :]
    gain = o_gain_grad[...]
    gain_state = decay * gain_sq[...] + (1.0 - decay) * (gain * gain + EPS_SQUARE)
    o_gain_sq[...] = gain_state
    gain_up = gain * lax.rsqrt(gain_state)
    o_gain_new[...] = apply(gains[...], gain_up, total(gain_up * gain_up), total(gains[...] * gains[...]), members * enc_w)
    bias_lanes = jnp.concatenate([cg[c, 3, 7:8, :] for c in range(4)] + [jnp.zeros((4, 128), f32)], axis=0)
    bias = from_lanes(bias_lanes)
    bias_state = decay * bias_sq[...] + (1.0 - decay) * (bias * bias + EPS_SQUARE)
    o_bias_grad[...] = bias
    o_bias_sq[...] = bias_state
    bias_up = bias * lax.rsqrt(bias_state)
    o_bias_new[...] = apply(head_bias[...], bias_up, total(bias_up * bias_up), total(head_bias[...] * head_bias[...]), members * CLASSES)
    rows_total = info[1:2, 0:1]
    o_rows[...] = rows_total
    o_loss[...] = lane_sum(sum(cg[c, 0, 7:8, :] for c in range(4)))
    spread_over = rows_total * (members * width)
    o_residual[...] = jnp.sqrt(lane_sum(sum(cg[c, 1, 7:8, :] for c in range(4))) / spread_over)
    o_branch[...] = jnp.sqrt(lane_sum(sum(cg[c, 2, 7:8, :] for c in range(4))) / spread_over)
    hcol_old = to_lanes(head_col[...])
    for cp in r1:
        cp.wait_recv()
    col_sums = colall[0]
    for d in range(1, 8):
        col_sums = col_sums + colall[d]
    row_sums = (rowall[0] + rowall[1]) + (rowall[2] + rowall[3])
    first_r = decay * first_row[...] + (1.0 - decay) / width * row_sums[0:1, 0:rf]
    second_r = decay * second_row[...] + (1.0 - decay) / width * row_sums[0:1, 128:128 + rs]
    first_c = decay * first_col[...] + (1.0 - decay) / enc_w * col_sums[0:1]
    second_c = decay * second_col[...] + (1.0 - decay) / width * col_sums[1:2]
    head_c = decay * hcol_old[0:4] + (1.0 - decay) / width * col_sums[2:6]
    o_first_row[...] = first_r
    o_second_row[...] = second_r
    o_first_col[...] = first_c
    o_second_col[...] = second_c
    o_head_col[...] = from_lanes(jnp.concatenate([head_c, jnp.zeros((4, 128), f32)], axis=0))
    ones1 = jnp.ones((1, 128), f32)
    first_up = first * lax.rsqrt(hdot(first_r, ones1, ((0,), (0,))) * first_c)
    second_up = second * lax.rsqrt(hdot(second_r, ones1, ((0,), (0,))) * second_c)
    head_up = [hg[c] * lax.rsqrt(hrowx[c] * head_c[c:c + 1] / (col_sums[8 + c:9 + c] / width)) for c in range(4)]
    lane = lax.broadcasted_iota(jnp.int32, (1, 128), 1)
    scalars = [total(first_up * first_up), lane_sum(first_r), total(second_up * second_up), lane_sum(second_r),
               own_w[0], own_w[1], sum(total(u * u) for u in head_up), own_w[2]]
    scalars += [total(u * u) for u in adapter_up] + adapter_w
    line = jnp.zeros((1, 128), f32)
    for i, v in enumerate(scalars):
        line = jnp.where(lane == i, v, line)
    msg[...] = jnp.broadcast_to(line, (8, 128))
    msgall[z, y, x, core] = msg[...]
    r2 = []
    for target in everyone:
        r2.append(send(msg, msgall.at[z, y, x, core], target))
    for c in range(4):
        o_head_grad[mem * c:mem * (c + 1)] = hg[c].T.reshape(mem, CLASSES, rs)
    for cp in r2:
        cp.wait_recv()
    def over_dp(cx, cc):
        out = msgall[0, 0, cx, cc, 0:1, :]
        for d in range(1, 8):
            out = out + msgall[d // 2, d % 2, cx, cc, 0:1, :]
        return out
    s_dp = over_dp(x, core)
    s_all = (over_dp(0, 0) + over_dp(0, 1)) + (over_dp(1, 0) + over_dp(1, 1))
    s_col = (msgall[z, y, 0, 0, 0:1, :] + msgall[z, y, 0, 1, 0:1, :]) + (msgall[z, y, 1, 0, 0:1, :] + msgall[z, y, 1, 1, 0:1, :])
    def item(v, i):
        return lane_sum(jnp.where(lane == i, v, 0.0))
    first_mean = item(s_dp, 1) / enc_w
    o_first_new[...] = apply(w1, first_up * jnp.sqrt(first_mean), item(s_all, 0) * first_mean, item(s_all, 4), enc_w * width)
    second_mean = item(s_dp, 3) / width
    o_second_new[...] = apply(w2, second_up * jnp.sqrt(second_mean), item(s_all, 2) * second_mean, item(s_all, 5), width * width)
    for j in range(5):
        o_adapter_new[j] = apply(adapters[j], adapter_up[j], item(s_col, 8 + j), item(s_col, 13 + j), members * width)
    for c in range(4):
        new = apply(wh[c], head_up[c], item(s_dp, 6), item(s_dp, 7), members * width * CLASSES)
        o_head_new[mem * c:mem * (c + 1)] = new.T.reshape(mem, CLASSES, rs)
    for cp in send.all:
        cp.wait_send()


def call_reduce(gbuf, hb, small, info, w_first, w_second, w_head, adapters, gains, head_bias,
                first_row, first_col, second_row, second_col, head_row, head_col, adapter_sq, gain_sq, bias_sq):
    members, enc_w = gains.shape
    rf, rs = w_first.shape[0], w_second.shape[0]
    both = rf + rs
    late = both - SPLIT
    width = w_first.shape[1] * 4
    def like(a):
        return jax.ShapeDtypeStruct(a.shape, f32)
    def row(a):
        return jax.ShapeDtypeStruct((1, a.shape[0]), f32)
    one = jax.ShapeDtypeStruct((1, 1), f32)
    def buffer(*shape, dtype=f32):
        return pltpu.VMEM(shape, dtype)
    outs = pl.pallas_call(
        functools.partial(reduce_kernel, enc_w, width, members),
        out_shape=(like(w_first), row(first_row), row(first_col), like(w_first),
                   like(w_second), row(second_row), row(second_col), like(w_second),
                   like(w_head), like(head_row), like(head_col), like(w_head),
                   like(adapters), like(adapters), like(adapters),
                   like(gains), like(gains), like(gains),
                   like(head_bias), like(head_bias), like(head_bias), one, one, one, one),
        in_specs=[VM] * 19, out_specs=(VM,) * 25,
        scratch_shapes=[
            buffer(4, 2, 2, both, 128, dtype=bf16), buffer(4, 2, 2, both, 128, dtype=bf16),
            buffer(3, 4, SPLIT, 128, dtype=bf16), buffer(4, SPLIT, 128, dtype=bf16),
            buffer(3, SPLIT, 128, dtype=bf16), buffer(3, 2, 2, late, 128, dtype=bf16),
            buffer(2, 2, late, 128, dtype=bf16), buffer(3, late, 128, dtype=bf16),
            buffer(4, rs, 128, dtype=bf16), buffer(4, rs, 128, dtype=bf16), buffer(3, rs, 128, dtype=bf16),
            buffer(4, rs, 128),
            buffer(7, 40, 128), buffer(8, 40, 128), buffer(4, 8, 8, 128), buffer(4, 8, 8, 128),
            buffer(16, 128), buffer(8, 16, 128), buffer(8, 256), buffer(4, 8, 256),
            buffer(8, 128), buffer(4, 2, 2, 2, 8, 128),
            pltpu.SemaphoreType.DMA((100,)), pltpu.SemaphoreType.DMA((100,)),
        ],
        compiler_params=pltpu.CompilerParams(collective_id=1, has_side_effects=True, vmem_limit_bytes=16 << 20),
    )(gbuf, hb, small, info, w_first, w_second, w_head, adapters, gains, head_bias,
      first_row.reshape(1, -1), first_col.reshape(1, -1), second_row.reshape(1, -1), second_col.reshape(1, -1),
      head_row, head_col, adapter_sq, gain_sq, bias_sq)
    outs = call_store(outs)
    for i in (1, 2, 5, 6):
        outs[i] = outs[i].reshape(-1)
    for i in (21, 22, 23, 24):
        outs[i] = outs[i].reshape(())
    for i in (8, 11):
        outs[i] = outs[i].transpose(0, 2, 1)
    for i in (10, 18, 19, 20):
        outs[i] = outs[i].T
    return tuple(outs)


def store_kernel(count, *refs):
    sems = refs[2 * count]
    copies = [pltpu.make_async_copy(refs[i], refs[count + i], sems.at[i]) for i in range(count)]
    for copy in copies:
        copy.start()
    for copy in copies:
        copy.wait()


def call_store(arrays):
    count = len(arrays)
    return list(pl.pallas_call(
        functools.partial(store_kernel, count),
        out_shape=tuple(jax.ShapeDtypeStruct(a.shape, a.dtype) for a in arrays),
        in_specs=[VM] * count, out_specs=(FAR,) * count,
        scratch_shapes=[pltpu.SemaphoreType.DMA((count,))],
        compiler_params=pltpu.CompilerParams(vmem_limit_bytes=16 << 20),
    )(*arrays))


def local_blocks(bin_index, bin_fraction, row_mask, targets, w_first, w_second, w_head, adapters, gains, head_bias,
          first_row, first_col, second_row, second_col, head_row, head_col, adapter_sq, gain_sq, bias_sq):
    members = gains.shape[0]
    mem = members // 4
    w_head, head_bias, head_col, bias_sq = w_head.transpose(0, 2, 1), head_bias.T, head_col.T, bias_sq.T
    buf, hbuf, adbuf, comp, info = call_gather(
        bin_index.T, bin_fraction.T, row_mask, targets, w_first, w_second, w_head, adapters, mem)
    gbuf, hb, small = call_compute(members, buf, hbuf, adbuf, comp, info, gains, head_bias)
    return call_reduce(gbuf, hb, small, info, w_first, w_second, w_head, adapters, gains, head_bias,
                       first_row, first_col, second_row, second_col, head_row, head_col, adapter_sq, gain_sq, bias_sq)


def finish(weight, update, update_sq, weight_sq, entries):
    rms_update = jnp.sqrt(update_sq / entries)
    rms_weight = jnp.sqrt(weight_sq / entries)
    update = update / jnp.maximum(1.0, rms_update / CLIP_LIMIT)
    return weight - RELATIVE_RATE * jnp.maximum(RATE_FLOOR, rms_weight) * update


def local_any(bin_index, bin_fraction, row_mask, targets, w_first, w_second, w_head, adapters, gains, head_bias,
              first_row, first_col, second_row, second_col, head_row, head_col, adapter_sq, gain_sq, bias_sq):
    count_col = lax.axis_size("col")
    count_dp = lax.axis_size("dp")
    col_place = lax.axis_index("col")
    dp_place = lax.axis_index("dp")
    members, enc_width = gains.shape
    col_width = adapters.shape[2]
    full_width = col_width * count_col
    mem = members // count_col
    rows = row_mask.shape[0]
    decay = 1.0 - STEP ** (-0.8)
    row_total = lax.psum(jnp.sum(row_mask.astype(f32)), "dp")
    hi = bin_fraction.astype(bf16).astype(f32)
    onehot = jax.nn.one_hot(targets, CLASSES, dtype=f32) * row_mask[:, None]
    table = jnp.concatenate([bin_index.astype(f32), hi, bin_fraction - hi, onehot, row_mask[:, None].astype(f32),
                             jnp.zeros((rows, 63), f32)], axis=1).astype(bf16)
    table = table.reshape(rows // count_dp, count_dp, 128)
    table = jnp.roll(table, -dp_place, axis=1).transpose(1, 0, 2).reshape(rows, 128)
    table = lax.all_to_all(table, "dp", 0, 0, tiled=True)
    mask = table[:, 64].astype(jnp.int32)
    spot = jnp.where(mask > 0, jnp.cumsum(mask) - 1, -1)
    comp = jnp.dot((jnp.arange(rows)[:, None] == spot[None, :]).astype(bf16), table, preferred_element_type=f32).astype(bf16)
    info = jnp.zeros((8, 128), f32).at[0].set(jnp.sum(mask).astype(f32)).at[1].set(row_total)

    def whole(part):
        return lax.all_gather(lax.all_gather(part.astype(bf16), "dp", axis=0, tiled=True), "col", axis=1, tiled=True)

    def blocks(full):
        return full.reshape(8, -1, 4, 128).transpose(0, 2, 1, 3)

    def unblock(part):
        return part.astype(f32).reshape(8, 4, -1, 128).transpose(0, 2, 1, 3).reshape(-1, full_width)
    buf = jnp.concatenate([blocks(whole(w_first)), blocks(whole(w_second))], axis=2).reshape(4, 2, 2, 2, -1, 128)
    heads = lax.all_gather(w_head.astype(bf16), "dp", axis=1, tiled=True)
    heads = lax.dynamic_slice_in_dim(heads, col_place * mem, mem, 0)
    hbuf = heads.transpose(1, 0, 2).reshape(4, 2, -1, mem * CLASSES)
    adbuf = lax.dynamic_slice_in_dim(lax.all_gather(adapters, "col", axis=0), col_place * mem, mem, 2)
    gbuf, hb, small = call_compute(members, buf, hbuf, adbuf, comp, info, gains, head_bias.T)
    rf = enc_width // 8
    first_part, second_part = unblock(gbuf[..., :rf, :]), unblock(gbuf[..., rf:, :])
    head_part = hb.astype(f32).reshape(full_width, mem, CLASSES).transpose(1, 0, 2)

    def scatter(part):
        return lax.psum_scatter(lax.psum_scatter(part, "dp", scatter_dimension=0, tiled=True), "col", scatter_dimension=1, tiled=True)
    first_grad, second_grad = scatter(first_part), scatter(second_part)
    head_grad = lax.all_gather(lax.psum_scatter(head_part, "dp", scatter_dimension=1, tiled=True), "col", axis=0, tiled=True)
    adapter_part = small[:, :32].reshape(mem, 4, 8, 128)[:, :, :5].transpose(2, 0, 1, 3).reshape(5, mem, full_width)
    adapter_grad = lax.psum(lax.all_to_all(adapter_part, "col", 2, 1, tiled=True), "dp")
    gain_part = small[:, 32:32 + enc_width // 128].reshape(mem, enc_width)
    bias_part = small[3, 39].reshape(mem, CLASSES)
    gain_grad, bias_grad = lax.psum(
        (lax.all_gather(gain_part, "col", axis=0, tiled=True), lax.all_gather(bias_part, "col", axis=0, tiled=True)), "dp")
    loss_sum, residual_sq, branch_sq = lax.psum(jnp.sum(small[:3, 39], axis=1), ("dp", "col"))
    first_square = first_grad * first_grad + EPS_SQUARE
    second_square = second_grad * second_grad + EPS_SQUARE
    head_square = head_grad * head_grad + EPS_SQUARE
    first_rowsum, second_rowsum = lax.psum(
        (jnp.sum(first_square, axis=1), jnp.sum(second_square, axis=1)), "col"
    )
    first_row_new = decay * first_row + (1.0 - decay) * (first_rowsum / full_width)
    second_row_new = decay * second_row + (1.0 - decay) * (second_rowsum / full_width)
    head_row_new = decay * head_row + (1.0 - decay) * jnp.mean(head_square, axis=-1)
    stats = lax.psum(
        (
            jnp.sum(first_square, axis=0),
            jnp.sum(second_square, axis=0),
            jnp.sum(head_square, axis=1),
            jnp.sum(first_row_new),
            jnp.sum(second_row_new),
            jnp.sum(head_row_new, axis=1),
        ),
        "dp",
    )
    first_colsum, second_colsum, head_colsum, first_rowtotal, second_rowtotal, head_rowtotal = stats
    first_col_new = decay * first_col + (1.0 - decay) * (first_colsum / enc_width)
    second_col_new = decay * second_col + (1.0 - decay) * (second_colsum / full_width)
    head_col_new = decay * head_col + (1.0 - decay) * (head_colsum / full_width)
    first_estimate = first_row_new[:, None] * first_col_new[None, :] / (first_rowtotal / enc_width)
    second_estimate = (
        second_row_new[:, None] * second_col_new[None, :] / (second_rowtotal / full_width)
    )
    head_estimate = (
        head_row_new[:, :, None]
        * head_col_new[:, None, :]
        / (head_rowtotal / full_width)[:, None, None]
    )
    first_update = first_grad * lax.rsqrt(first_estimate)
    second_update = second_grad * lax.rsqrt(second_estimate)
    head_update = head_grad * lax.rsqrt(head_estimate)
    adapter_sq_new = decay * adapter_sq + (1.0 - decay) * (adapter_grad * adapter_grad + EPS_SQUARE)
    adapter_update = adapter_grad * lax.rsqrt(adapter_sq_new)
    gain_sq_new = decay * gain_sq + (1.0 - decay) * (gain_grad * gain_grad + EPS_SQUARE)
    gain_update = gain_grad * lax.rsqrt(gain_sq_new)
    bias_sq_new = decay * bias_sq + (1.0 - decay) * (bias_grad * bias_grad + EPS_SQUARE)
    bias_update = bias_grad * lax.rsqrt(bias_sq_new)
    share_col = 1.0 / count_col
    share_dp = 1.0 / count_dp
    sums = lax.psum(
        (
            jnp.sum(first_update * first_update),
            jnp.sum(w_first * w_first),
            jnp.sum(second_update * second_update),
            jnp.sum(w_second * w_second),
            jnp.sum(head_update * head_update) * share_col,
            jnp.sum(w_head * w_head) * share_col,
            jnp.sum(adapter_update * adapter_update, axis=(1, 2)) * share_dp,
            jnp.sum(adapters * adapters, axis=(1, 2)) * share_dp,
        ),
        ("dp", "col"),
    )
    first_new = finish(w_first, first_update, sums[0], sums[1], enc_width * full_width)
    second_new = finish(w_second, second_update, sums[2], sums[3], full_width * full_width)
    head_new = finish(w_head, head_update, sums[4], sums[5], members * full_width * CLASSES)
    adapter_new = finish(
        adapters,
        adapter_update,
        sums[6].reshape(5, 1, 1),
        sums[7].reshape(5, 1, 1),
        members * full_width,
    )
    gain_new = finish(
        gains,
        gain_update,
        jnp.sum(gain_update * gain_update),
        jnp.sum(gains * gains),
        members * enc_width,
    )
    bias_new = finish(
        head_bias,
        bias_update,
        jnp.sum(bias_update * bias_update),
        jnp.sum(head_bias * head_bias),
        members * CLASSES,
    )
    residual_rms = jnp.sqrt(residual_sq / (row_total * members * full_width))
    branch_rms = jnp.sqrt(branch_sq / (row_total * members * full_width))
    return (
        first_grad,
        first_row_new,
        first_col_new,
        first_new,
        second_grad,
        second_row_new,
        second_col_new,
        second_new,
        head_grad,
        head_row_new,
        head_col_new,
        head_new,
        adapter_grad,
        adapter_sq_new,
        adapter_new,
        gain_grad,
        gain_sq_new,
        gain_new,
        bias_grad,
        bias_sq_new,
        bias_new,
        loss_sum,
        row_total,
        residual_rms,
        branch_rms,
    )


def local(*args):
    if lax.axis_size("dp") == 8 and lax.axis_size("col") == 4:
        return local_blocks(*args)
    return local_any(*args)


def solution(mesh):
    placed = (
        P("dp", None),
        P("dp", None),
        P("dp"),
        P("dp"),
        P("dp", "col"),
        P("dp", "col"),
        P(None, "dp", None),
        P(None, None, "col"),
        P(),
        P(),
        P("dp"),
        P("col"),
        P("dp"),
        P("col"),
        P(None, "dp"),
        P(),
        P(None, None, "col"),
        P(),
        P(),
    )
    return jax.shard_map(
        local,
        mesh=mesh,
        in_specs=placed,
        out_specs=(
            P("dp", "col"),
            P("dp"),
            P("col"),
            P("dp", "col"),
            P("dp", "col"),
            P("dp"),
            P("col"),
            P("dp", "col"),
            P(None, "dp", None),
            P(None, "dp"),
            P(),
            P(None, "dp", None),
            P(None, None, "col"),
            P(None, None, "col"),
            P(None, None, "col"),
            P(),
            P(),
            P(),
            P(),
            P(),
            P(),
            P(),
            P(),
            P(),
            P(),
        ),
        check_vma=False,
    )
```

time: 1100 us -> 93 us (0.08)
  waiting for transfers between devices: 673 us -> 0 us
  blocking collectives: 206 us -> 0 us
  matrix products: 103 us -> 0 us
  Pallas kernels: 0 us -> 91.6 us
  other arithmetic: 47.4 us -> 0 us
  local copies, waits for them, and re-layouts: 35 us -> 0.07 us
  between operations: 29.7 us -> 1.1 us
    reduce_scatter x3 -> x0, waiting for transfers between devices: 310 us -> none  [the longest x1 234 us: local(): lax.psum_scatter(partial_in, 'col', scatter_dimension=2, tiled=True)]
    psum x2 -> x0, waiting for transfers between devices: 180 us -> none  [the longest x1 110 us: local(): lax.psum((gain_part, residual_part, branch_part), ('dp', 'col'))]
    all_gather x2 -> x0, waiting for transfers between devices: 119 us -> none  [the longest x1 78.1 us: local(): second_all = lax.all_gather(second_in, 'col', axis=2, tiled=True)]
    all_gather x3 -> x0, blocking collectives: 104 us -> none  [the longest x1 41.3 us: local(): lax.all_gather(w_head.astype(jnp.bfloat16), 'dp', axis=1, tiled=True)]
    dot_general x9 -> x0, matrix products: 103 us -> none  [the longest x2 28.5 us: shared_product(): jnp.dot(left.reshape(-1, shape_left[-1]), right, preferred_element_type=j...]
    psum x4 -> x0, blocking collectives: 102 us -> none  [the longest x1 37.4 us: local(): lax.psum((jnp.sum(first_update * first_update), jnp.sum(w_first * w_first...]
    pallas_call x0 -> x4, Pallas kernels: none -> 91.6 us  [the longest x1 35.9 us: call_reduce(): pl.pallas_call(functools.partial(reduce_kernel, enc_w, width, members), o...]
    unnamed x9 -> x0, waiting for transfers between devices: 64.4 us -> none
  transfers between devices with their start and end apart: 8 -> 0, of which waited for: 8 -> 0; matrix products, arithmetic and copies ran while one was open for 6% -> 0% of each run, Pallas kernels for 0% -> 0%
where the time goes in v1:
time: 93 us; the launch traced here: 92.8 us
  Pallas kernels  91.6 us (98%)
  between operations  1.1 us (1%)
    pallas_call x1, Pallas kernels, call_reduce(): pl.pallas_call(functools.partial(reduce_kernel, enc_w, width, members), o...  35.9 us
    pallas_call x1, Pallas kernels, call_compute(): pl.pallas_call(functools.partial(compute_kernel, members), out_shape=(jax...  32.2 us
    pallas_call x1, Pallas kernels, call_gather(): pl.pallas_call(gather_kernel, out_shape=(jax.ShapeDtypeStruct((4, 2, 2, 2...  19.6 us
    pallas_call x1, Pallas kernels, call_store(): pl.pallas_call(functools.partial(store_kernel, count), out_shape=tuple((j...  3.83 us

profile of v1, /device:TPU:0, one launch (start us, length us, event | category | flops | bytes accessed | tf_op | source)
XLA Modules:
  0.0 92.8 jit_solution(6804368385142361085)
XLA Ops:
  0.7 0.0 copy-start.1
  0.7 0.0 copy-start.2
  0.7 0.0 copy-start.4
  0.7 0.0 copy-start.3
  0.7 0.0 copy-start.10
  0.7 0.0 copy-start.5
  0.7 0.0 copy-start.6
  0.7 0.0 copy-start.9
  0.8 0.0 copy-start.8
  0.8 0.0 copy-start.14
  0.8 0.0 copy-start.13
  0.8 0.0 copy-start.12
  0.8 0.0 copy-start.11
  0.8 0.0 copy-start.7
  0.8 0.0 copy-start
  0.8 19.6 %shard_map.378 = (bf16[4,2,2,2,160,128]{5,4,3,2,1,0:T(8,128)(2,1)S(1)}, bf16[4,2,64,128]{3,2,1,0:T(8,128)(2,1)S(1)}, f32[4,5,8,128]{3,2,1,0:T(8,128)S(1)}, bf16[512,128]{1,0:T(8,128)(2,1)S(1)}, f32[8,128]{1,0:T(8,128)S(1)}) custom-call(s32[16,512]{1,0:T(8,128)} %bitcast.36, f32[16,512]{1,0:T(8,128)} %bitcast.37, s32[1,512]{1,0:T(1,128)} %bitcast.38, ...), custom_call_target="tpu_custom_call" | custom-call | tf_op jit(solution)/shard_map/pallas_call | solution.py:195
  20.4 32.2 %shard_map.379 = (bf16[4,2,2,2,160,128]{5,4,3,2,1,0:T(8,128)(2,1)S(1)}, bf16[4,2,64,128]{3,2,1,0:T(8,128)(2,1)S(1)}, f32[8,40,128]{2,1,0:T(8,128)S(1)}) custom-call(bf16[4,2,2,2,160,128]{5,4,3,2,1,0:T(8,128)(2,1)S(1)} %get-tuple-element.83.buf, bf16[4,2,64,128]{3,2,1,0:T(8,128)(2,1)S(1)} %get-tuple-element.84.hbuf, ...), custom_call_target="tpu_custom_call" | custom-call | tf_op jit(solution)/shard_map/pallas_call | solution.py:399
  52.7 0.0 copy-done.1
  52.7 0.0 copy-done.2
  52.7 0.0 copy-done.4
  52.7 0.0 copy-done.3
  52.7 0.0 copy-done.10
  52.7 0.0 copy-done.5
  52.7 0.0 copy-done.6
  52.8 0.0 copy-done.9
  52.8 0.0 copy-done.8
  52.8 0.0 copy-done.14
  52.8 0.0 copy-done.13
  52.8 0.0 copy-done.12
  52.8 0.0 copy-done.11
  52.8 0.0 copy-done.7
  52.8 0.0 copy-done
  52.8 35.9 %shard_map.380 = (f32[96,128]{1,0:T(8,128)S(1)}, f32[1,96]{1,0:T(1,128)S(1)}, f32[1,128]{1,0:T(1,128)S(1)}, f32[96,128]{1,0:T(8,128)S(1)}, f32[64,128]{1,0:T(8,1...) custom-call(bf16[4,2,2,2,160,128]{5,4,3,2,1,0:T(8,128)(2,1)S(1)} %ge, ...), custom_call_target="tpu_custom_call" | custom-call | tf_op jit(solution)/shard_map/pallas_call | solution.py:674
  88.8 3.8 %shard_map.381 = (f32[96,128]{1,0:T(8,128)}, f32[1,96]{1,0:T(1,128)}, f32[1,128]{1,0:T(1,128)}, f32[96,128]{1,0:T(8,128)}, f32[64,128]{1,0:T(8,128)}, /*index=5*...) custom-call(f32[96,128]{1,0:T(8,128)S(1)} %get-tuple-element.91.refs, ...), custom_call_target="tpu_custom_call" | custom-call | tf_op jit(solution)/shard_map/pallas_call | solution.py:722
Async XLA Ops:
  0.7 52.0 %copy-start.1 = (f32[32,768]{1,0:T(8,128)S(1)}, f32[32,768]{1,0:T(8,128)}, u32[]{:S(2)}) copy-start(f32[32,768]{1,0:T(8,128)} %gains.1) | copy-start | bytes 294916
  0.7 52.0 %copy-start.2 = (f32[5,32,128]{2,1,0:T(8,128)S(1)}, f32[5,32,128]{2,1,0:T(8,128)}, u32[]{:S(2)}) copy-start(f32[5,32,128]{2,1,0:T(8,128)} %adapters.1) | copy-start | bytes 245764
  0.7 52.0 %copy-start.4 = (f32[64,128]{1,0:T(8,128)S(1)}, f32[64,128]{1,0:T(8,128)}, u32[]{:S(2)}) copy-start(f32[64,128]{1,0:T(8,128)} %w_second.3) | copy-start | bytes 98308
  0.7 52.0 %copy-start.3 = (f32[96,128]{1,0:T(8,128)S(1)}, f32[96,128]{1,0:T(8,128)}, u32[]{:S(2)}) copy-start(f32[96,128]{1,0:T(8,128)} %w_first.3) | copy-start | bytes 147460
  0.7 52.0 %copy-start.10 = (f32[32,16]{0,1:T(8,128)S(1)}, f32[32,16]{0,1:T(8,128)}, u32[]{:S(2)}) copy-start(f32[32,16]{0,1:T(8,128)} %param.37) | copy-start | bytes 6148
  0.7 52.0 %copy-start.5 = (f32[32,768]{1,0:T(8,128)S(1)}, f32[32,768]{1,0:T(8,128)}, u32[]{:S(2)}) copy-start(f32[32,768]{1,0:T(8,128)} %gain_sq.1) | copy-start | bytes 294916
  0.7 52.0 %copy-start.6 = (f32[5,32,128]{2,1,0:T(8,128)S(1)}, f32[5,32,128]{2,1,0:T(8,128)}, u32[]{:S(2)}) copy-start(f32[5,32,128]{2,1,0:T(8,128)} %adapter_sq.1) | copy-start | bytes 245764
  0.7 52.0 %copy-start.9 = (f32[32,16]{0,1:T(8,128)S(1)}, f32[32,16]{0,1:T(8,128)}, u32[]{:S(2)}) copy-start(f32[32,16]{0,1:T(8,128)} %param.34) | copy-start | bytes 6148
  0.8 52.0 %copy-start.8 = (f32[32,64]{1,0:T(8,128)S(1)}, f32[32,64]{1,0:T(8,128)}, u32[]{:S(2)}) copy-start(f32[32,64]{1,0:T(8,128)} %head_row.1) | copy-start | bytes 24580
  0.8 52.0 %copy-start.14 = (f32[128]{0:T(128)S(1)}, f32[128]{0:T(128)}, u32[]{:S(2)}) copy-start(f32[128]{0:T(128)} %param.32) | copy-start | bytes 1540
  0.8 52.0 %copy-start.13 = (f32[64]{0:T(128)S(1)}, f32[64]{0:T(128)}, u32[]{:S(2)}) copy-start(f32[64]{0:T(128)} %param.31) | copy-start | bytes 772
  0.8 52.0 %copy-start.12 = (f32[128]{0:T(128)S(1)}, f32[128]{0:T(128)}, u32[]{:S(2)}) copy-start(f32[128]{0:T(128)} %param.30) | copy-start | bytes 1540
  0.8 52.0 %copy-start.11 = (f32[96]{0:T(128)S(1)}, f32[96]{0:T(128)}, u32[]{:S(2)}) copy-start(f32[96]{0:T(128)} %param.29) | copy-start | bytes 1156
  0.8 52.0 %copy-start.7 = (f32[32,16]{0,1:T(8,128)S(1)}, f32[32,16]{0,1:T(8,128)}, u32[]{:S(2)}) copy-start(f32[32,16]{0,1:T(8,128)} %param.28) | copy-start | bytes 6148
  0.8 52.0 %copy-start = (f32[32,64,16]{1,2,0:T(8,128)S(1)}, f32[32,64,16]{1,2,0:T(8,128)}, u32[]{:S(2)}) copy-start(f32[32,64,16]{1,2,0:T(8,128)} %param.25) | copy-start | bytes 393220

commit v2 on v1

--- a/solution.py
+++ b/solution.py
@@ -11,7 +11,9 @@
 CLIP_LIMIT = 1.0
 RELATIVE_RATE = 0.4
 RATE_FLOOR = 0.001
-R = 32
+R = 64
+GROUPS = 2
+ORDER = (0, 1, 0, 1, 0, 1, 0, 1, 0, 1, 0, 1, 0, 1, 0, 1, 0, 1, 0, 1, 0, 1)
 f32, bf16 = jnp.float32, jnp.bfloat16
 
 def dot(a, b):
@@ -86,7 +88,7 @@
 
 
 def gather_kernel(bin_index, bin_fraction, row_mask, targets, w_first, w_second, w_head, adapters_far,
-                  buf, hbuf, adbuf, comp, info, table, recv,
+                  buf, hbuf, adbuf, enc, onehots, info, table, recv,
                   w_first_v, w_second_v, w_head_v, adapters, bin_index_v, bin_fraction_v, row_mask_v, targets_v,
                   load_sem, send_sem, recv_sem):
     z, y, x, core = place()
@@ -168,7 +170,18 @@
     pos = dot(mask_row.astype(bf16), (i_row < i_col).astype(bf16))
     spot = jnp.where(mask_row > 0.5, pos, -1.0)[0:1]
     perm = (i_row.astype(f32) == spot).astype(bf16)
-    comp[...] = dot(perm, got).astype(bf16)
+    enc_w, hw = enc.shape[1], onehots.shape[1]
+    kk = lax.broadcasted_iota(jnp.int32, (128, enc_w), 1)
+    ll = lax.broadcasted_iota(jnp.int32, (128, enc_w), 0)
+    ff = ll & (FEATS - 1)
+    spread = ((ll < 48) & (kk >= ff * BINS) & (kk < (ff + 1) * BINS)).astype(bf16)
+    lev = (lax.broadcasted_iota(jnp.int32, (1, enc_w), 1) % BINS).astype(f32)
+    l2 = lax.broadcasted_iota(jnp.int32, (128, hw), 0)
+    c2 = lax.broadcasted_iota(jnp.int32, (128, hw), 1)
+    oh_spread = (l2 == 48 + (c2 & (CLASSES - 1))).astype(bf16)
+    comp = dot(perm, got).astype(bf16)
+    enc[...] = jnp.clip(dot(comp, spread) - lev, 0.0, 1.0).astype(bf16)
+    onehots[...] = dot(comp, oh_spread).astype(bf16)
     lane = lax.broadcasted_iota(jnp.int32, (1, 128), 1)
     per_row = jnp.where(lane == 65, 16.0, jnp.where(lane == 66, 1.0, 0.0))
     total = jnp.sum(jnp.sum(got.astype(f32), axis=0, keepdims=True) * per_row, axis=1, keepdims=True) / slot
@@ -198,10 +211,11 @@
             jax.ShapeDtypeStruct((4, 2, 2, 2, both, 128), bf16),
             jax.ShapeDtypeStruct((4, 2, w_head.shape[2], 128), bf16),
             jax.ShapeDtypeStruct((4, 5, mem, 128), f32),
-            jax.ShapeDtypeStruct((rows, 128), bf16),
+            jax.ShapeDtypeStruct((rows, FEATS * BINS), bf16),
+            jax.ShapeDtypeStruct((rows, mem * CLASSES), bf16),
             jax.ShapeDtypeStruct((8, 128), f32),
         ),
-        in_specs=[FAR] * 8, out_specs=(VM,) * 5,
+        in_specs=[FAR] * 8, out_specs=(VM,) * 6,
         scratch_shapes=[pltpu.VMEM((rows, 128), bf16), pltpu.VMEM((rows, 128), bf16),
                         pltpu.VMEM(w_first.shape, f32), pltpu.VMEM(w_second.shape, f32),
                         pltpu.VMEM(w_head.shape, f32), pltpu.VMEM(adapters.shape, f32),
@@ -224,11 +238,15 @@
     return x
 
 
-def compute_kernel(members, buf, hbuf, adbuf, comp, info, gains_far, bias_far,
-                   gbuf, hb, small,
-                   w1, w2, w2t, head, headt, adapters, gains, enc_all, fog_all,
-                   first_acc, second_acc, head_acc, adapt, gain_acc, sums, gains_all, bias_all, load_sem):
-    rows_all = comp.shape[0]
+def fold8(v):
+    return sum(v[8 * i:8 * i + 8] for i in range(v.shape[0] // 8))
+
+
+def compute_kernel(members, buf, hbuf, adbuf, enc_all, onehots, info, gains_far, bias_far,
+                   w1, fog_all, sbuf, hb, small,
+                   w2, w2t, head, headt, adapters, gains, low_gains,
+                   second_acc, head_acc, adapt, sums, halves, gains_all, bias_all, load_sem):
+    rows_all = enc_all.shape[0]
     enc_w, width = w1.shape
     mem = adbuf.shape[2]
     hw = mem * CLASSES
@@ -246,12 +264,15 @@
         head[rs * d:rs * (d + 1), :] = hbuf[d // 2, d % 2]
     for c in range(4):
         adapters[:, :, 128 * c:128 * c + 128] = adbuf[c]
+    for j in (0, 1, 3, 4):
+        halves[j] = 0.5 * adapters[j]
     w2t[...] = w2[...].T
     headt[...] = head[...].T
     for load in loads:
         load.wait()
     own = pl.ds(pl.multiple_of(me_c * mem, mem), mem)
     gains[...] = gains_all[own, :]
+    low_gains[...] = gains[...].astype(bf16)
     owner = lax.broadcasted_iota(jnp.int32, (1, hw), 1) // CLASSES
     fold = (lax.broadcasted_iota(jnp.int32, (CLASSES, hw), 1) % CLASSES
             == lax.broadcasted_iota(jnp.int32, (CLASSES, hw), 0)).astype(f32)
@@ -262,136 +283,149 @@
     loss_scale = 1.0 / (members * info[1:2, :])
     tiles = (n_rows + (R - 1)) // R
     fog_all[...] = jnp.zeros_like(fog_all)
-    enc_all[...] = jnp.zeros_like(enc_all)
     second_acc[...] = jnp.zeros_like(second_acc)
     head_acc[...] = jnp.zeros_like(head_acc)
     adapt[...] = jnp.zeros_like(adapt)
     sums[...] = jnp.zeros_like(sums)
 
-    kk = lax.broadcasted_iota(jnp.int32, (128, enc_w), 1)
-    ll = lax.broadcasted_iota(jnp.int32, (128, enc_w), 0)
-    ff = ll & (FEATS - 1)
-    spread = ((ll < 48) & (kk >= ff * BINS) & (kk < (ff + 1) * BINS)).astype(bf16)
-    lev = (lax.broadcasted_iota(jnp.int32, (1, enc_w), 1) % BINS).astype(f32)
-    l2 = lax.broadcasted_iota(jnp.int32, (128, 2 * hw), 0)
-    c2 = lax.broadcasted_iota(jnp.int32, (128, 2 * hw), 1)
-    oh_spread = (l2 == jnp.where(c2 < hw, 48 + (c2 & (CLASSES - 1)), 64)).astype(bf16)
     s_i = lax.broadcasted_iota(jnp.int32, (hw, hw), 0) // CLASSES
     s_j = lax.broadcasted_iota(jnp.int32, (hw, hw), 1) // CLASSES
     seg = (s_i == s_j).astype(bf16)
 
-    def tile(t, carry):
-        rows = pl.ds(pl.multiple_of(t * R, R), R)
-        T = comp[rows, :]
-        enc = jnp.clip(dot(T, spread) - lev, 0.0, 1.0)
-        enc_all[rows, :] = enc.astype(bf16)
-        fin = jnp.concatenate([(enc * gains[m:m + 1, :]).astype(bf16) for m in range(mem)], axis=0)
+    def group(rows, pad_rows, oh, mk, enc, ms, out):
+        count = len(ms)
+        fin = jnp.concatenate([enc * low_gains[m:m + 1, :] for m in ms], axis=0)
         fo = dot(fin, w1[...])
+        yield
         hs, us, sos, sins = [], [], [], []
-        res = jnp.zeros((R, width), f32)
-        for m in range(mem):
-            h = fo[m * R:(m + 1) * R] * (0.5 * adapters[0, m:m + 1, :]) + 0.5 * adapters[1, m:m + 1, :]
+        res = jnp.zeros((8, width), f32)
+        res_pad = jnp.zeros((1, width), f32)
+        for i, m in enumerate(ms):
+            h = fo[i * R:(i + 1) * R] * halves[0, m:m + 1, :] + halves[1, m:m + 1, :]
             u = 1.0 + jnp.tanh(h)
             so = h * u
-            res += so * so
+            sq = so * so
+            res += fold8(sq)
+            res_pad += sq[R - 1:R]
             hs.append(h)
             us.append(u)
             sos.append(so)
             sins.append((so * adapters[2, m:m + 1, :]).astype(bf16))
+        sums[2] += res
+        sums[4, 0:1] -= pad_rows * res_pad
         sin = jnp.concatenate(sins, axis=0)
+        yield
         s2 = dot(sin, w2[...])
+        yield
         h2s, u2s, brs, sts = [], [], [], []
-        bres = jnp.zeros((R, width), f32)
-        for m in range(mem):
-            h = s2[m * R:(m + 1) * R] * (0.5 * adapters[3, m:m + 1, :]) + 0.5 * adapters[4, m:m + 1, :]
+        bres = jnp.zeros((8, width), f32)
+        bres_pad = jnp.zeros((1, width), f32)
+        for i, m in enumerate(ms):
+            h = s2[i * R:(i + 1) * R] * halves[3, m:m + 1, :] + halves[4, m:m + 1, :]
             u = 1.0 + jnp.tanh(h)
             br = h * u
-            bres += br * br
+            sq = br * br
+            bres += fold8(sq)
+            bres_pad += sq[R - 1:R]
             h2s.append(h)
             u2s.append(u)
             brs.append(br)
-            sts.append((sos[m] + br).astype(bf16))
+            sts.append((sos[i] + br).astype(bf16))
+        sums[3] += bres
+        sums[4, 1:2] -= pad_rows * bres_pad
         st = jnp.concatenate(sts, axis=0)
+        yield
         lo = dot(st, head[...])
+        yield
         logits = bias
-        for m in range(mem):
-            logits = logits + jnp.where(owner == m, lo[m * R:(m + 1) * R], 0.0)
+        for i, m in enumerate(ms):
+            logits = logits + jnp.where(owner == m, lo[i * R:(i + 1) * R], 0.0)
         top = seg_max(logits)
         ex = jnp.exp(logits - top)
         exh = ex.astype(bf16)
         exl = (ex - exh.astype(f32)).astype(bf16)
-        tot = dot(exh, seg) + dot(exl, seg)
-        ohm = dot(T, oh_spread)
-        oh, mk = ohm[:, :hw], ohm[:, hw:]
+        both = dot(jnp.concatenate([exh, exl], axis=0), seg)
+        tot = both[:R] + both[R:]
         loss_c = (top + jnp.log(tot) - logits) * oh
         lgf = ((ex / tot * mk - oh) * loss_scale).astype(bf16).astype(f32)
-        lgm = jnp.concatenate([jnp.where(owner == m, lgf, 0.0).astype(bf16) for m in range(mem)], axis=0)
+        lgm = jnp.concatenate([jnp.where(owner == m, lgf, 0.0).astype(bf16) for m in ms], axis=0)
+        out.append((loss_c, lgf))
+        yield
+        sg = dot(lgm, headt[...])
+        yield
+        ogs = []
+        for i, m in enumerate(ms):
+            pg = sg[i * R:(i + 1) * R] * (u2s[i] + brs[i] * (2.0 - u2s[i]))
+            adapt[3, m] += fold8(pg * h2s[i])
+            adapt[4, m] += fold8(pg)
+            ogs.append((pg * halves[3, m:m + 1, :]).astype(bf16))
+        og = jnp.concatenate(ogs, axis=0)
+        yield
+        ig = dot(og, w2t[...])
+        yield
         head_acc[...] += t_dot(lgm, st)
-        sg = dot(lgm, headt[...])
-        ogs = []
-        for m in range(mem):
-            pg = sg[m * R:(m + 1) * R] * (u2s[m] + brs[m] * (2.0 - u2s[m]))
-            adapt[3, m:m + 1, :] += jnp.sum(pg * h2s[m], axis=0, keepdims=True)
-            adapt[4, m:m + 1, :] += jnp.sum(pg, axis=0, keepdims=True)
-            ogs.append((pg * (0.5 * adapters[3, m:m + 1, :])).astype(bf16))
-        og = jnp.concatenate(ogs, axis=0)
         second_acc[...] += t_dot(sin, og)
-        ig = dot(og, w2t[...])
-        for m in range(mem):
-            igm = ig[m * R:(m + 1) * R]
-            adapt[2, m:m + 1, :] += jnp.sum(igm * sos[m], axis=0, keepdims=True)
-            one = sg[m * R:(m + 1) * R] + igm * adapters[2, m:m + 1, :]
-            low = one * (us[m] + sos[m] * (2.0 - us[m]))
-            adapt[0, m:m + 1, :] += jnp.sum(low * hs[m], axis=0, keepdims=True)
-            adapt[1, m:m + 1, :] += jnp.sum(low, axis=0, keepdims=True)
-            fog_all[m, rows, :] = (low * (0.5 * adapters[0, m:m + 1, :])).astype(bf16)
-        spare = jnp.maximum((t + 1) * R - n_rows, 0).astype(f32)
-        sums[0:1, :hw] += jnp.sum(lgf, axis=0, keepdims=True)
-        sums[1:2, :hw] += jnp.sum(loss_c, axis=0, keepdims=True)
-        sums[2:3, :] += jnp.sum(res, axis=0, keepdims=True) - spare * res[R - 1:R]
-        sums[3:4, :] += jnp.sum(bres, axis=0, keepdims=True) - spare * bres[R - 1:R]
+        yield
+        for i, m in enumerate(ms):
+            igm = ig[i * R:(i + 1) * R]
+            adapt[2, m] += fold8(igm * sos[i])
+            one = sg[i * R:(i + 1) * R] + igm * adapters[2, m:m + 1, :]
+            low = one * (us[i] + sos[i] * (2.0 - us[i]))
+            adapt[0, m] += fold8(low * hs[i])
+            adapt[1, m] += fold8(low)
+            fog_all[m, rows, :] = (low * halves[0, m:m + 1, :]).astype(bf16)
+        yield
+
+    def tile(t, carry):
+        rows = pl.ds(pl.multiple_of(t * R, R), R)
+        enc = enc_all[rows, :]
+        oh = onehots[rows, :].astype(f32)
+        mk = (lax.broadcasted_iota(jnp.int32, (R, hw), 0) + t * R < n_rows).astype(f32)
+        pad_rows = jnp.maximum((t + 1) * R - n_rows, 0).astype(f32)
+        out = []
+        per = mem // GROUPS
+        runs = [group(rows, pad_rows, oh, mk, enc, tuple(range(g * per, (g + 1) * per)), out) for g in range(GROUPS)]
+        for g in ORDER:
+            next(runs[g])
+        lane = lax.broadcasted_iota(jnp.int32, (1, hw), 1)
+        loss_c, lgf = out[0]
+        for g in range(1, GROUPS):
+            late = lane >= g * per * CLASSES
+            loss_c = jnp.where(late, out[g][0], loss_c)
+            lgf = jnp.where(late, out[g][1], lgf)
+        sums[0, :, :hw] += fold8(lgf)
+        sums[1, :, :hw] += fold8(loss_c)
         return carry
 
     lax.fori_loop(0, tiles, tile, 0)
-    enct = enc_all[...].T
-    gcol = jnp.concatenate([gains[...], jnp.zeros((128 - mem, enc_w), f32)], axis=0).T
-    for m in range(mem):
-        g = dot(enct, fog_all[m])
-        gain_acc[:, m:m + 1] = jnp.sum(g * w1[...].astype(f32), axis=1, keepdims=True)
-        if m == 0:
-            first_acc[...] = g * gcol[:, m:m + 1]
-        else:
-            first_acc[...] += g * gcol[:, m:m + 1]
-    gain_rows = gain_acc[...].T
     for d in range(8):
         for c in range(4):
             lanes = slice(128 * c, 128 * c + 128)
-            gbuf[d // 2, d % 2, c // 2, c % 2, 0:rf, :] = first_acc[rf * d:rf * (d + 1), lanes].astype(bf16)
-            gbuf[d // 2, d % 2, c // 2, c % 2, rf:rf + rs, :] = second_acc[rs * d:rs * (d + 1), lanes].astype(bf16)
+            sbuf[d // 2, d % 2, c // 2, c % 2] = second_acc[rs * d:rs * (d + 1), lanes].astype(bf16)
     head_t = head_acc[...].T
     for d in range(8):
         hb[d // 2, d % 2] = head_t[rs * d:rs * (d + 1), :].astype(bf16)
     small[...] = jnp.zeros_like(small)
-    a0, a1, a2 = adapt[0], adapt[1], adapt[2]
-    a3, a4 = adapt[3], adapt[4]
+    a0, a1, a2, a3, a4 = (jnp.sum(adapt[j], axis=1) for j in range(5))
     fixed = ((a0 - 0.5 * adapters[1] * a1) / adapters[0], 0.5 * a1, a2,
              (a3 - 0.5 * adapters[4] * a4) / adapters[3], 0.5 * a4)
     for m in range(mem):
         for k in range(4):
             for j in range(5):
                 small[m, 8 * k + j:8 * k + j + 1, :] = fixed[j][m:m + 1, 128 * k:128 * k + 128]
-        for i in range(enc_w // 128):
-            small[m, 32 + i:33 + i, :] = gain_rows[m:m + 1, 128 * i:128 * i + 128]
     def four(row):
         return row[:, 0:128] + row[:, 128:256] + row[:, 256:384] + row[:, 384:512]
-    small[0, 39:40, :] = sums[1:2, 0:128]
-    small[1, 39:40, :] = four(sums[2:3, :])
-    small[2, 39:40, :] = four(sums[3:4, :])
-    small[3, 39:40, :] = sums[0:1, 0:128]
-
-
-def call_compute(members, buf, hbuf, adbuf, comp, info, gains, bias):
-    rows = comp.shape[0]
+    def rows_sum(v):
+        return jnp.sum(v, axis=0, keepdims=True)
+    extra = (rows_sum(sums[1, :, 0:128]), four(rows_sum(sums[2]) + sums[4, 0:1]),
+             four(rows_sum(sums[3]) + sums[4, 1:2]), rows_sum(sums[0, :, 0:128]))
+    for m, row in enumerate(extra):
+        for k in range(4):
+            small[m, 8 * k + 5:8 * k + 6, :] = row
+
+
+def call_compute(members, buf, hbuf, adbuf, enc, onehots, info, gains, bias):
+    rows = enc.shape[0]
     enc_w = gains.shape[1]
     mem = adbuf.shape[2]
     width = adbuf.shape[0] * 128
@@ -399,27 +433,30 @@
     return pl.pallas_call(
         functools.partial(compute_kernel, members),
         out_shape=(
-            jax.ShapeDtypeStruct(buf.shape, bf16),
+            jax.ShapeDtypeStruct((enc_w, width), bf16),
+            jax.ShapeDtypeStruct((mem, rows, width), bf16),
+            jax.ShapeDtypeStruct((4, 2, 2, 2, width // 8, 128), bf16),
             jax.ShapeDtypeStruct(hbuf.shape, bf16),
-            jax.ShapeDtypeStruct((8, 40, 128), f32),
+            jax.ShapeDtypeStruct((8, 32, 128), f32),
         ),
-        in_specs=[VM] * 5 + [FAR] * 2, out_specs=(VM,) * 3,
+        in_specs=[VM] * 6 + [FAR] * 2, out_specs=(VM,) * 5,
         scratch_shapes=[
-            pltpu.VMEM((enc_w, width), bf16), pltpu.VMEM((width, width), bf16), pltpu.VMEM((width, width), bf16),
+            pltpu.VMEM((width, width), bf16), pltpu.VMEM((width, width), bf16),
             pltpu.VMEM((width, hw), bf16), pltpu.VMEM((hw, width), bf16),
             pltpu.VMEM((5, mem, width), f32), pltpu.VMEM((mem, enc_w), f32),
-            pltpu.VMEM((rows, enc_w), bf16), pltpu.VMEM((mem, rows, width), bf16),
-            pltpu.VMEM((enc_w, width), f32), pltpu.VMEM((width, width), f32), pltpu.VMEM((hw, width), f32),
-            pltpu.VMEM((5, mem, width), f32), pltpu.VMEM((enc_w, 128), f32), pltpu.VMEM((8, width), f32),
+            pltpu.VMEM((mem, enc_w), bf16),
+            pltpu.VMEM((width, width), f32), pltpu.VMEM((hw, width), f32),
+            pltpu.VMEM((5, mem, 8, width), f32), pltpu.VMEM((5, 8, width), f32), pltpu.VMEM((5, mem, width), f32),
             pltpu.VMEM(gains.shape, f32), pltpu.VMEM(bias.shape, f32), pltpu.SemaphoreType.DMA((2,)),
         ],
         compiler_params=pltpu.CompilerParams(vmem_limit_bytes=30 << 20),
-    )(buf, hbuf, adbuf, comp, info, far(gains), far(bias))
+    )(buf, hbuf, adbuf, enc, onehots, info, far(gains), far(bias))
 
 
 def reduce_kernel(enc_w, width, members,
-                  gbuf, hb, small, info, w_first, w_second, w_head, adapters, gains, head_bias,
-                  first_row, first_col, second_row, second_col, head_row, head_col, adapter_sq, gain_sq, bias_sq,
+                  enc, w1_all, fog, sbuf, hb, small, info,
+                  f_w_first, f_w_second, f_w_head, f_adapters, f_gains, f_head_bias,
+                  f_first_row, f_first_col, f_second_row, f_second_col, f_head_row, f_head_col, f_adapter_sq, f_gain_sq, f_bias_sq,
                   o_first_grad, o_first_row, o_first_col, o_first_new,
                   o_second_grad, o_second_row, o_second_col, o_second_new,
                   o_head_grad, o_head_row, o_head_col, o_head_new,
@@ -427,10 +464,33 @@
                   o_gain_grad, o_gain_sq, o_gain_new,
                   o_bias_grad, o_bias_sq, o_bias_new,
                   o_loss, o_rows, o_residual, o_branch,
-                  cbuf, sbuf, plane0, held0, zed0, zed1, held1, plane1, hy, hsum, hz, hcol,
-                  fr, gall, ca, cg, colmsg, colall, rowmsg, rowall, msg, msgall, send_sem, recv_sem):
+                  w1t, own_gains, first_acc, gain_acc, far_half, own_half, far_got, own_got, far_sum, far_x, own_sum, own_pair, first_y, first_pair, first_in,
+                  second_got, second_sum, second_x, second_own, second_y, second_pair, second_in,
+                  hy, hsum, hz, hcol, small_y, small_sum, small_z, gall, ca, gain_part, gain_in, gain_all, gain_cols,
+                  colmsg, colall, rowmsg, rowall, msg, msgall,
+                  w_first, w_second, w_head, adapters, gains, head_bias,
+                  first_row, first_col, second_row, second_col, head_row, head_col, adapter_sq, gain_sq, bias_sq,
+                  load_sem, send_sem, recv_sem):
     z, y, x, core = place()
-    me_c = 2 * x + core
+    me_c, me_d = 2 * x + core, 2 * z + y
+    loads = [pltpu.make_async_copy(src, dst, load_sem.at[i]) for i, (src, dst) in enumerate((
+        (f_gains, gains),
+        (f_w_first, w_first),
+        (f_w_second, w_second),
+        (f_w_head, w_head),
+        (f_adapters, adapters),
+        (f_head_bias, head_bias),
+        (f_first_row, first_row),
+        (f_first_col, first_col),
+        (f_second_row, second_row),
+        (f_second_col, second_col),
+        (f_head_row, head_row),
+        (f_head_col, head_col),
+        (f_adapter_sq, adapter_sq),
+        (f_gain_sq, gain_sq),
+        (f_bias_sq, bias_sq)))]
+    for load in loads:
+        load.start()
     rf, rs = w_first.shape[0], w_second.shape[0]
     mem = members // 4
     hw = mem * CLASSES
@@ -443,88 +503,117 @@
                     if kz or ky or kx or kc:
                         everyone.append(device(z_other(z, kz), other(y, ky), other(x, kx), other(core, kc)))
     barrier, count = greet(everyone)
+    send = Sender(send_sem, recv_sem)
+    mate = device(z, y, x, 1 - core)
+    beside = device(z, y, 1 - x, core)
+    dp_peers = [(z_other(z, kz), other(y, ky)) for kz, ky in DP_PEERS]
+
+    def received(copies):
+        for cp in copies:
+            cp.wait_recv()
+
+    def quarter(side, ms):
+        half = pl.ds(pl.multiple_of(256 * side, 256), 256)
+        parts = jnp.concatenate([fog[m, :, half].T for m in ms], axis=0)
+        g = dot(parts, enc[...])
+        for i, m in enumerate(ms):
+            gm = g[256 * i:256 * (i + 1)]
+            gain_acc[m] += fold8(gm * w1t[half, :].astype(f32))
+            scaled = gm * own_gains[m:m + 1, :]
+            if m == 0:
+                first_acc[...] = scaled
+            else:
+                first_acc[...] += scaled
+
+    def lay_out(half):
+        flipped = first_acc[...].astype(bf16).T
+        for d in range(8):
+            for c in range(2):
+                half[d // 2, d % 2, c] = flipped[rf * d:rf * (d + 1), 128 * c:128 * c + 128]
+
+    def to_z(ref, into, send=send):
+        return [send(ref(z_other(z, k)), into(k), device(z_other(z, k), y, x, core)) for k in (1, 2, 3)]
+
+    y_mate = device(z, 1 - y, x, core)
+    w1t[...] = w1_all[...].T
+    loads[0].wait()
+    own_gains[...] = gains[pl.ds(pl.multiple_of(me_c * mem, mem), mem), :]
+    gain_acc[...] = jnp.zeros_like(gain_acc)
+    early, late = range(mem // 2), range(mem // 2, mem)
+    quarter(1 - x, early)
+    quarter(1 - x, late)
+    lay_out(far_half)
     pl.semaphore_wait(barrier, count)
-    send = Sender(send_sem, recv_sem)
-    s0, s1 = pl.ds(0, SPLIT), pl.ds(SPLIT, rf + rs - SPLIT)
-    mate = device(z, y, x, 1 - core)
-    swap1 = send(gbuf.at[:, :, :, 1 - core, s1], cbuf.at[:, :, :, s1], mate)
-    swap0 = send(gbuf.at[:, :, :, 1 - core, s0], cbuf.at[:, :, :, s0], mate)
-    head1 = send(hb.at[:, 1 - y], hy, device(z, 1 - y, x, core))
-    deal = [send(small.at[2 * z_other(z, kz) + other(y, ky)], fr.at[i], device(z_other(z, kz), other(y, ky), x, core))
-            for i, (kz, ky) in enumerate(DP_PEERS)]
+    swap_far = send(far_half.at[:, :, 1 - core], far_got, mate)
+    swap_second = send(sbuf.at[:, :, :, 1 - core], second_got, mate)
+    small1 = send(small.at[:, 1 - y], small_y, y_mate)
+    head1 = send(hb.at[:, 1 - y], hy, y_mate)
+    quarter(x, early)
+    received([swap_far])
+    far_sum[...] = (far_half[:, :, core].astype(f32) + far_got[...].astype(f32)).astype(bf16)
+    across_far = send(far_sum, far_x, beside)
+    received([swap_second])
+    second_sum[...] = (sbuf[:, :, :, core].astype(f32) + second_got[...].astype(f32)).astype(bf16)
+    second2 = send(second_sum.at[:, 1 - y], second_y, y_mate)
+    quarter(x, late)
+    lay_out(own_half)
+    swap_own = send(own_half.at[:, :, 1 - core], own_got, mate)
+    gain_part[...] = jnp.zeros_like(gain_part)
+    for m in range(mem):
+        row = jnp.sum(gain_acc[m], axis=0, keepdims=True)
+        for i in range(enc_w // 128):
+            gain_part[m, i:i + 1, :] = row[:, 128 * i:128 * i + 128]
+    gain_deal = [send(gain_part.at[2 * pz + py], gain_in.at[i], device(pz, py, x, core)) for i, (pz, py) in enumerate(dp_peers)]
+    received([small1])
+    small_sum[...] = small[:, y] + small_y[...]
+    small2 = to_z(lambda pz: small_sum.at[pz], lambda k: small_z.at[k - 1])
+    received([head1])
+    hsum[...] = (hb[:, y].astype(f32) + hy[...].astype(f32)).astype(bf16)
+    head2 = to_z(lambda pz: hsum.at[pz], lambda k: hz.at[k - 1])
+    for load in loads[1:]:
+        load.wait()
     w1, w2 = w_first[...], w_second[...]
     wh = [w_head[mem * c:mem * (c + 1)].reshape(hw, rs).T for c in range(4)]
     own_w = (jnp.sum(w1 * w1), jnp.sum(w2 * w2), sum(jnp.sum(w * w) for w in wh))
     adapter_w = [jnp.sum(adapters[j] * adapters[j]) for j in range(5)]
-    swap1.wait_recv()
-    sbuf[:, :, :, s1, :] = (gbuf[:, :, :, core, s1, :].astype(f32) + cbuf[:, :, :, s1, :].astype(f32)).astype(bf16)
-    p1 = [send(sbuf.at[z_other(z, k), :, :, s1], zed1.at[k - 1], device(z_other(z, k), y, x, core)) for k in (1, 2, 3)]
-    swap0.wait_recv()
-    sbuf[:, :, :, s0, :] = (gbuf[:, :, :, core, s0, :].astype(f32) + cbuf[:, :, :, s0, :].astype(f32)).astype(bf16)
-    p0 = [send(sbuf.at[:, other(y, ky), other(x, kx), s0], plane0.at[i], device(z, other(y, ky), other(x, kx), core))
-          for i, (ky, kx) in enumerate(PLANE)]
-    head1.wait_recv()
-    hsum[...] = (hb[:, y].astype(f32) + hy[...].astype(f32)).astype(bf16)
-    head2 = [send(hsum.at[z_other(z, k)], hz.at[k - 1], device(z_other(z, k), y, x, core)) for k in (1, 2, 3)]
-    for cp in deal:
-        cp.wait_recv()
-    me_d = 2 * z + y
-    mine = small[me_d]
+    received([second2])
+    second_own[...] = (second_sum[:, y].astype(f32) + second_y[...].astype(f32)).astype(bf16)
+    second3 = send(second_own.at[:, 1 - x], second_x, beside)
+    received([swap_own])
+    own_sum[...] = own_half[:, :, core].astype(f32) + own_got[...].astype(f32)
+    received([across_far])
+    own_pair[...] = (own_sum[...] + far_x[...].astype(f32)).astype(bf16)
+    first2 = send(own_pair.at[:, 1 - y], first_y, y_mate)
+    received(gain_deal)
+    mine = gain_part[me_d]
     for i in range(7):
-        mine = mine + fr[i]
-    gall[me_d] = mine
-    spread_dp = [send(gall.at[me_d], gall.at[me_d], device(z_other(z, kz), other(y, ky), x, core)) for kz, ky in DP_PEERS]
-    for cp in p1:
-        cp.wait_recv()
-    part = sbuf[z, :, :, s1, :].astype(f32)
+        mine = mine + gain_in[i]
+    gain_all[me_d] = mine
+    gain_dp = [send(gain_all.at[me_d], gain_all.at[me_d], device(pz, py, x, core)) for pz, py in dp_peers]
+    received(small2)
+    gall[z, y] = ((small_sum[z] + small_z[0]) + small_z[1]) + small_z[2]
+    small3 = to_z(lambda pz: gall.at[z, y], lambda k: gall.at[z, y])
+    received(head2)
+    hcol[me_c] = (hsum[z].astype(f32) + hz[0].astype(f32)) + (hz[1].astype(f32) + hz[2].astype(f32))
+    head3 = [send(hcol.at[me_c], hcol.at[me_c], device(z, y, other(x, kx), other(core, kc))) for kx, kc in COL_PEERS]
+    received([second3])
+    second_pair[...] = (second_own[:, x].astype(f32) + second_x[...].astype(f32)).astype(bf16)
+    second4 = to_z(lambda pz: second_pair.at[pz], lambda k: second_in.at[k - 1])
+    received([first2])
+    first_pair[...] = (own_pair[:, y].astype(f32) + first_y[...].astype(f32)).astype(bf16)
+    first3 = to_z(lambda pz: first_pair.at[pz], lambda k: first_in.at[k - 1])
+    received(small3)
+    small4 = send(gall.at[:, y], gall.at[:, y], y_mate)
+    received(gain_dp)
+    gain_cols[me_c] = gain_all[...]
+    gain_spread = [send(gain_all, gain_cols.at[me_c], device(z, y, other(x, kx), other(core, kc))) for kx, kc in COL_PEERS]
+    received(second4)
+    second = second_pair[z].astype(f32)
     for i in range(3):
-        part = part + zed1[i].astype(f32)
-    held1[...] = part.astype(bf16)
-    q1 = [send(held1.at[other(y, ky), other(x, kx)], plane1.at[i], device(z, other(y, ky), other(x, kx), core))
-          for i, (ky, kx) in enumerate(PLANE)]
-    for cp in head2:
-        cp.wait_recv()
-    hown = hsum[z].astype(f32)
-    for i in range(3):
-        hown = hown + hz[i].astype(f32)
-    hcol[me_c] = hown
-    head3 = [send(hcol.at[me_c], hcol.at[me_c], device(z, y, other(x, kx), other(core, kc))) for kx, kc in COL_PEERS]
-    for cp in p0:
-        cp.wait_recv()
-    part = sbuf[:, y, x, s0, :].astype(f32)
-    for i in range(3):
-        part = part + plane0[i].astype(f32)
-    held0[...] = part.astype(bf16)
-    q0 = [send(held0.at[z_other(z, k)], zed0.at[k - 1], device(z_other(z, k), y, x, core)) for k in (1, 2, 3)]
-    for cp in spread_dp:
-        cp.wait_recv()
-    own8 = pl.ds(pl.multiple_of(8 * me_c, 8), 8)
-    ca[me_c] = gall[:, own8, :]
-    cg[me_c] = gall[:, 32:40, :]
-    spread_col = []
-    for kx, kc in COL_PEERS:
-        px, pc = other(x, kx), other(core, kc)
-        theirs = pl.ds(pl.multiple_of(8 * (2 * px + pc), 8), 8)
-        spread_col.append(send(gall.at[:, theirs], ca.at[me_c], device(z, y, px, pc)))
-        spread_col.append(send(gall.at[:, 32:40], cg.at[me_c], device(z, y, px, pc)))
-    g0 = held0[z].astype(f32)
-    g1 = held1[y, x].astype(f32)
-    for cp in q1:
-        cp.wait_recv()
-    for i in range(3):
-        g1 = g1 + plane1[i].astype(f32)
-    for cp in q0:
-        cp.wait_recv()
-    for i in range(3):
-        g0 = g0 + zed0[i].astype(f32)
-    first = g0[0:rf]
-    second = jnp.concatenate([g0[rf:SPLIT], g1], axis=0)
-    o_first_grad[...] = first
+        second = second + second_in[i].astype(f32)
+    second_sq = second * second + EPS_SQUARE
     o_second_grad[...] = second
-    first_sq = first * first + EPS_SQUARE
-    second_sq = second * second + EPS_SQUARE
-    for cp in head3:
-        cp.wait_recv()
+    received(head3)
     hg = [hcol[c] for c in range(4)]
     hsq = [g * g + EPS_SQUARE for g in hg]
     seg8 = (lax.broadcasted_iota(jnp.int32, (mem, hw), 1) // CLASSES
@@ -533,23 +622,36 @@
     hrow = [decay * head_row[mem * c:mem * (c + 1), :]
             + (1.0 - decay) / CLASSES * hdot(seg8, hsq[c], ((1,), (1,))) for c in range(4)]
     hrowx = [hdot(hrow[c], seg8, ((0,), (0,))) for c in range(4)]
+    def add_up(v):
+        return jnp.sum(v, axis=0, keepdims=True)
     for c in range(4):
         o_head_row[mem * c:mem * (c + 1), :] = hrow[c]
-    rowmsg[:, 0:rf] = hdot(ones8, first_sq, ((1,), (1,)))
-    rowmsg[:, 128:128 + rs] = hdot(ones8, second_sq, ((1,), (1,)))
-    rowall[me_c] = rowmsg[...]
-    def add_up(v):
-        return jnp.sum(v, axis=0, keepdims=True)
-    colmsg[0:1, :] = add_up(first_sq)
-    colmsg[1:2, :] = add_up(second_sq)
-    for c in range(4):
+        o_head_grad[mem * c:mem * (c + 1)] = hg[c].T.reshape(mem, CLASSES, rs)
         colmsg[2 + c:3 + c, :] = add_up(hsq[c])
         colmsg[8 + c:9 + c, :] = add_up(hrowx[c])
+    colmsg[1:2, :] = add_up(second_sq)
+    rowmsg[:, 128:128 + rs] = hdot(ones8, second_sq, ((1,), (1,)))
+    received([small4])
+    own8 = pl.ds(pl.multiple_of(8 * me_c, 8), 8)
+    ca[me_c] = gall[:, :, own8, :]
+    spread_col = []
+    for kx, kc in COL_PEERS:
+        px, pc = other(x, kx), other(core, kc)
+        theirs = pl.ds(pl.multiple_of(8 * (2 * px + pc), 8), 8)
+        spread_col.append(send(gall.at[:, :, theirs], ca.at[me_c], device(z, y, px, pc)))
+    received(first3)
+    first = first_pair[z].astype(f32)
+    for i in range(3):
+        first = first + first_in[i].astype(f32)
+    o_first_grad[...] = first
+    first_sq = first * first + EPS_SQUARE
+    rowmsg[:, 0:rf] = hdot(ones8, first_sq, ((1,), (1,)))
+    rowall[me_c] = rowmsg[...]
+    colmsg[0:1, :] = add_up(first_sq)
     colall[me_d] = colmsg[...]
     r1 = [send(colmsg, colall.at[me_d], device(z_other(z, kz), other(y, ky), x, core)) for kz, ky in DP_PEERS]
     r1 += [send(rowmsg, rowall.at[me_c], device(z, y, other(x, kx), other(core, kc))) for kx, kc in COL_PEERS]
-    for cp in spread_col:
-        cp.wait_recv()
+    received(spread_col)
     fold = (lax.broadcasted_iota(jnp.int32, (CLASSES, hw), 1) % CLASSES
             == lax.broadcasted_iota(jnp.int32, (CLASSES, hw), 0)).astype(f32)
     to8 = (lax.broadcasted_iota(jnp.int32, (8, members), 1) // mem
@@ -571,20 +673,12 @@
         return weight - step_size(weight_sq, entries) * (update / limit)
     adapter_up = []
     for j in range(5):
-        grad = jnp.concatenate([ca[c, :, j, :] for c in range(4)], axis=0)
+        grad = jnp.concatenate([ca[c, m // 2, m % 2, j:j + 1, :] for c in range(4) for m in range(mem)], axis=0)
         sq = decay * adapter_sq[j] + (1.0 - decay) * (grad * grad + EPS_SQUARE)
         o_adapter_grad[j] = grad
         o_adapter_sq[j] = sq
         adapter_up.append(grad * lax.rsqrt(sq))
-    for c in range(4):
-        for i in range(enc_w // 128):
-            o_gain_grad[mem * c:mem * (c + 1), 128 * i:128 * (i + 1)] = cg[c, :, i, :]
-    gain = o_gain_grad[...]
-    gain_state = decay * gain_sq[...] + (1.0 - decay) * (gain * gain + EPS_SQUARE)
-    o_gain_sq[...] = gain_state
-    gain_up = gain * lax.rsqrt(gain_state)
-    o_gain_new[...] = apply(gains[...], gain_up, total(gain_up * gain_up), total(gains[...] * gains[...]), members * enc_w)
-    bias_lanes = jnp.concatenate([cg[c, 3, 7:8, :] for c in range(4)] + [jnp.zeros((4, 128), f32)], axis=0)
+    bias_lanes = jnp.concatenate([ca[c, 1, 1, 5:6, :] for c in range(4)] + [jnp.zeros((4, 128), f32)], axis=0)
     bias = from_lanes(bias_lanes)
     bias_state = decay * bias_sq[...] + (1.0 - decay) * (bias * bias + EPS_SQUARE)
     o_bias_grad[...] = bias
@@ -593,10 +687,10 @@
     o_bias_new[...] = apply(head_bias[...], bias_up, total(bias_up * bias_up), total(head_bias[...] * head_bias[...]), members * CLASSES)
     rows_total = info[1:2, 0:1]
     o_rows[...] = rows_total
-    o_loss[...] = lane_sum(sum(cg[c, 0, 7:8, :] for c in range(4)))
+    o_loss[...] = lane_sum(sum(ca[c, 0, 0, 5:6, :] for c in range(4)))
     spread_over = rows_total * (members * width)
-    o_residual[...] = jnp.sqrt(lane_sum(sum(cg[c, 1, 7:8, :] for c in range(4))) / spread_over)
-    o_branch[...] = jnp.sqrt(lane_sum(sum(cg[c, 2, 7:8, :] for c in range(4))) / spread_over)
+    o_residual[...] = jnp.sqrt(lane_sum(sum(ca[c, 0, 1, 5:6, :] for c in range(4))) / spread_over)
+    o_branch[...] = jnp.sqrt(lane_sum(sum(ca[c, 1, 0, 5:6, :] for c in range(4))) / spread_over)
     hcol_old = to_lanes(head_col[...])
     for cp in r1:
         cp.wait_recv()
@@ -630,8 +724,17 @@
     r2 = []
     for target in everyone:
         r2.append(send(msg, msgall.at[z, y, x, core], target))
+    received(gain_spread)
     for c in range(4):
-        o_head_grad[mem * c:mem * (c + 1)] = hg[c].T.reshape(mem, CLASSES, rs)
+        for i in range(enc_w // 128):
+            o_gain_grad[mem * c:mem * (c + 1), 128 * i:128 * (i + 1)] = gain_cols[c, :, i, :]
+    gain = o_gain_grad[...]
+    gain_state = decay * gain_sq[...] + (1.0 - decay) * (gain * gain + EPS_SQUARE)
+    o_gain_sq[...] = gain_state
+    gain_up = gain * lax.rsqrt(gain_state)
+    o_gain_new[...] = apply(gains[...], gain_up, total(gain_up * gain_up), total(gains[...] * gains[...]), members * enc_w)
+    for cp in send.all[:-len(r2)]:
+        cp.wait_send()
     for cp in r2:
         cp.wait_recv()
     def over_dp(cx, cc):
@@ -653,17 +756,16 @@
     for c in range(4):
         new = apply(wh[c], head_up[c], item(s_dp, 6), item(s_dp, 7), members * width * CLASSES)
         o_head_new[mem * c:mem * (c + 1)] = new.T.reshape(mem, CLASSES, rs)
-    for cp in send.all:
+    for cp in r2:
         cp.wait_send()
 
 
-def call_reduce(gbuf, hb, small, info, w_first, w_second, w_head, adapters, gains, head_bias,
+def call_reduce(enc, w1_all, fog, sbuf, hb, small, info, w_first, w_second, w_head, adapters, gains, head_bias,
                 first_row, first_col, second_row, second_col, head_row, head_col, adapter_sq, gain_sq, bias_sq):
     members, enc_w = gains.shape
     rf, rs = w_first.shape[0], w_second.shape[0]
-    both = rf + rs
-    late = both - SPLIT
     width = w_first.shape[1] * 4
+    mem = members // 4
     def like(a):
         return jax.ShapeDtypeStruct(a.shape, f32)
     def row(a):
@@ -671,6 +773,9 @@
     one = jax.ShapeDtypeStruct((1, 1), f32)
     def buffer(*shape, dtype=f32):
         return pltpu.VMEM(shape, dtype)
+    params = (w_first, w_second, w_head, adapters, gains, head_bias,
+              first_row.reshape(1, -1), first_col.reshape(1, -1), second_row.reshape(1, -1), second_col.reshape(1, -1),
+              head_row, head_col, adapter_sq, gain_sq, bias_sq)
     outs = pl.pallas_call(
         functools.partial(reduce_kernel, enc_w, width, members),
         out_shape=(like(w_first), row(first_row), row(first_col), like(w_first),
@@ -679,23 +784,27 @@
                    like(adapters), like(adapters), like(adapters),
                    like(gains), like(gains), like(gains),
                    like(head_bias), like(head_bias), like(head_bias), one, one, one, one),
-        in_specs=[VM] * 19, out_specs=(VM,) * 25,
+        in_specs=[VM] * 7 + [FAR] * 15, out_specs=(VM,) * 25,
         scratch_shapes=[
-            buffer(4, 2, 2, both, 128, dtype=bf16), buffer(4, 2, 2, both, 128, dtype=bf16),
-            buffer(3, 4, SPLIT, 128, dtype=bf16), buffer(4, SPLIT, 128, dtype=bf16),
-            buffer(3, SPLIT, 128, dtype=bf16), buffer(3, 2, 2, late, 128, dtype=bf16),
-            buffer(2, 2, late, 128, dtype=bf16), buffer(3, late, 128, dtype=bf16),
+            buffer(width, enc_w, dtype=bf16), buffer(mem, enc_w), buffer(256, enc_w), buffer(mem, 8, enc_w),
+            buffer(4, 2, 2, rf, 128, dtype=bf16), buffer(4, 2, 2, rf, 128, dtype=bf16),
+            buffer(4, 2, rf, 128, dtype=bf16), buffer(4, 2, rf, 128, dtype=bf16), buffer(4, 2, rf, 128, dtype=bf16),
+            buffer(4, 2, rf, 128, dtype=bf16), buffer(4, 2, rf, 128), buffer(4, 2, rf, 128, dtype=bf16),
+            buffer(4, rf, 128, dtype=bf16), buffer(4, rf, 128, dtype=bf16), buffer(3, rf, 128, dtype=bf16),
+            buffer(4, 2, 2, rs, 128, dtype=bf16), buffer(4, 2, 2, rs, 128, dtype=bf16), buffer(4, rs, 128, dtype=bf16),
+            buffer(4, 2, rs, 128, dtype=bf16), buffer(4, 2, rs, 128, dtype=bf16), buffer(4, rs, 128, dtype=bf16),
+            buffer(3, rs, 128, dtype=bf16),
             buffer(4, rs, 128, dtype=bf16), buffer(4, rs, 128, dtype=bf16), buffer(3, rs, 128, dtype=bf16),
             buffer(4, rs, 128),
-            buffer(7, 40, 128), buffer(8, 40, 128), buffer(4, 8, 8, 128), buffer(4, 8, 8, 128),
+            buffer(4, 32, 128), buffer(4, 32, 128), buffer(3, 32, 128), buffer(4, 2, 32, 128), buffer(4, 4, 2, 8, 128),
+            buffer(mem, 8, 128), buffer(7, 8, 128), buffer(8, 8, 128), buffer(4, 8, 8, 128),
             buffer(16, 128), buffer(8, 16, 128), buffer(8, 256), buffer(4, 8, 256),
             buffer(8, 128), buffer(4, 2, 2, 2, 8, 128),
-            pltpu.SemaphoreType.DMA((100,)), pltpu.SemaphoreType.DMA((100,)),
+            *[buffer(*p.shape) for p in params], pltpu.SemaphoreType.DMA((15,)),
+            pltpu.SemaphoreType.DMA((112,)), pltpu.SemaphoreType.DMA((112,)),
         ],
-        compiler_params=pltpu.CompilerParams(collective_id=1, has_side_effects=True, vmem_limit_bytes=16 << 20),
-    )(gbuf, hb, small, info, w_first, w_second, w_head, adapters, gains, head_bias,
-      first_row.reshape(1, -1), first_col.reshape(1, -1), second_row.reshape(1, -1), second_col.reshape(1, -1),
-      head_row, head_col, adapter_sq, gain_sq, bias_sq)
+        compiler_params=pltpu.CompilerParams(collective_id=1, has_side_effects=True, vmem_limit_bytes=26 << 20),
+    )(enc, w1_all, fog, sbuf, hb, small.reshape(4, 2, 32, 128), info, *map(far, params))
     outs = call_store(outs)
     for i in (1, 2, 5, 6):
         outs[i] = outs[i].reshape(-1)
@@ -733,10 +842,10 @@
     members = gains.shape[0]
     mem = members // 4
     w_head, head_bias, head_col, bias_sq = w_head.transpose(0, 2, 1), head_bias.T, head_col.T, bias_sq.T
-    buf, hbuf, adbuf, comp, info = call_gather(
+    buf, hbuf, adbuf, enc, onehots, info = call_gather(
         bin_index.T, bin_fraction.T, row_mask, targets, w_first, w_second, w_head, adapters, mem)
-    gbuf, hb, small = call_compute(members, buf, hbuf, adbuf, comp, info, gains, head_bias)
-    return call_reduce(gbuf, hb, small, info, w_first, w_second, w_head, adapters, gains, head_bias,
+    w1_all, fog, sbuf, hb, small = call_compute(members, buf, hbuf, adbuf, enc, onehots, info, gains, head_bias)
+    return call_reduce(enc, w1_all, fog, sbuf, hb, small, info, w_first, w_second, w_head, adapters, gains, head_bias,
                        first_row, first_col, second_row, second_col, head_row, head_col, adapter_sq, gain_sq, bias_sq)
 
 
@@ -770,6 +879,10 @@
     mask = table[:, 64].astype(jnp.int32)
     spot = jnp.where(mask > 0, jnp.cumsum(mask) - 1, -1)
     comp = jnp.dot((jnp.arange(rows)[:, None] == spot[None, :]).astype(bf16), table, preferred_element_type=f32).astype(bf16)
+    levels = jnp.arange(BINS, dtype=f32)
+    where_at = (comp[:, :FEATS].astype(f32) + comp[:, FEATS:2 * FEATS].astype(f32) + comp[:, 2 * FEATS:3 * FEATS].astype(f32))
+    enc = jnp.clip(where_at[:, :, None] - levels, 0.0, 1.0).reshape(rows, enc_width).astype(bf16)
+    onehots = jnp.tile(comp[:, 48:48 + CLASSES], (1, mem))
     info = jnp.zeros((8, 128), f32).at[0].set(jnp.sum(mask).astype(f32)).at[1].set(row_total)
 
     def whole(part):
@@ -785,9 +898,12 @@
     heads = lax.dynamic_slice_in_dim(heads, col_place * mem, mem, 0)
     hbuf = heads.transpose(1, 0, 2).reshape(4, 2, -1, mem * CLASSES)
     adbuf = lax.dynamic_slice_in_dim(lax.all_gather(adapters, "col", axis=0), col_place * mem, mem, 2)
-    gbuf, hb, small = call_compute(members, buf, hbuf, adbuf, comp, info, gains, head_bias.T)
-    rf = enc_width // 8
-    first_part, second_part = unblock(gbuf[..., :rf, :]), unblock(gbuf[..., rf:, :])
+    w1_all, fog, sbuf, hb, small = call_compute(members, buf, hbuf, adbuf, enc, onehots, info, gains, head_bias.T)
+    own_gains = lax.dynamic_slice_in_dim(gains, col_place * mem, mem, 0)
+    sums = jnp.einsum("rk,mrd->mkd", enc, fog, preferred_element_type=f32)
+    first_part = jnp.einsum("mkd,mk->kd", sums, own_gains, precision=HIGH)
+    gain_part = jnp.einsum("mkd,kd->mk", sums, w1_all.astype(f32), precision=HIGH)
+    second_part = unblock(sbuf)
     head_part = hb.astype(f32).reshape(full_width, mem, CLASSES).transpose(1, 0, 2)
 
     def scatter(part):
@@ -796,11 +912,10 @@
     head_grad = lax.all_gather(lax.psum_scatter(head_part, "dp", scatter_dimension=1, tiled=True), "col", axis=0, tiled=True)
     adapter_part = small[:, :32].reshape(mem, 4, 8, 128)[:, :, :5].transpose(2, 0, 1, 3).reshape(5, mem, full_width)
     adapter_grad = lax.psum(lax.all_to_all(adapter_part, "col", 2, 1, tiled=True), "dp")
-    gain_part = small[:, 32:32 + enc_width // 128].reshape(mem, enc_width)
-    bias_part = small[3, 39].reshape(mem, CLASSES)
+    bias_part = small[3, 5].reshape(mem, CLASSES)
     gain_grad, bias_grad = lax.psum(
         (lax.all_gather(gain_part, "col", axis=0, tiled=True), lax.all_gather(bias_part, "col", axis=0, tiled=True)), "dp")
-    loss_sum, residual_sq, branch_sq = lax.psum(jnp.sum(small[:3, 39], axis=1), ("dp", "col"))
+    loss_sum, residual_sq, branch_sq = lax.psum(jnp.sum(small[:3, 5], axis=1), ("dp", "col"))
     first_square = first_grad * first_grad + EPS_SQUARE
     second_square = second_grad * second_grad + EPS_SQUARE
     head_square = head_grad * head_grad + EPS_SQUARE

time: 93 us -> 75.5 us (0.81)
  Pallas kernels: 91.6 us -> 74.4 us
    pallas_call x1, Pallas kernels: 32.2 us -> 16.6 us  [call_compute(): pl.pallas_call(functools.partial(compute_kernel, members), out_shape=(jax...]
    pallas_call x1, Pallas kernels: 35.9 us -> 34.2 us  [call_reduce(): pl.pallas_call(functools.partial(reduce_kernel, enc_w, width, members), o...]
where the time goes in v2:
time: 75.5 us; the launch traced here: 75.3 us
  Pallas kernels  74.4 us (99%)
  between operations  0.85 us (1%)
    pallas_call x1, Pallas kernels, call_reduce(): pl.pallas_call(functools.partial(reduce_kernel, enc_w, width, members), o...  34.2 us
    pallas_call x1, Pallas kernels, call_gather(): pl.pallas_call(gather_kernel, out_shape=(jax.ShapeDtypeStruct((4, 2, 2, 2...  19.9 us
    pallas_call x1, Pallas kernels, call_compute(): pl.pallas_call(functools.partial(compute_kernel, members), out_shape=(jax...  16.6 us
    pallas_call x1, Pallas kernels, call_store(): pl.pallas_call(functools.partial(store_kernel, count), out_shape=tuple((j...  3.74 us

profile of v2, /device:TPU:0, one launch (start us, length us, event | category | flops | bytes accessed | tf_op | source)
XLA Modules:
  0.0 75.3 jit_solution(10714364335779238626)
XLA Ops:
  0.7 19.9 %shard_map.378 = (bf16[4,2,2,2,160,128]{5,4,3,2,1,0:T(8,128)(2,1)S(1)}, bf16[4,2,64,128]{3,2,1,0:T(8,128)(2,1)S(1)}, f32[4,5,8,128]{3,2,1,0:T(8,128)S(1)}, bf16[...) custom-call(s32[16,512]{1,0:T(8,128)} %bitcast.32, f32[16,512]{1,0:T(8,128)} %bitcast.33, ...), custom_call_target="tpu_custom_call" | custom-call | tf_op jit(solution)/shard_map/pallas_call | solution.py:208
  20.6 16.6 %shard_map.379 = (bf16[768,512]{1,0:T(8,128)(2,1)S(1)}, bf16[8,512,512]{2,1,0:T(8,128)(2,1)S(1)}, bf16[4,2,2,2,64,128]{5,4,3,2,1,0:T(8,128)(2,1)S(1)}, bf16[4,2,...) custom-call(bf16[4,2,2,2,160,128]{5,4,3,2,1,0:T(8,128)(2,1)S(1)} %get-tuple-element.87.buf, ...), custom_call_target="tpu_custom_call" | custom-call | tf_op jit(solution)/shard_map/pallas_call | solution.py:433
  37.1 34.2 %shard_map.380 = (f32[96,128]{1,0:T(8,128)S(1)}, f32[1,96]{1,0:T(1,128)S(1)}, f32[1,128]{1,0:T(1,128)S(1)}, f32[96,128]{1,0:T(8,128)S(1)}, f32[64,128]{1,0:T(8,1...) custom-call(bf16[512,768]{1,0:T(8,128)(2,1)S(1)} %get-tuple-element., ...), custom_call_target="tpu_custom_call" | custom-call | tf_op jit(solution)/shard_map/pallas_call | solution.py:779
  71.4 3.7 %shard_map.381 = (f32[96,128]{1,0:T(8,128)}, f32[1,96]{1,0:T(1,128)}, f32[1,128]{1,0:T(1,128)}, f32[96,128]{1,0:T(8,128)}, f32[64,128]{1,0:T(8,128)}, /*index=5*...) custom-call(f32[96,128]{1,0:T(8,128)S(1)} %get-tuple-element.97.refs, ...), custom_call_target="tpu_custom_call" | custom-call | tf_op jit(solution)/shard_map/pallas_call | solution.py:831

commit v3 on v2

--- a/solution.py
+++ b/solution.py
@@ -14,6 +14,7 @@
 R = 64
 GROUPS = 2
 ORDER = (0, 1, 0, 1, 0, 1, 0, 1, 0, 1, 0, 1, 0, 1, 0, 1, 0, 1, 0, 1, 0, 1)
+WIDE = True
 f32, bf16 = jnp.float32, jnp.bfloat16
 
 def dot(a, b):
@@ -57,7 +58,9 @@
 PLANE = ((0, 1), (1, 0), (1, 1))
 DP_PEERS = tuple((kz, ky) for kz in range(4) for ky in range(2))[1:]
 COL_PEERS = ((0, 1), (1, 0), (1, 1))
-SPLIT = 112
+NSEM1 = 28
+NSEM3 = 24
+CUTS = (64, 112)
 
 
 class Sender:
@@ -68,12 +71,36 @@
     def __call__(self, src, dst, target):
         i = self.count
         self.count += 1
+        assert i < self.send_sem.shape[0]
         copy = pltpu.make_async_remote_copy(
             src_ref=src, dst_ref=dst, send_sem=self.send_sem.at[i], recv_sem=self.recv_sem.at[i],
             device_id=target, device_id_type=MESH)
         copy.start()
         self.all.append(copy)
         return copy
+
+    def group(self, whole, copies):
+        i = self.count
+        self.count += 1
+        assert i < self.send_sem.shape[0]
+        for src, dst, target in copies:
+            pltpu.make_async_remote_copy(
+                src_ref=src, dst_ref=dst, send_sem=self.send_sem.at[i], recv_sem=self.recv_sem.at[i],
+                device_id=target, device_id_type=MESH).start()
+        self.all.append(Group(whole, self.send_sem.at[i], self.recv_sem.at[i]))
+        return [self.all[-1]]
+
+
+class Group:
+    def __init__(self, whole, send_sem, recv_sem):
+        self.sent = pltpu.make_async_copy(whole, whole, send_sem)
+        self.landed = pltpu.make_async_copy(whole, whole, recv_sem)
+
+    def wait_recv(self):
+        self.landed.wait()
+
+    def wait_send(self):
+        self.sent.wait()
 
 
 def greet(targets):
@@ -111,54 +138,65 @@
     buf[z, y, x, core, rf:rf + rs, :] = w_second_v[...].astype(bf16)
     pl.semaphore_wait(barrier, count)
     send = Sender(send_sem, recv_sem)
-    s0, s1 = pl.ds(0, SPLIT), pl.ds(SPLIT, rf + rs - SPLIT)
-    own0, own1 = buf.at[z, y, x, core, s0], buf.at[z, y, x, core, s1]
-    a0 = [send(own0, own0, device(z_other(z, k), y, x, core)) for k in (1, 2, 3)]
-    a1 = [send(own1, own1, device(z, other(y, ky), other(x, kx), core)) for ky, kx in PLANE]
+    parts = [pl.ds(lo, hi - lo) for lo, hi in zip((0,) + CUTS, CUTS + (rf + rs,))]
+    mine = [buf.at[z, y, x, core, part] for part in parts]
+    a0, b0 = [], []
+    for i in range(len(parts) - 1):
+        a0.append(send.group(buf.at[0:3, 0, 0, 0, parts[i]],
+                             [(mine[i], mine[i], device(z_other(z, k), y, x, core)) for k in (1, 2, 3)]))
+        if i == 0:
+            a1 = send.group(buf.at[0:3, 0, 0, 0, parts[-1]],
+                            [(mine[-1], mine[-1], device(z, other(y, ky), other(x, kx), core)) for ky, kx in PLANE])
     for load in loads[2:]:
         load.wait()
     hbuf[z, y] = w_head_v[pl.ds(me_c * mem, mem)].reshape(mem * CLASSES, rs).T.astype(bf16)
     adbuf[me_c] = adapters[:, pl.ds(pl.multiple_of(me_c * mem, mem), mem), :]
-    slot = rows // 8
+    slot = rows // 16
     i_row = lax.broadcasted_iota(jnp.int32, (rows, rows), 0)
     i_col = lax.broadcasted_iota(jnp.int32, (rows, rows), 1)
     me_d = 2 * z + y
-    wanted = (i_row % slot) * 8 + (i_row // slot + me_d) % 8
-    deal = (i_col == wanted).astype(bf16)
+    p_row = lax.broadcasted_iota(jnp.int32, (rows // 2, rows), 0)
+    p_col = lax.broadcasted_iota(jnp.int32, (rows // 2, rows), 1)
+    wanted = (p_row % slot) * 8 + (p_row // slot + me_d) % 8
     frac = bin_fraction_v[...]
-    hi = frac.astype(bf16).astype(f32)
     mask = row_mask_v[...].astype(f32)
     length = jnp.sum(mask, axis=1, keepdims=True)
     high = jnp.floor(length * (1.0 / 16.0))
     c_i = lax.broadcasted_iota(jnp.int32, (CLASSES, rows), 0)
-    m_i = lax.broadcasted_iota(jnp.int32, (64, rows), 0)
-    marks = jnp.where(m_i == 0, mask, jnp.where(m_i == 1, high, jnp.where(m_i == 2, length - 16.0 * high, 0.0)))
-    columns = jnp.concatenate([bin_index_v[...].astype(f32), hi, frac - hi, jnp.where(c_i == targets_v[...], mask, 0.0), marks], axis=0)
-    table[...] = dot_t(deal, columns.astype(bf16)).astype(bf16)
+    marks = jnp.where(c_i == 0, mask, jnp.where(c_i == 1, high, jnp.where(c_i == 2, length - 16.0 * high, 0.0)))
+    columns = jnp.concatenate([bin_index_v[...].astype(f32), frac, jnp.where(c_i == targets_v[...], mask, 0.0), marks], axis=0).astype(bf16)
+    nothing = jnp.zeros((64, rows), bf16)
+    table[...] = (dot_t((p_col == wanted).astype(bf16), jnp.concatenate([columns, nothing], axis=0))
+                  + dot_t((p_col == wanted + 8 * slot).astype(bf16), jnp.concatenate([nothing, columns], axis=0))).astype(bf16)
     own_rows = pl.ds(pl.multiple_of(me_d * slot, slot), slot)
     recv[own_rows, :] = table[own_rows, :]
     t = []
     for kz, ky in DP_PEERS:
         pz, py = z_other(z, kz), other(y, ky)
         theirs = pl.ds(pl.multiple_of((2 * pz + py) * slot, slot), slot)
-        t.append(send(table.at[theirs], recv.at[own_rows], device(pz, py, x, core)))
-    h = [send(hbuf.at[z, y], hbuf.at[z, y], device(z_other(z, k), y, x, core)) for k in (1, 2, 3)]
+        t.append((table.at[theirs], recv.at[own_rows], device(pz, py, x, core)))
+    t = send.group(recv.at[0:7 * slot], t)
+    h = send.group(hbuf.at[0:3, 0], [(hbuf.at[z, y], hbuf.at[z, y], device(z_other(z, k), y, x, core)) for k in (1, 2, 3)])
+    ad = []
     for kx, kc in COL_PEERS:
         px, pc = other(x, kx), other(core, kc)
         theirs = pl.ds(pl.multiple_of((2 * px + pc) * mem, mem), mem)
-        send(adapters.at[:, theirs, :], adbuf.at[me_c], device(z, y, px, pc))
-    ad = send.all[-3:]
-    for cp in a0:
-        cp.wait_recv()
-    b0 = [send(buf.at[:, y, x, core, s0], buf.at[:, y, x, core, s0], device(z, other(y, ky), other(x, kx), core))
-          for ky, kx in PLANE]
+        ad.append((adapters.at[:, theirs, :], adbuf.at[me_c], device(z, y, px, pc)))
+    ad = send.group(adbuf.at[0:3], ad)
     mate = device(z, y, x, 1 - core)
-    for cp in a1:
-        cp.wait_recv()
-    b1 = [send(buf.at[z, :, :, core, s1], buf.at[z, :, :, core, s1], device(z_other(z, k), y, x, core))
-          for k in (1, 2, 3)]
-    last = [send(buf.at[:, y, x, core, s0], buf.at[:, y, x, core, s0], mate),
-            send(buf.at[z, :, :, core, s1], buf.at[z, :, :, core, s1], mate)]
+    last = []
+    for i, part in enumerate(parts[:-1]):
+        for cp in a0[i]:
+            cp.wait_recv()
+        column = buf.at[:, y, x, core, part]
+        b0.append([send(column, column, device(z, other(y, ky), other(x, kx), core)) for ky, kx in PLANE])
+        if i == 0:
+            for cp in a1:
+                cp.wait_recv()
+            plane = buf.at[z, :, :, core, parts[-1]]
+            b1 = [send(plane, plane, device(z_other(z, k), y, x, core)) for k in (1, 2, 3)]
+            last.append(send(plane, plane, mate))
+        last.append(send(column, column, mate))
     for cp in h:
         cp.wait_recv()
     h2 = send(hbuf.at[:, y], hbuf.at[:, y], device(z, 1 - y, x, core))
@@ -166,36 +204,38 @@
         cp.wait_recv()
     lane8 = lax.broadcasted_iota(jnp.int32, (8, 128), 1)
     got = recv[...]
-    mask_row = dot_t((lane8 == 64).astype(bf16), got)
+    mask_row = jnp.concatenate([dot_t((lane8 == 48).astype(bf16), got), dot_t((lane8 == 112).astype(bf16), got)], axis=1)
     pos = dot(mask_row.astype(bf16), (i_row < i_col).astype(bf16))
     spot = jnp.where(mask_row > 0.5, pos, -1.0)[0:1]
     perm = (i_row.astype(f32) == spot).astype(bf16)
+    lane = lax.broadcasted_iota(jnp.int32, (1, 128), 1)
+    low_half = (lane < 64).astype(bf16)
+    comp = (dot(perm[:, :rows // 2], got * low_half) + dot(perm[:, rows // 2:], got * (1.0 - low_half))).astype(bf16)
     enc_w, hw = enc.shape[1], onehots.shape[1]
     kk = lax.broadcasted_iota(jnp.int32, (128, enc_w), 1)
     ll = lax.broadcasted_iota(jnp.int32, (128, enc_w), 0)
     ff = ll & (FEATS - 1)
-    spread = ((ll < 48) & (kk >= ff * BINS) & (kk < (ff + 1) * BINS)).astype(bf16)
+    spread = (((ll & 63) < 2 * FEATS) & (kk >= ff * BINS) & (kk < (ff + 1) * BINS)).astype(bf16)
     lev = (lax.broadcasted_iota(jnp.int32, (1, enc_w), 1) % BINS).astype(f32)
+    enc[...] = jnp.clip(dot(comp, spread) - lev, 0.0, 1.0).astype(bf16)
     l2 = lax.broadcasted_iota(jnp.int32, (128, hw), 0)
     c2 = lax.broadcasted_iota(jnp.int32, (128, hw), 1)
-    oh_spread = (l2 == 48 + (c2 & (CLASSES - 1))).astype(bf16)
-    comp = dot(perm, got).astype(bf16)
-    enc[...] = jnp.clip(dot(comp, spread) - lev, 0.0, 1.0).astype(bf16)
-    onehots[...] = dot(comp, oh_spread).astype(bf16)
-    lane = lax.broadcasted_iota(jnp.int32, (1, 128), 1)
-    per_row = jnp.where(lane == 65, 16.0, jnp.where(lane == 66, 1.0, 0.0))
-    total = jnp.sum(jnp.sum(got.astype(f32), axis=0, keepdims=True) * per_row, axis=1, keepdims=True) / slot
+    onehots[...] = dot(comp, ((l2 & 63) == 2 * FEATS + (c2 & (CLASSES - 1))).astype(bf16)).astype(bf16)
+    per_row = jnp.where((lane & 63) == 49, 16.0, jnp.where((lane & 63) == 50, 1.0, 0.0))
+    total = jnp.sum(jnp.sum(got.astype(f32), axis=0, keepdims=True) * per_row, axis=1, keepdims=True) / (2 * slot)
     info[0:1, :] = jnp.zeros((1, 128), f32) + jnp.sum(mask_row[0:1], axis=1, keepdims=True)
     info[1:2, :] = jnp.zeros((1, 128), f32) + total
     info[2:8, :] = jnp.zeros((6, 128), f32)
-    for cp, k in zip(b1, (1, 2, 3)):
-        cp.wait_recv()
-        pz = z_other(z, k)
-        last.append(send(buf.at[pz, :, :, core, s1], buf.at[pz, :, :, core, s1], mate))
-    for cp, (ky, kx) in zip(b0, PLANE):
-        cp.wait_recv()
-        py, px = other(y, ky), other(x, kx)
-        last.append(send(buf.at[:, py, px, core, s0], buf.at[:, py, px, core, s0], mate))
+    for i, part in enumerate(parts[:-1]):
+        for cp, (ky, kx) in zip(b0[i], PLANE):
+            cp.wait_recv()
+            column = buf.at[:, other(y, ky), other(x, kx), core, part]
+            last.append(send(column, column, mate))
+        if i == 0:
+            for cp, k in zip(b1, (1, 2, 3)):
+                cp.wait_recv()
+                plane = buf.at[z_other(z, k), :, :, core, parts[-1]]
+                last.append(send(plane, plane, mate))
     for cp in last + ad + [h2]:
         cp.wait_recv()
     for cp in send.all:
@@ -216,13 +256,13 @@
             jax.ShapeDtypeStruct((8, 128), f32),
         ),
         in_specs=[FAR] * 8, out_specs=(VM,) * 6,
-        scratch_shapes=[pltpu.VMEM((rows, 128), bf16), pltpu.VMEM((rows, 128), bf16),
+        scratch_shapes=[pltpu.VMEM((rows // 2, 128), bf16), pltpu.VMEM((rows // 2, 128), bf16),
                         pltpu.VMEM(w_first.shape, f32), pltpu.VMEM(w_second.shape, f32),
                         pltpu.VMEM(w_head.shape, f32), pltpu.VMEM(adapters.shape, f32),
                         pltpu.VMEM(bin_index.shape, jnp.int32), pltpu.VMEM(bin_fraction.shape, f32),
                         pltpu.VMEM((1, rows), jnp.int32), pltpu.VMEM((1, rows), jnp.int32),
                         pltpu.SemaphoreType.DMA((8,)),
-                        pltpu.SemaphoreType.DMA((40,)), pltpu.SemaphoreType.DMA((40,))],
+                        pltpu.SemaphoreType.DMA((NSEM1,)), pltpu.SemaphoreType.DMA((NSEM1,))],
         compiler_params=pltpu.CompilerParams(collective_id=0, has_side_effects=True, vmem_limit_bytes=16 << 20),
     )(*map(far, (bin_index, bin_fraction, row_mask.reshape(1, -1), targets.reshape(1, -1),
                  w_first, w_second, w_head, adapters)))
@@ -281,8 +321,6 @@
     bias = jnp.sum(jnp.where(at == me_c * mem + owner, wide, 0.0), axis=0, keepdims=True)
     n_rows = jnp.max(info[0:1, :]).astype(jnp.int32)
     loss_scale = 1.0 / (members * info[1:2, :])
-    tiles = (n_rows + (R - 1)) // R
-    fog_all[...] = jnp.zeros_like(fog_all)
     second_acc[...] = jnp.zeros_like(second_acc)
     head_acc[...] = jnp.zeros_like(head_acc)
     adapt[...] = jnp.zeros_like(adapt)
@@ -292,7 +330,7 @@
     s_j = lax.broadcasted_iota(jnp.int32, (hw, hw), 1) // CLASSES
     seg = (s_i == s_j).astype(bf16)
 
-    def group(rows, pad_rows, oh, mk, enc, ms, out):
+    def group(R, rows, pad_rows, oh, mk, enc, ms, out, grads):
         count = len(ms)
         fin = jnp.concatenate([enc * low_gains[m:m + 1, :] for m in ms], axis=0)
         fo = dot(fin, w1[...])
@@ -363,8 +401,11 @@
         yield
         ig = dot(og, w2t[...])
         yield
-        head_acc[...] += t_dot(lgm, st)
-        second_acc[...] += t_dot(sin, og)
+        grads.append((lgm, st, sin, og))
+        if len(grads) == GROUPS:
+            lgms, sts_all, sins_all, ogs_all = (jnp.concatenate(v, axis=0) for v in zip(*grads))
+            head_acc[...] += t_dot(lgms, sts_all)
+            second_acc[...] += t_dot(sins_all, ogs_all)
         yield
         for i, m in enumerate(ms):
             igm = ig[i * R:(i + 1) * R]
@@ -376,15 +417,15 @@
             fog_all[m, rows, :] = (low * halves[0, m:m + 1, :]).astype(bf16)
         yield
 
-    def tile(t, carry):
-        rows = pl.ds(pl.multiple_of(t * R, R), R)
+    def tile(R, start):
+        rows = pl.ds(pl.multiple_of(start, 64), R)
         enc = enc_all[rows, :]
         oh = onehots[rows, :].astype(f32)
-        mk = (lax.broadcasted_iota(jnp.int32, (R, hw), 0) + t * R < n_rows).astype(f32)
-        pad_rows = jnp.maximum((t + 1) * R - n_rows, 0).astype(f32)
-        out = []
+        mk = (lax.broadcasted_iota(jnp.int32, (R, hw), 0) + start < n_rows).astype(f32)
+        pad_rows = jnp.maximum(start + R - n_rows, 0).astype(f32)
+        out, grads = [], []
         per = mem // GROUPS
-        runs = [group(rows, pad_rows, oh, mk, enc, tuple(range(g * per, (g + 1) * per)), out) for g in range(GROUPS)]
+        runs = [group(R, rows, pad_rows, oh, mk, enc, tuple(range(g * per, (g + 1) * per)), out, grads) for g in range(GROUPS)]
         for g in ORDER:
             next(runs[g])
         lane = lax.broadcasted_iota(jnp.int32, (1, hw), 1)
@@ -395,9 +436,24 @@
             lgf = jnp.where(late, out[g][1], lgf)
         sums[0, :, :hw] += fold8(lgf)
         sums[1, :, :hw] += fold8(loss_c)
+
+    def wide_tile(t, carry):
+        tile(2 * R, t * 2 * R)
         return carry
 
-    lax.fori_loop(0, tiles, tile, 0)
+    def narrow_tile(t, carry):
+        tile(R, t * R)
+        return carry
+
+    def clear(t, carry):
+        for m in range(mem):
+            fog_all[m, pl.ds(pl.multiple_of(t * R, R), R), :] = jnp.zeros((R, width), bf16)
+        return carry
+    wide = (n_rows + (R - 1)) // (2 * R) if WIDE else 0
+    lax.fori_loop(0, wide, wide_tile, 0)
+    tiles = jnp.maximum((n_rows + (R - 1)) // R, 2 * wide)
+    lax.fori_loop(2 * wide, tiles, narrow_tile, 0)
+    lax.fori_loop(tiles, rows_all // R, clear, 0)
     for d in range(8):
         for c in range(4):
             lanes = slice(128 * c, 128 * c + 128)
@@ -449,7 +505,7 @@
             pltpu.VMEM((5, mem, 8, width), f32), pltpu.VMEM((5, 8, width), f32), pltpu.VMEM((5, mem, width), f32),
             pltpu.VMEM(gains.shape, f32), pltpu.VMEM(bias.shape, f32), pltpu.SemaphoreType.DMA((2,)),
         ],
-        compiler_params=pltpu.CompilerParams(vmem_limit_bytes=30 << 20),
+        compiler_params=pltpu.CompilerParams(vmem_limit_bytes=36 << 20),
     )(buf, hbuf, adbuf, enc, onehots, info, far(gains), far(bias))
 
 
@@ -463,11 +519,11 @@
                   o_adapter_grad, o_adapter_sq, o_adapter_new,
                   o_gain_grad, o_gain_sq, o_gain_new,
                   o_bias_grad, o_bias_sq, o_bias_new,
-                  o_loss, o_rows, o_residual, o_branch,
+                  o_scalars,
                   w1t, own_gains, first_acc, gain_acc, far_half, own_half, far_got, own_got, far_sum, far_x, own_sum, own_pair, first_y, first_pair, first_in,
                   second_got, second_sum, second_x, second_own, second_y, second_pair, second_in,
                   hy, hsum, hz, hcol, small_y, small_sum, small_z, gall, ca, gain_part, gain_in, gain_all, gain_cols,
-                  colmsg, colall, rowmsg, rowall, msg, msgall,
+                  colmsg, colall, rowmsg, rowall, msg, msgall, early_line,
                   w_first, w_second, w_head, adapters, gains, head_bias,
                   first_row, first_col, second_row, second_col, head_row, head_col, adapter_sq, gain_sq, bias_sq,
                   load_sem, send_sem, recv_sem):
@@ -531,8 +587,15 @@
             for c in range(2):
                 half[d // 2, d % 2, c] = flipped[rf * d:rf * (d + 1), 128 * c:128 * c + 128]
 
-    def to_z(ref, into, send=send):
-        return [send(ref(z_other(z, k)), into(k), device(z_other(z, k), y, x, core)) for k in (1, 2, 3)]
+    def to_z(whole, ref, into):
+        return send.group(whole, [(ref(z_other(z, k)), into(k), device(z_other(z, k), y, x, core)) for k in (1, 2, 3)])
+
+    def to_dp(whole, ref, into):
+        return send.group(whole, [(ref(2 * pz + py), into(i), device(pz, py, x, core)) for i, (pz, py) in enumerate(dp_peers)])
+
+    def to_col(whole, ref, into):
+        return send.group(whole, [(ref(2 * other(x, kx) + other(core, kc)), into, device(z, y, other(x, kx), other(core, kc)))
+                                  for kx, kc in COL_PEERS])
 
     y_mate = device(z, 1 - y, x, core)
     w1t[...] = w1_all[...].T
@@ -548,10 +611,10 @@
     swap_second = send(sbuf.at[:, :, :, 1 - core], second_got, mate)
     small1 = send(small.at[:, 1 - y], small_y, y_mate)
     head1 = send(hb.at[:, 1 - y], hy, y_mate)
-    quarter(x, early)
     received([swap_far])
     far_sum[...] = (far_half[:, :, core].astype(f32) + far_got[...].astype(f32)).astype(bf16)
     across_far = send(far_sum, far_x, beside)
+    quarter(x, early)
     received([swap_second])
     second_sum[...] = (sbuf[:, :, :, core].astype(f32) + second_got[...].astype(f32)).astype(bf16)
     second2 = send(second_sum.at[:, 1 - y], second_y, y_mate)
@@ -563,13 +626,13 @@
         row = jnp.sum(gain_acc[m], axis=0, keepdims=True)
         for i in range(enc_w // 128):
             gain_part[m, i:i + 1, :] = row[:, 128 * i:128 * i + 128]
-    gain_deal = [send(gain_part.at[2 * pz + py], gain_in.at[i], device(pz, py, x, core)) for i, (pz, py) in enumerate(dp_peers)]
+    gain_deal = to_dp(gain_in, lambda d: gain_part.at[d], lambda i: gain_in.at[i])
     received([small1])
     small_sum[...] = small[:, y] + small_y[...]
-    small2 = to_z(lambda pz: small_sum.at[pz], lambda k: small_z.at[k - 1])
+    small2 = to_z(small_z, lambda pz: small_sum.at[pz], lambda k: small_z.at[k - 1])
     received([head1])
     hsum[...] = (hb[:, y].astype(f32) + hy[...].astype(f32)).astype(bf16)
-    head2 = to_z(lambda pz: hsum.at[pz], lambda k: hz.at[k - 1])
+    head2 = to_z(hz, lambda pz: hsum.at[pz], lambda k: hz.at[k - 1])
     for load in loads[1:]:
         load.wait()
     w1, w2 = w_first[...], w_second[...]
@@ -589,24 +652,24 @@
     for i in range(7):
         mine = mine + gain_in[i]
     gain_all[me_d] = mine
-    gain_dp = [send(gain_all.at[me_d], gain_all.at[me_d], device(pz, py, x, core)) for pz, py in dp_peers]
+    gain_dp = to_dp(gain_in, lambda d: gain_all.at[me_d], lambda i: gain_all.at[me_d])
     received(small2)
     gall[z, y] = ((small_sum[z] + small_z[0]) + small_z[1]) + small_z[2]
-    small3 = to_z(lambda pz: gall.at[z, y], lambda k: gall.at[z, y])
+    small3 = to_z(gall.at[0:3, 0], lambda pz: gall.at[z, y], lambda k: gall.at[z, y])
     received(head2)
     hcol[me_c] = (hsum[z].astype(f32) + hz[0].astype(f32)) + (hz[1].astype(f32) + hz[2].astype(f32))
-    head3 = [send(hcol.at[me_c], hcol.at[me_c], device(z, y, other(x, kx), other(core, kc))) for kx, kc in COL_PEERS]
+    head3 = to_col(hcol.at[0:3], lambda c: hcol.at[me_c], hcol.at[me_c])
     received([second3])
     second_pair[...] = (second_own[:, x].astype(f32) + second_x[...].astype(f32)).astype(bf16)
-    second4 = to_z(lambda pz: second_pair.at[pz], lambda k: second_in.at[k - 1])
+    second4 = to_z(second_in, lambda pz: second_pair.at[pz], lambda k: second_in.at[k - 1])
     received([first2])
     first_pair[...] = (own_pair[:, y].astype(f32) + first_y[...].astype(f32)).astype(bf16)
-    first3 = to_z(lambda pz: first_pair.at[pz], lambda k: first_in.at[k - 1])
+    first3 = to_z(first_in, lambda pz: first_pair.at[pz], lambda k: first_in.at[k - 1])
     received(small3)
     small4 = send(gall.at[:, y], gall.at[:, y], y_mate)
     received(gain_dp)
     gain_cols[me_c] = gain_all[...]
-    gain_spread = [send(gain_all, gain_cols.at[me_c], device(z, y, other(x, kx), other(core, kc))) for kx, kc in COL_PEERS]
+    gain_spread = to_col(gain_cols.at[0:3], lambda c: gain_all, gain_cols.at[me_c])
     received(second4)
     second = second_pair[z].astype(f32)
     for i in range(3):
@@ -634,11 +697,7 @@
     received([small4])
     own8 = pl.ds(pl.multiple_of(8 * me_c, 8), 8)
     ca[me_c] = gall[:, :, own8, :]
-    spread_col = []
-    for kx, kc in COL_PEERS:
-        px, pc = other(x, kx), other(core, kc)
-        theirs = pl.ds(pl.multiple_of(8 * (2 * px + pc), 8), 8)
-        spread_col.append(send(gall.at[:, :, theirs], ca.at[me_c], device(z, y, px, pc)))
+    spread_col = to_col(ca.at[0:3], lambda c: gall.at[:, :, pl.ds(pl.multiple_of(8 * c, 8), 8)], ca.at[me_c])
     received(first3)
     first = first_pair[z].astype(f32)
     for i in range(3):
@@ -649,8 +708,8 @@
     rowall[me_c] = rowmsg[...]
     colmsg[0:1, :] = add_up(first_sq)
     colall[me_d] = colmsg[...]
-    r1 = [send(colmsg, colall.at[me_d], device(z_other(z, kz), other(y, ky), x, core)) for kz, ky in DP_PEERS]
-    r1 += [send(rowmsg, rowall.at[me_c], device(z, y, other(x, kx), other(core, kc))) for kx, kc in COL_PEERS]
+    r1 = to_dp(colall.at[0:7], lambda d: colmsg, lambda i: colall.at[me_d])
+    r1 += to_col(rowall.at[0:3], lambda c: rowmsg, rowall.at[me_c])
     received(spread_col)
     fold = (lax.broadcasted_iota(jnp.int32, (CLASSES, hw), 1) % CLASSES
             == lax.broadcasted_iota(jnp.int32, (CLASSES, hw), 0)).astype(f32)
@@ -686,12 +745,18 @@
     bias_up = bias * lax.rsqrt(bias_state)
     o_bias_new[...] = apply(head_bias[...], bias_up, total(bias_up * bias_up), total(head_bias[...] * head_bias[...]), members * CLASSES)
     rows_total = info[1:2, 0:1]
-    o_rows[...] = rows_total
-    o_loss[...] = lane_sum(sum(ca[c, 0, 0, 5:6, :] for c in range(4)))
+    loss_total = lane_sum(sum(ca[c, 0, 0, 5:6, :] for c in range(4)))
     spread_over = rows_total * (members * width)
-    o_residual[...] = jnp.sqrt(lane_sum(sum(ca[c, 0, 1, 5:6, :] for c in range(4))) / spread_over)
-    o_branch[...] = jnp.sqrt(lane_sum(sum(ca[c, 1, 0, 5:6, :] for c in range(4))) / spread_over)
+    residual = jnp.sqrt(lane_sum(sum(ca[c, 0, 1, 5:6, :] for c in range(4))) / spread_over)
+    branch_size = jnp.sqrt(lane_sum(sum(ca[c, 1, 0, 5:6, :] for c in range(4))) / spread_over)
+    spot = lax.broadcasted_iota(jnp.int32, (8, 128), 0)
+    o_scalars[...] = jnp.where(spot == 0, loss_total, jnp.where(spot == 1, rows_total, jnp.where(spot == 2, residual, branch_size)))
     hcol_old = to_lanes(head_col[...])
+    lane = lax.broadcasted_iota(jnp.int32, (1, 128), 1)
+    line = jnp.zeros((1, 128), f32)
+    for i, v in enumerate([total(u * u) for u in adapter_up] + adapter_w):
+        line = jnp.where(lane == 8 + i, v, line)
+    early_line[...] = jnp.where(lax.broadcasted_iota(jnp.int32, (8, 128), 0) == 0, line, 0.0)
     for cp in r1:
         cp.wait_recv()
     col_sums = colall[0]
@@ -703,27 +768,23 @@
     first_c = decay * first_col[...] + (1.0 - decay) / enc_w * col_sums[0:1]
     second_c = decay * second_col[...] + (1.0 - decay) / width * col_sums[1:2]
     head_c = decay * hcol_old[0:4] + (1.0 - decay) / width * col_sums[2:6]
+    ones1 = jnp.ones((1, 128), f32)
+    first_up = first * lax.rsqrt(hdot(first_r, ones1, ((0,), (0,))) * first_c)
+    second_up = second * lax.rsqrt(hdot(second_r, ones1, ((0,), (0,))) * second_c)
+    head_up = [hg[c] * lax.rsqrt(hrowx[c] * head_c[c:c + 1] / (col_sums[8 + c:9 + c] / width)) for c in range(4)]
+    scalars = [total(first_up * first_up), lane_sum(first_r), total(second_up * second_up), lane_sum(second_r),
+               own_w[0], own_w[1], total(sum(u * u for u in head_up)), own_w[2]]
+    line = jnp.sum(early_line[...], axis=0, keepdims=True)
+    for i, v in enumerate(scalars):
+        line = jnp.where(lane == i, v, line)
+    msg[...] = jnp.broadcast_to(line, (8, 128))
+    msgall[4 * me_d + me_c] = msg[...]
+    r2 = send.group(msgall.at[0:31], [(msg, msgall.at[4 * me_d + me_c], target) for target in everyone[::-1]])
     o_first_row[...] = first_r
     o_second_row[...] = second_r
     o_first_col[...] = first_c
     o_second_col[...] = second_c
     o_head_col[...] = from_lanes(jnp.concatenate([head_c, jnp.zeros((4, 128), f32)], axis=0))
-    ones1 = jnp.ones((1, 128), f32)
-    first_up = first * lax.rsqrt(hdot(first_r, ones1, ((0,), (0,))) * first_c)
-    second_up = second * lax.rsqrt(hdot(second_r, ones1, ((0,), (0,))) * second_c)
-    head_up = [hg[c] * lax.rsqrt(hrowx[c] * head_c[c:c + 1] / (col_sums[8 + c:9 + c] / width)) for c in range(4)]
-    lane = lax.broadcasted_iota(jnp.int32, (1, 128), 1)
-    scalars = [total(first_up * first_up), lane_sum(first_r), total(second_up * second_up), lane_sum(second_r),
-               own_w[0], own_w[1], sum(total(u * u) for u in head_up), own_w[2]]
-    scalars += [total(u * u) for u in adapter_up] + adapter_w
-    line = jnp.zeros((1, 128), f32)
-    for i, v in enumerate(scalars):
-        line = jnp.where(lane == i, v, line)
-    msg[...] = jnp.broadcast_to(line, (8, 128))
-    msgall[z, y, x, core] = msg[...]
-    r2 = []
-    for target in everyone:
-        r2.append(send(msg, msgall.at[z, y, x, core], target))
     received(gain_spread)
     for c in range(4):
         for i in range(enc_w // 128):
@@ -737,14 +798,14 @@
         cp.wait_send()
     for cp in r2:
         cp.wait_recv()
-    def over_dp(cx, cc):
-        out = msgall[0, 0, cx, cc, 0:1, :]
+    def over_dp(c):
+        out = msgall[c, 0:1, :]
         for d in range(1, 8):
-            out = out + msgall[d // 2, d % 2, cx, cc, 0:1, :]
+            out = out + msgall[4 * d + c, 0:1, :]
         return out
-    s_dp = over_dp(x, core)
-    s_all = (over_dp(0, 0) + over_dp(0, 1)) + (over_dp(1, 0) + over_dp(1, 1))
-    s_col = (msgall[z, y, 0, 0, 0:1, :] + msgall[z, y, 0, 1, 0:1, :]) + (msgall[z, y, 1, 0, 0:1, :] + msgall[z, y, 1, 1, 0:1, :])
+    s_dp = over_dp(me_c)
+    s_all = (over_dp(0) + over_dp(1)) + (over_dp(2) + over_dp(3))
+    s_col = (msgall[4 * me_d, 0:1, :] + msgall[4 * me_d + 1, 0:1, :]) + (msgall[4 * me_d + 2, 0:1, :] + msgall[4 * me_d + 3, 0:1, :])
     def item(v, i):
         return lane_sum(jnp.where(lane == i, v, 0.0))
     first_mean = item(s_dp, 1) / enc_w
@@ -770,7 +831,6 @@
         return jax.ShapeDtypeStruct(a.shape, f32)
     def row(a):
         return jax.ShapeDtypeStruct((1, a.shape[0]), f32)
-    one = jax.ShapeDtypeStruct((1, 1), f32)
     def buffer(*shape, dtype=f32):
         return pltpu.VMEM(shape, dtype)
     params = (w_first, w_second, w_head, adapters, gains, head_bias,
@@ -783,8 +843,8 @@
                    like(w_head), like(head_row), like(head_col), like(w_head),
                    like(adapters), like(adapters), like(adapters),
                    like(gains), like(gains), like(gains),
-                   like(head_bias), like(head_bias), like(head_bias), one, one, one, one),
-        in_specs=[VM] * 7 + [FAR] * 15, out_specs=(VM,) * 25,
+                   like(head_bias), like(head_bias), like(head_bias), jax.ShapeDtypeStruct((8, 128), f32)),
+        in_specs=[VM] * 7 + [FAR] * 15, out_specs=(VM,) * 22,
         scratch_shapes=[
             buffer(width, enc_w, dtype=bf16), buffer(mem, enc_w), buffer(256, enc_w), buffer(mem, 8, enc_w),
             buffer(4, 2, 2, rf, 128, dtype=bf16), buffer(4, 2, 2, rf, 128, dtype=bf16),
@@ -799,9 +859,9 @@
             buffer(4, 32, 128), buffer(4, 32, 128), buffer(3, 32, 128), buffer(4, 2, 32, 128), buffer(4, 4, 2, 8, 128),
             buffer(mem, 8, 128), buffer(7, 8, 128), buffer(8, 8, 128), buffer(4, 8, 8, 128),
             buffer(16, 128), buffer(8, 16, 128), buffer(8, 256), buffer(4, 8, 256),
-            buffer(8, 128), buffer(4, 2, 2, 2, 8, 128),
+            buffer(8, 128), buffer(32, 8, 128), buffer(8, 128),
             *[buffer(*p.shape) for p in params], pltpu.SemaphoreType.DMA((15,)),
-            pltpu.SemaphoreType.DMA((112,)), pltpu.SemaphoreType.DMA((112,)),
+            pltpu.SemaphoreType.DMA((NSEM3,)), pltpu.SemaphoreType.DMA((NSEM3,)),
         ],
         compiler_params=pltpu.CompilerParams(collective_id=1, has_side_effects=True, vmem_limit_bytes=26 << 20),
     )(enc, w1_all, fog, sbuf, hb, small.reshape(4, 2, 32, 128), info, *map(far, params))
@@ -818,21 +878,28 @@
 
 
 def store_kernel(count, *refs):
-    sems = refs[2 * count]
-    copies = [pltpu.make_async_copy(refs[i], refs[count + i], sems.at[i]) for i in range(count)]
+    arrays, scalars = refs[:count], refs[count]
+    outs, singles = refs[count + 1:2 * count + 1], refs[2 * count + 1:2 * count + 5]
+    kept, sems = refs[2 * count + 5:2 * count + 9], refs[2 * count + 9]
+    copies = [pltpu.make_async_copy(src, dst, sems.at[i]) for i, (src, dst) in enumerate(zip(arrays, outs))]
     for copy in copies:
         copy.start()
+    for i, (one, single) in enumerate(zip(kept, singles)):
+        one[...] = scalars[i:i + 1, 0:1]
+        copies.append(pltpu.make_async_copy(one, single, sems.at[count + i]))
+        copies[-1].start()
     for copy in copies:
         copy.wait()
 
 
 def call_store(arrays):
-    count = len(arrays)
+    count = len(arrays) - 1
+    one = jax.ShapeDtypeStruct((1, 1), f32)
     return list(pl.pallas_call(
         functools.partial(store_kernel, count),
-        out_shape=tuple(jax.ShapeDtypeStruct(a.shape, a.dtype) for a in arrays),
-        in_specs=[VM] * count, out_specs=(FAR,) * count,
-        scratch_shapes=[pltpu.SemaphoreType.DMA((count,))],
+        out_shape=tuple(jax.ShapeDtypeStruct(a.shape, a.dtype) for a in arrays[:-1]) + (one,) * 4,
+        in_specs=[VM] * (count + 1), out_specs=(FAR,) * (count + 4),
+        scratch_shapes=[pltpu.VMEM((1, 1), f32)] * 4 + [pltpu.SemaphoreType.DMA((count + 4,))],
         compiler_params=pltpu.CompilerParams(vmem_limit_bytes=16 << 20),
     )(*arrays))
 

time: 75.5 us -> 67.5 us (0.89)
  Pallas kernels: 74.4 us -> 66.5 us
    pallas_call x1, Pallas kernels: 34.2 us -> 31.6 us  [call_reduce(): pl.pallas_call(functools.partial(reduce_kernel, enc_w, width, members), o...]
    pallas_call x1, Pallas kernels: 3.74 us -> 1.3 us  [call_store(): pl.pallas_call(functools.partial(store_kernel, count), out_shape=tuple((j...]
    pallas_call x1, Pallas kernels: 19.9 us -> 17.8 us  [call_gather(): pl.pallas_call(gather_kernel, out_shape=(jax.ShapeDtypeStruct((4, 2, 2, 2...]
    pallas_call x1, Pallas kernels: 16.6 us -> 15.8 us  [call_compute(): pl.pallas_call(functools.partial(compute_kernel, members), out_shape=(jax...]
where the time goes in v3:
time: 67.5 us; the launch traced here: 67.3 us
  Pallas kernels  66.5 us (99%)
  between operations  0.85 us (1%)
    pallas_call x1, Pallas kernels, call_reduce(): pl.pallas_call(functools.partial(reduce_kernel, enc_w, width, members), o...  31.6 us
    pallas_call x1, Pallas kernels, call_gather(): pl.pallas_call(gather_kernel, out_shape=(jax.ShapeDtypeStruct((4, 2, 2, 2...  17.8 us
    pallas_call x1, Pallas kernels, call_compute(): pl.pallas_call(functools.partial(compute_kernel, members), out_shape=(jax...  15.8 us

profile of v3, /device:TPU:0, one launch (start us, length us, event | category | flops | bytes accessed | tf_op | source)
XLA Modules:
  0.0 67.3 jit_solution(10866631347900275585)
XLA Ops:
  0.7 17.8 %shard_map.378 = (bf16[4,2,2,2,160,128]{5,4,3,2,1,0:T(8,128)(2,1)S(1)}, bf16[4,2,64,128]{3,2,1,0:T(8,128)(2,1)S(1)}, f32[4,5,8,128]{3,2,1,0:T(8,128)S(1)}, bf16[...) custom-call(s32[16,512]{1,0:T(8,128)} %bitcast.32, f32[16,512]{1,0:T(8,128)} %bitcast.33, ...), custom_call_target="tpu_custom_call" | custom-call | tf_op jit(solution)/shard_map/pallas_call | solution.py:248
  18.5 15.8 %shard_map.379 = (bf16[768,512]{1,0:T(8,128)(2,1)S(1)}, bf16[8,512,512]{2,1,0:T(8,128)(2,1)S(1)}, bf16[4,2,2,2,64,128]{5,4,3,2,1,0:T(8,128)(2,1)S(1)}, bf16[4,2,...) custom-call(bf16[4,2,2,2,160,128]{5,4,3,2,1,0:T(8,128)(2,1)S(1)} %get-tuple-element.84.buf, ...), custom_call_target="tpu_custom_call" | custom-call | tf_op jit(solution)/shard_map/pallas_call | solution.py:489
  34.3 31.6 %shard_map.380 = (f32[96,128]{1,0:T(8,128)S(1)}, f32[1,96]{1,0:T(1,128)S(1)}, f32[1,128]{1,0:T(1,128)S(1)}, f32[96,128]{1,0:T(8,128)S(1)}, f32[64,128]{1,0:T(8,1...) custom-call(bf16[512,768]{1,0:T(8,128)(2,1)S(1)} %get-tuple-element., ...), custom_call_target="tpu_custom_call" | custom-call | tf_op jit(solution)/shard_map/pallas_call | solution.py:839
  65.9 1.3 %shard_map.381 = (f32[96,128]{1,0:T(8,128)}, f32[1,96]{1,0:T(1,128)}, f32[1,128]{1,0:T(1,128)}, f32[96,128]{1,0:T(8,128)}, f32[64,128]{1,0:T(8,128)}, /*index=5*...) custom-call(f32[96,128]{1,0:T(8,128)S(1)} %get-tuple-element.94.refs, ...), custom_call_target="tpu_custom_call" | custom-call | tf_op jit(solution)/shard_map/pallas_call | solution.py:898

commit v4 on v3

--- a/solution.py
+++ b/solution.py
@@ -58,8 +58,8 @@
 PLANE = ((0, 1), (1, 0), (1, 1))
 DP_PEERS = tuple((kz, ky) for kz in range(4) for ky in range(2))[1:]
 COL_PEERS = ((0, 1), (1, 0), (1, 1))
-NSEM1 = 28
-NSEM3 = 24
+NSEM1 = 29
+NSEM3 = 26
 CUTS = (64, 112)
 
 
@@ -166,16 +166,15 @@
     marks = jnp.where(c_i == 0, mask, jnp.where(c_i == 1, high, jnp.where(c_i == 2, length - 16.0 * high, 0.0)))
     columns = jnp.concatenate([bin_index_v[...].astype(f32), frac, jnp.where(c_i == targets_v[...], mask, 0.0), marks], axis=0).astype(bf16)
     nothing = jnp.zeros((64, rows), bf16)
-    table[...] = (dot_t((p_col == wanted).astype(bf16), jnp.concatenate([columns, nothing], axis=0))
+    dealt = (dot_t((p_col == wanted).astype(bf16), jnp.concatenate([columns, nothing], axis=0))
                   + dot_t((p_col == wanted + 8 * slot).astype(bf16), jnp.concatenate([nothing, columns], axis=0))).astype(bf16)
-    own_rows = pl.ds(pl.multiple_of(me_d * slot, slot), slot)
-    recv[own_rows, :] = table[own_rows, :]
+    table[...] = dealt.reshape(table.shape)
+    recv[me_d] = table[me_d]
     t = []
     for kz, ky in DP_PEERS:
         pz, py = z_other(z, kz), other(y, ky)
-        theirs = pl.ds(pl.multiple_of((2 * pz + py) * slot, slot), slot)
-        t.append((table.at[theirs], recv.at[own_rows], device(pz, py, x, core)))
-    t = send.group(recv.at[0:7 * slot], t)
+        t.append((table.at[2 * pz + py, core], recv.at[me_d, core], device(pz, py, x, core)))
+    t = send.group(recv.at[0:7, 0], t)
     h = send.group(hbuf.at[0:3, 0], [(hbuf.at[z, y], hbuf.at[z, y], device(z_other(z, k), y, x, core)) for k in (1, 2, 3)])
     ad = []
     for kx, kc in COL_PEERS:
@@ -202,8 +201,12 @@
     h2 = send(hbuf.at[:, y], hbuf.at[:, y], device(z, 1 - y, x, core))
     for cp in t:
         cp.wait_recv()
+    t2 = send.group(recv.at[0:7, 0], [(recv.at[2 * pz + py, core], recv.at[2 * pz + py, core], mate)
+                                      for pz, py in [(z_other(z, kz), other(y, ky)) for kz, ky in DP_PEERS]])
+    for cp in t2:
+        cp.wait_recv()
     lane8 = lax.broadcasted_iota(jnp.int32, (8, 128), 1)
-    got = recv[...]
+    got = recv[...].reshape(rows // 2, 128)
     mask_row = jnp.concatenate([dot_t((lane8 == 48).astype(bf16), got), dot_t((lane8 == 112).astype(bf16), got)], axis=1)
     pos = dot(mask_row.astype(bf16), (i_row < i_col).astype(bf16))
     spot = jnp.where(mask_row > 0.5, pos, -1.0)[0:1]
@@ -256,7 +259,7 @@
             jax.ShapeDtypeStruct((8, 128), f32),
         ),
         in_specs=[FAR] * 8, out_specs=(VM,) * 6,
-        scratch_shapes=[pltpu.VMEM((rows // 2, 128), bf16), pltpu.VMEM((rows // 2, 128), bf16),
+        scratch_shapes=[pltpu.VMEM((8, 2, rows // 32, 128), bf16), pltpu.VMEM((8, 2, rows // 32, 128), bf16),
                         pltpu.VMEM(w_first.shape, f32), pltpu.VMEM(w_second.shape, f32),
                         pltpu.VMEM(w_head.shape, f32), pltpu.VMEM(adapters.shape, f32),
                         pltpu.VMEM(bin_index.shape, jnp.int32), pltpu.VMEM(bin_fraction.shape, f32),
@@ -593,6 +596,14 @@
     def to_dp(whole, ref, into):
         return send.group(whole, [(ref(2 * pz + py), into(i), device(pz, py, x, core)) for i, (pz, py) in enumerate(dp_peers)])
 
+    mate_c, beside_c, corner_c = 2 * x + 1 - core, 2 * (1 - x) + core, 2 * (1 - x) + 1 - core
+
+    def to_near(buffer, src):
+        return send.group(buffer.at[0:2], [(src, buffer.at[me_c], mate), (src, buffer.at[me_c], beside)])
+
+    def pass_on(buffer):
+        return [send(buffer.at[beside_c], buffer.at[beside_c], mate)]
+
     def to_col(whole, ref, into):
         return send.group(whole, [(ref(2 * other(x, kx) + other(core, kc)), into, device(z, y, other(x, kx), other(core, kc)))
                                   for kx, kc in COL_PEERS])
@@ -658,25 +669,27 @@
     small3 = to_z(gall.at[0:3, 0], lambda pz: gall.at[z, y], lambda k: gall.at[z, y])
     received(head2)
     hcol[me_c] = (hsum[z].astype(f32) + hz[0].astype(f32)) + (hz[1].astype(f32) + hz[2].astype(f32))
-    head3 = to_col(hcol.at[0:3], lambda c: hcol.at[me_c], hcol.at[me_c])
+    head3 = to_near(hcol, hcol.at[me_c])
     received([second3])
     second_pair[...] = (second_own[:, x].astype(f32) + second_x[...].astype(f32)).astype(bf16)
     second4 = to_z(second_in, lambda pz: second_pair.at[pz], lambda k: second_in.at[k - 1])
     received([first2])
     first_pair[...] = (own_pair[:, y].astype(f32) + first_y[...].astype(f32)).astype(bf16)
     first3 = to_z(first_in, lambda pz: first_pair.at[pz], lambda k: first_in.at[k - 1])
+    received(head3)
+    head4 = pass_on(hcol)
     received(small3)
     small4 = send(gall.at[:, y], gall.at[:, y], y_mate)
     received(gain_dp)
     gain_cols[me_c] = gain_all[...]
-    gain_spread = to_col(gain_cols.at[0:3], lambda c: gain_all, gain_cols.at[me_c])
+    gain_spread = to_near(gain_cols, gain_cols.at[me_c])
     received(second4)
     second = second_pair[z].astype(f32)
     for i in range(3):
         second = second + second_in[i].astype(f32)
     second_sq = second * second + EPS_SQUARE
     o_second_grad[...] = second
-    received(head3)
+    received(head4)
     hg = [hcol[c] for c in range(4)]
     hsq = [g * g + EPS_SQUARE for g in hg]
     seg8 = (lax.broadcasted_iota(jnp.int32, (mem, hw), 1) // CLASSES
@@ -698,6 +711,8 @@
     own8 = pl.ds(pl.multiple_of(8 * me_c, 8), 8)
     ca[me_c] = gall[:, :, own8, :]
     spread_col = to_col(ca.at[0:3], lambda c: gall.at[:, :, pl.ds(pl.multiple_of(8 * c, 8), 8)], ca.at[me_c])
+    received(gain_spread)
+    gain_last = pass_on(gain_cols)
     received(first3)
     first = first_pair[z].astype(f32)
     for i in range(3):
@@ -785,7 +800,7 @@
     o_first_col[...] = first_c
     o_second_col[...] = second_c
     o_head_col[...] = from_lanes(jnp.concatenate([head_c, jnp.zeros((4, 128), f32)], axis=0))
-    received(gain_spread)
+    received(gain_last)
     for c in range(4):
         for i in range(enc_w // 128):
             o_gain_grad[mem * c:mem * (c + 1), 128 * i:128 * (i + 1)] = gain_cols[c, :, i, :]

time: 67.5 us -> 66.4 us (0.984)
  Pallas kernels: 66.5 us -> 65.4 us
    pallas_call x1, Pallas kernels: 31.6 us -> 30.6 us  [call_reduce(): pl.pallas_call(functools.partial(reduce_kernel, enc_w, width, members), o...]
where the time goes in v4:
time: 66.4 us; the launch traced here: 66.2 us
  Pallas kernels  65.4 us (98%)
  between operations  0.85 us (1%)
    pallas_call x1, Pallas kernels, call_reduce(): pl.pallas_call(functools.partial(reduce_kernel, enc_w, width, members), o...  30.6 us
    pallas_call x1, Pallas kernels, call_gather(): pl.pallas_call(gather_kernel, out_shape=(jax.ShapeDtypeStruct((4, 2, 2, 2...  17.7 us
    pallas_call x1, Pallas kernels, call_compute(): pl.pallas_call(functools.partial(compute_kernel, members), out_shape=(jax...  15.8 us

profile of v4, /device:TPU:0, one launch (start us, length us, event | category | flops | bytes accessed | tf_op | source)
XLA Modules:
  0.0 66.2 jit_solution(4146779356096051335)
XLA Ops:
  0.7 17.7 %shard_map.378 = (bf16[4,2,2,2,160,128]{5,4,3,2,1,0:T(8,128)(2,1)S(1)}, bf16[4,2,64,128]{3,2,1,0:T(8,128)(2,1)S(1)}, f32[4,5,8,128]{3,2,1,0:T(8,128)S(1)}, bf16[...) custom-call(s32[16,512]{1,0:T(8,128)} %bitcast.32, f32[16,512]{1,0:T(8,128)} %bitcast.33, ...), custom_call_target="tpu_custom_call" | custom-call | tf_op jit(solution)/shard_map/pallas_call | solution.py:251
  18.4 15.8 %shard_map.379 = (bf16[768,512]{1,0:T(8,128)(2,1)S(1)}, bf16[8,512,512]{2,1,0:T(8,128)(2,1)S(1)}, bf16[4,2,2,2,64,128]{5,4,3,2,1,0:T(8,128)(2,1)S(1)}, bf16[4,2,...) custom-call(bf16[4,2,2,2,160,128]{5,4,3,2,1,0:T(8,128)(2,1)S(1)} %get-tuple-element.84.buf, ...), custom_call_target="tpu_custom_call" | custom-call | tf_op jit(solution)/shard_map/pallas_call | solution.py:492
  34.2 30.6 %shard_map.380 = (f32[96,128]{1,0:T(8,128)S(1)}, f32[1,96]{1,0:T(1,128)S(1)}, f32[1,128]{1,0:T(1,128)S(1)}, f32[96,128]{1,0:T(8,128)S(1)}, f32[64,128]{1,0:T(8,1...) custom-call(bf16[512,768]{1,0:T(8,128)(2,1)S(1)} %get-tuple-element., ...), custom_call_target="tpu_custom_call" | custom-call | tf_op jit(solution)/shard_map/pallas_call | solution.py:854
  64.8 1.3 %shard_map.381 = (f32[96,128]{1,0:T(8,128)}, f32[1,96]{1,0:T(1,128)}, f32[1,128]{1,0:T(1,128)}, f32[96,128]{1,0:T(8,128)}, f32[64,128]{1,0:T(8,128)}, /*index=5*...) custom-call(f32[96,128]{1,0:T(8,128)S(1)} %get-tuple-element.94.refs, ...), custom_call_target="tpu_custom_call" | custom-call | tf_op jit(solution)/shard_map/pallas_call | solution.py:913
